TPU v7x, 32 devices: a whole 2x2x4 slice. The times are simulated.
32 devices in a mesh: group: 2 (over x), row: 16 (over z, y, core).
Axes of the slice: x: 2, y: 2, z: 4, core: 2. Of those that a mesh axis runs over, the one named last changes fastest.
Arguments:
- base_currents: bfloat16 [32768, 1024], P(('group', 'row')), parts along dimension 0, may hold values from -6 to 6
- term_rows: bfloat16 [8192, 1024], P(('group', 'row')), parts along dimension 0, may hold values from -12 to 12
- term_owner: int32 [8192, 1], P(('group', 'row')), parts along dimension 0, may hold values from 0 to 15; in each aligned block of 256 rows (0 to 255, 256 to 511, ...) at most 32 rows name the same one
- term_slot: int32 [8192, 1], P(('group', 'row')), parts along dimension 0, may hold values from 0 to 1023
- inductance: bfloat16 [64, 20, 256, 256], P('row'), may hold values from -0.078125 to 0.078125
- block_cols: int32 [64, 20], P('row'), may hold values from 0 to 63, as said below
Outputs:
- flux: bfloat16 [32768, 1024], P(('group', 'row')), parts along dimension 0
There are 2 independent parts, one for each index of `group`. A program takes and returns all parts, laid end to end along the dimension named above; an argument that names none is the same for every part. Nothing has to cross between parts.
Inputs may be any that keep to these rules, and one draw needn't show every extreme that they name: `block_cols`: the block rows of device i (block rows i * 4 to i * 4 + 3) list only block columns of devices i - 2 to i + 2; every block row lists a column of device max(i - 2, 0) and one of device min(i + 2, the last device). Columns may repeat. `term_owner`: among the 256 terminal rows of one device, at most 32 name the same owner, and that many is reached.
All inputs are finite; a program needn't handle non-finite values.
Results may differ from a plain program's by a relative error of at most 0.0046.
Values may be sent and summed in bfloat16 or wider, within the bound.
No kernel may reach another device: no remote copies, remote signals or barrier semaphores. Data moves between devices by JAX's collectives and lax.ppermute only.
A program may use at most 128 MiB of HBM per device.

v0:
```python
import jax
import jax.numpy as jnp
from jax import lax
from jax.sharding import PartitionSpec as P

HALO = 2


def shifted(value, axis, by):
    size = lax.axis_size(axis)
    pairs = [(i, i + by) for i in range(size) if 0 <= i + by < size]
    return lax.ppermute(value, axis, pairs)


def shards(base_currents, term_rows, term_owner, term_slot, inductance, block_cols):
    devices = lax.axis_size("row")
    own_index = lax.axis_index("row")
    seg_dev, width = base_currents.shape
    capacity = max(2, 2 * term_rows.shape[0] // devices)
    owner_ids = term_owner[:, 0]
    target = term_slot[:, 0]
    peer_ids = jnp.arange(devices, dtype=jnp.int32)
    matches = (owner_ids[:, None] == peer_ids[None, :]).astype(jnp.int32)
    earlier = jnp.cumsum(matches, axis=0) - matches
    order_in = jnp.sum(earlier * matches, axis=1)
    position = owner_ids * capacity + order_in
    slot_ids = jnp.arange(devices * capacity, dtype=jnp.int32)
    picker = slot_ids[:, None] == position[None, :]
    outgoing = jnp.dot(picker.astype(jnp.bfloat16), term_rows, preferred_element_type=jnp.float32)
    outgoing = outgoing.astype(jnp.bfloat16).reshape(devices, capacity, width)
    slot_tags = jnp.sum(jnp.where(picker, target[None, :] + 1, 0), axis=1)
    slot_tags = slot_tags.reshape(devices, capacity)
    arrived, arrived_tags = (
        lax.all_to_all(outgoing, "row", split_axis=0, concat_axis=0, tiled=True),
        lax.all_to_all(slot_tags, "row", split_axis=0, concat_axis=0, tiled=True),
    )
    seg_ids = jnp.arange(seg_dev, dtype=jnp.int32)
    landing = (arrived_tags.reshape(-1)[None, :] - 1 == seg_ids[:, None]).astype(jnp.bfloat16)
    injected = jnp.dot(landing, arrived.reshape(-1, width), preferred_element_type=jnp.float32)
    currents = (base_currents.astype(jnp.float32) + injected).astype(jnp.bfloat16)
    below = []
    above = []
    offsets = list(range(1, HALO + 1)) + [-step for step in range(1, HALO + 1)]
    for offset in offsets:
        moved = shifted(currents, "row", offset)
        if offset > 0:
            below.append(moved)
        else:
            above.append(moved)
    window = jnp.concatenate(below[::-1] + [currents] + above, axis=0)
    rows_dev = inductance.shape[0]
    block = inductance.shape[2]
    window_blocks = window.reshape(-1, block, width)
    first_block = (own_index - HALO) * rows_dev
    results = []
    for block_row in range(rows_dev):
        local_cols = block_cols[block_row] - first_block
        picked = window_blocks[local_cols]
        linked = jnp.einsum(
            "kab,kbw->aw", inductance[block_row], picked, preferred_element_type=jnp.float32
        )
        results.append(linked)
    return jnp.concatenate(results, axis=0).astype(jnp.bfloat16)


def solution(mesh):
    placed = (
        P(("group", "row"), None),
        P(("group", "row"), None),
        P(("group", "row"), None),
        P(("group", "row"), None),
        P("row", None, None, None),
        P("row", None),
    )
    return jax.shard_map(
        shards, mesh=mesh, in_specs=placed, out_specs=P(("group", "row"), None), check_vma=False
    )
```

profile of v0, /device:TPU:12, one launch (start us, length us, event | category | flops | bytes accessed | tf_op | source)
XLA Modules:
  0.0 267.1 jit_solution(7701543596068987871)
XLA Ops:
  0.0 0.0 copy-start
  0.0 0.0 copy-start.4
  0.0 0.7 fusion.53
  0.7 0.6 reduce-window.6
  1.3 0.2 slice_reduce_fusion
  1.5 0.8 fusion.52
  2.3 0.7 multiply_add_fusion
  3.0 0.7 broadcast_add_fusion
  3.7 0.1 select_reduce_fusion
  3.8 0.7 all_to_all.9
  4.5 6.2 %all-to-all-start = ((s32[16,1,32]{2,1,0:T(1,128)}), s32[16,1,32]{2,1,0:T(1,128)S(1)}, u32[]{:S(2)}, u32[]{:S(2)}) async-start(s32[16,1,32]{2,1,0:T(1,128)} %all_to_all.9), calls=%async_computation | async-start | bytes 16384 | tf_op jit(solution)/shard_map/all_to_all | solution.py:35
  10.8 0.0 copy-done
  10.8 1.4 convolution_convert_fusion
  12.2 2.7 %all-to-all-done = s32[16,1,32]{2,1,0:T(1,128)S(1)} async-done(((s32[16,1,32]{2,1,0:T(1,128)}), s32[16,1,32]{2,1,0:T(1,128)S(1)}, u32[]{:S(2)}, u32[]{:S(2)}) %all-to-all-start) | async-done | bytes 2080 | tf_op jit(solution)/shard_map/all_to_all | solution.py:35
  14.9 5.9 %all-to-all-start.1 = ((bf16[16,32,1024]{2,1,0:T(8,128)(2,1)}), bf16[16,32,1024]{2,1,0:T(8,128)(2,1)S(1)}, u32[]{:S(2)}, u32[]{:S(2)}) async-start(bf16[16,32,1024]{2,1,0:T(8,128)(2,1)} %bitcast.4), calls=%async_computation.1 | async-start | bytes 2097152 | tf_op jit(solution)/shard_map/all_to_all | solution.py:34
  20.8 0.1 sub.72
  20.9 24.6 %all-to-all-done.1 = bf16[16,32,1024]{2,1,0:T(8,128)(2,1)S(1)} async-done(((bf16[16,32,1024]{2,1,0:T(8,128)(2,1)}), bf16[16,32,1024]{2,1,0:T(8,128)(2,1)S(1)}, u32[]{:S(2)}, u32[]{:S(2)}) %all-to-all-start.1) | async-done | bytes 1048608 | tf_op jit(solution)/shard_map/all_to_all | solution.py:34
  45.5 0.0 copy-start.3
  45.5 1.0 copy-done.3
  46.5 3.2 %add_convert_fusion = bf16[1024,1024]{1,0:T(8,128)(2,1)S(1)} fusion(bf16[1024,1024]{1,0:T(8,128)(2,1)} %param.6, bf16[512,1024]{1,0:T(8,128)(2,1)} %bitcast.115, s32[512]{0:T(512)S(1)} %sub.72), kind=kOutput, calls=%fused_computation.4 | convolution fusion | flops 1077411840 | bytes 5244928 | tf_op jit(solution)/shard_map/dot_general | solution.py:39
  49.7 3.8 %collective-permute-start = (bf16[1024,1024]{1,0:T(8,128)(2,1)S(1)}, bf16[1024,1024]{1,0:T(8,128)(2,1)}, u32[]{:S(2)}, u32[]{:S(2)}) collective-permute-start(bf16[1024,1024]{1,0:T(8,128)(2,1)S(1)} %add_convert_fusion), channel_id=1, source_target_pairs={{0,2},{1,3},{2,4},{3,5},{4,6},{5,7},{6,8},{7,9},{8,10},{9,11},{10,... | collective-permute-start | bytes 6291464 | tf_op jit(solution)/shard_map/ppermute | solution.py:12
  53.5 1.9 collective-permute-start.1
  55.4 3.6 %collective-permute-start.2 = (bf16[1024,1024]{1,0:T(8,128)(2,1)S(1)}, bf16[1024,1024]{1,0:T(8,128)(2,1)}, u32[]{:S(2)}, u32[]{:S(2)}) collective-permute-start(bf16[1024,1024]{1,0:T(8,128)(2,1)S(1)} %add_convert_fusion), channel_id=1, source_target_pairs={{1,0},{2,1},{3,2},{4,3},{5,4},{6,5},{7,6},{8,7},{9,8},{10,9},{11,1... | collective-permute-start | bytes 6291464 | tf_op jit(solution)/shard_map/ppermute | solution.py:12
  59.1 2.9 %collective-permute-start.3 = (bf16[1024,1024]{1,0:T(8,128)(2,1)S(1)}, bf16[1024,1024]{1,0:T(8,128)(2,1)}, u32[]{:S(2)}, u32[]{:S(2)}) collective-permute-start(bf16[1024,1024]{1,0:T(8,128)(2,1)S(1)} %add_convert_fusion), channel_id=1, source_target_pairs={{2,0},{3,1},{4,2},{5,3},{6,4},{7,5},{8,6},{9,7},{10,8},{11,9},{12,... | collective-permute-start | bytes 6291464 | tf_op jit(solution)/shard_map/ppermute | solution.py:12
  62.0 0.0 copy-done.4
  62.1 105.5 %collective-permute-done = bf16[1024,1024]{1,0:T(8,128)(2,1)} collective-permute-done((bf16[1024,1024]{1,0:T(8,128)(2,1)S(1)}, bf16[1024,1024]{1,0:T(8,128)(2,1)}, u32[]{:S(2)}, u32[]{:S(2)}) %collective-permute-start) | collective-permute-done | bytes 2097184 | tf_op jit(solution)/shard_map/ppermute | solution.py:12
  167.5 3.1 %constant_dynamic-update-slice_fusion.4 = bf16[5120,1024]{1,0:T(8,128)(2,1)} fusion(bf16[1024,1024]{1,0:T(8,128)(2,1)} %collective-permute-done), kind=kLoop, calls=%fused_computation.49 | loop fusion | bytes 4194304
  170.6 18.7 %collective-permute-done.1 = bf16[1024,1024]{1,0:T(8,128)(2,1)} collective-permute-done((bf16[1024,1024]{1,0:T(8,128)(2,1)S(1)}, bf16[1024,1024]{1,0:T(8,128)(2,1)}, u32[]{:S(2)}, u32[]{:S(2)}) %collective-permute-start.1) | collective-permute-done | bytes 2097184 | tf_op jit(solution)/shard_map/ppermute | solution.py:12
  189.4 3.1 %constant_dynamic-update-slice_fusion.3 = bf16[5120,1024]{1,0:T(8,128)(2,1)} fusion(bf16[5120,1024]{1,0:T(8,128)(2,1)} %constant_dynamic-update-slice_fusion.4, bf16[1024,1024]{1,0:T(8,128)(2,1)} %collective-permute-done.1), kind=kLoop, calls=%fused_computation.48 | loop fusion | bytes 4194304
  192.4 1.5 constant_dynamic-update-slice_fusion.2
  193.9 0.0 collective-permute-done.2
  193.9 3.1 %constant_dynamic-update-slice_fusion.1 = bf16[5120,1024]{1,0:T(8,128)(2,1)} fusion(bf16[5120,1024]{1,0:T(8,128)(2,1)} %constant_dynamic-update-slice_fusion.2, bf16[1024,1024]{1,0:T(8,128)(2,1)} %collective-permute-done.2), kind=kLoop, calls=%fused_computation.46 | loop fusion | bytes 4194304
  197.1 0.0 collective-permute-done.3
  197.1 3.2 %constant_dynamic-update-slice_fusion = bf16[5120,1024]{1,0:T(8,128)(2,1)} fusion(bf16[5120,1024]{1,0:T(8,128)(2,1)} %constant_dynamic-update-slice_fusion.1, bf16[1024,1024]{1,0:T(8,128)(2,1)} %collective-permute-done.3), kind=kLoop, calls=%fused_computation.45 | loop fusion | bytes 4194304 | tf_op jit(solution)/shard_map/concatenate | solution.py:50
  200.2 9.6 %gather_fusion = bf16[20,256,1024]{2,1,0:T(8,128)(2,1)} fusion(bf16[20,256,1024]{2,1,0:T(8,128)(2,1)} %bitcast.6, s32[1024]{0:T(1024)S(1)} %get-tuple-element.12), kind=kCustom, calls=%fused_computation | custom fusion | bytes 20971600 | tf_op jit(solution)/shard_map/gather | solution.py:58
  209.8 9.4 %gather_fusion.1 = bf16[20,256,1024]{2,1,0:T(8,128)(2,1)} fusion(bf16[20,256,1024]{2,1,0:T(8,128)(2,1)} %bitcast.6, s32[1024]{0:T(1024)S(1)} %get-tuple-element.11), kind=kCustom, calls=%fused_computation.1 | custom fusion | bytes 20971600 | tf_op jit(solution)/shard_map/gather | solution.py:58
  219.2 0.0 copy-start.2
  219.2 7.8 %fusion.36 = bf16[256,1024]{1,0:T(8,128)(2,1)S(1)} fusion(bf16[20,256,1024]{2,1,0:T(8,128)(2,1)} %gather_fusion, bf16[4,20,256,256]{3,2,1,0:T(8,128)(2,1)} %param.10), kind=kOutput, calls=%fused_computation.28 | convolution fusion | flops 2684616704 | bytes 13631488 | tf_op jit(solution)/shard_map/kab,kbw->aw/dot_general | solution.py:59
  226.9 0.0 copy-done.2
  227.0 4.7 %fusion.39 = bf16[256,1024]{1,0:T(8,128)(2,1)S(1)} fusion(bf16[20,256,1024]{2,1,0:T(8,128)(2,1)S(1)} %copy-done.2, bf16[4,20,256,256]{3,2,1,0:T(8,128)(2,1)} %param.10), kind=kOutput, calls=%fused_computation.29 | convolution fusion | flops 2684616704 | bytes 13631488 | tf_op jit(solution)/shard_map/kab,kbw->aw/dot_general | solution.py:59
  231.6 9.3 %gather_fusion.2 = bf16[20,256,1024]{2,1,0:T(8,128)(2,1)} fusion(bf16[20,256,1024]{2,1,0:T(8,128)(2,1)} %bitcast.6, s32[1024]{0:T(1024)S(1)} %get-tuple-element.10), kind=kCustom, calls=%fused_computation.2 | custom fusion | bytes 20971600 | tf_op jit(solution)/shard_map/gather | solution.py:58
  241.0 7.6 %fusion.42 = bf16[256,1024]{1,0:T(8,128)(2,1)S(1)} fusion(bf16[20,256,1024]{2,1,0:T(8,128)(2,1)} %gather_fusion.2, bf16[4,20,256,256]{3,2,1,0:T(8,128)(2,1)} %param.10), kind=kOutput, calls=%fused_computation.30 | convolution fusion | flops 2684616704 | bytes 13631488 | tf_op jit(solution)/shard_map/kab,kbw->aw/dot_general | solution.py:59
  248.6 0.0 copy-start.1
  248.6 9.4 %gather_fusion.3 = bf16[20,256,1024]{2,1,0:T(8,128)(2,1)} fusion(bf16[20,256,1024]{2,1,0:T(8,128)(2,1)} %bitcast.6, s32[1024]{0:T(1024)S(1)} %get-tuple-element.9), kind=kCustom, calls=%fused_computation.3 | custom fusion | bytes 20971600 | tf_op jit(solution)/shard_map/gather | solution.py:58
  258.0 7.6 %fusion.45 = bf16[256,1024]{1,0:T(8,128)(2,1)S(1)} fusion(bf16[20,256,1024]{2,1,0:T(8,128)(2,1)} %gather_fusion.3, bf16[4,20,256,256]{3,2,1,0:T(8,128)(2,1)} %param.10), kind=kOutput, calls=%fused_computation.31 | convolution fusion | flops 2684616704 | bytes 13631488 | tf_op jit(solution)/shard_map/kab,kbw->aw/dot_general | solution.py:59
  265.7 1.5 pad_maximum_fusion
  267.1 0.0 copy-done.1
  (6 shorter events, 0.1 us)
Async XLA Ops:
  0.0 10.8 %copy-start = (bf16[256,1024]{1,0:T(8,128)(2,1)S(1)}, bf16[256,1024]{1,0:T(8,128)(2,1)}, u32[]{:S(2)}) copy-start(bf16[256,1024]{1,0:T(8,128)(2,1)} %param.7) | copy-start | bytes 1572868
  0.0 62.0 %copy-start.4 = (s32[4,20]{1,0:T(4,128)S(1)}, s32[4,20]{1,0:T(4,128)}, u32[]{:S(2)}) copy-start(s32[4,20]{1,0:T(4,128)} %param.11) | copy-start | bytes 964
  4.5 10.3 %all-to-all-start = ((s32[16,1,32]{2,1,0:T(1,128)}), s32[16,1,32]{2,1,0:T(1,128)S(1)}, u32[]{:S(2)}, u32[]{:S(2)}) async-start(s32[16,1,32]{2,1,0:T(1,128)} %all_to_all.9), calls=%async_computation | async-start | bytes 16384 | tf_op jit(solution)/shard_map/all_to_all | solution.py:35
  14.9 30.6 %all-to-all-start.1 = ((bf16[16,32,1024]{2,1,0:T(8,128)(2,1)}), bf16[16,32,1024]{2,1,0:T(8,128)(2,1)S(1)}, u32[]{:S(2)}, u32[]{:S(2)}) async-start(bf16[16,32,1024]{2,1,0:T(8,128)(2,1)} %bitcast.4), calls=%async_computation.1 | async-start | bytes 2097152 | tf_op jit(solution)/shard_map/all_to_all | solution.py:34
  45.5 1.0 copy-start.3
  49.7 117.9 %collective-permute-start = (bf16[1024,1024]{1,0:T(8,128)(2,1)S(1)}, bf16[1024,1024]{1,0:T(8,128)(2,1)}, u32[]{:S(2)}, u32[]{:S(2)}) collective-permute-start(bf16[1024,1024]{1,0:T(8,128)(2,1)S(1)} %add_convert_fusion), channel_id=1, source_target_pairs={{0,2},{1,3},{2,4},{3,5},{4,6},{5,7},{6,8},{7,9},{8,10},{9,11},{10,... | collective-permute-start | bytes 6291464 | tf_op jit(solution)/shard_map/ppermute | solution.py:12
  53.5 135.9 %collective-permute-start.1 = (bf16[1024,1024]{1,0:T(8,128)(2,1)S(1)}, bf16[1024,1024]{1,0:T(8,128)(2,1)}, u32[]{:S(2)}, u32[]{:S(2)}) collective-permute-start(bf16[1024,1024]{1,0:T(8,128)(2,1)S(1)} %add_convert_fusion), channel_id=1, source_target_pairs={{0,1},{1,2},{2,3},{3,4},{4,5},{5,6},{6,7},{7,8},{8,9},{9,10},{10,1... | collective-permute-start | bytes 6291464 | tf_op jit(solution)/shard_map/ppermute | solution.py:12
  55.4 138.5 %collective-permute-start.2 = (bf16[1024,1024]{1,0:T(8,128)(2,1)S(1)}, bf16[1024,1024]{1,0:T(8,128)(2,1)}, u32[]{:S(2)}, u32[]{:S(2)}) collective-permute-start(bf16[1024,1024]{1,0:T(8,128)(2,1)S(1)} %add_convert_fusion), channel_id=1, source_target_pairs={{1,0},{2,1},{3,2},{4,3},{5,4},{6,5},{7,6},{8,7},{9,8},{10,9},{11,1... | collective-permute-start | bytes 6291464 | tf_op jit(solution)/shard_map/ppermute | solution.py:12
  59.1 138.0 %collective-permute-start.3 = (bf16[1024,1024]{1,0:T(8,128)(2,1)S(1)}, bf16[1024,1024]{1,0:T(8,128)(2,1)}, u32[]{:S(2)}, u32[]{:S(2)}) collective-permute-start(bf16[1024,1024]{1,0:T(8,128)(2,1)S(1)} %add_convert_fusion), channel_id=1, source_target_pairs={{2,0},{3,1},{4,2},{5,3},{6,4},{7,5},{8,6},{9,7},{10,8},{11,9},{12,... | collective-permute-start | bytes 6291464 | tf_op jit(solution)/shard_map/ppermute | solution.py:12
  219.2 7.8 %copy-start.2 = (bf16[20,256,1024]{2,1,0:T(8,128)(2,1)S(1)}, bf16[20,256,1024]{2,1,0:T(8,128)(2,1)}, u32[]{:S(2)}) copy-start(bf16[20,256,1024]{2,1,0:T(8,128)(2,1)} %gather_fusion.1) | copy-start | bytes 31457284
  248.6 18.5 %copy-start.1 = (bf16[256,1024]{1,0:T(8,128)(2,1)S(1)}, bf16[256,1024]{1,0:T(8,128)(2,1)}, u32[]{:S(2)}) copy-start(bf16[256,1024]{1,0:T(8,128)(2,1)} %param.7) | copy-start | bytes 1572868
where the time goes:
time: 268 us; the launch traced here: 267 us
  waiting for transfers between devices  152 us (57%)
  local copies, waits for them, and re-layouts  53.5 us (20%)
  matrix products  32.4 us (12%)
  starting transfers between devices  24.4 us (9%)
  other arithmetic  5.17 us (2%)
    ppermute x4, waiting for transfers between devices, shifted(): return lax.ppermute(value, axis, pairs)  124 us
    gather x4, local copies, waits for them, and re-layouts, shards(): picked = window_blocks[local_cols]  37.6 us
    dot_general x4, matrix products, shards(): jnp.einsum('kab,kbw->aw', inductance[block_row], picked, preferred_elemen...  27.7 us
    all_to_all x1, waiting for transfers between devices, shards(): lax.all_to_all(outgoing, 'row', split_axis=0, concat_axis=0, tiled=True)  24.6 us
    ppermute x4, starting transfers between devices, shifted(): return lax.ppermute(value, axis, pairs)  12.3 us
    unnamed x14, local copies, waits for them, and re-layouts  11.8 us
    all_to_all x1, starting transfers between devices, shards(): lax.all_to_all(slot_tags, 'row', split_axis=0, concat_axis=0, tiled=True)  6.24 us
    all_to_all x1, starting transfers between devices, shards(): lax.all_to_all(outgoing, 'row', split_axis=0, concat_axis=0, tiled=True)  5.89 us
  transfers between devices with their start and end apart: 6, of which 4 were waited for; matrix products, arithmetic and copies ran while one was open for 5% of the time, Pallas kernels for 0%

commit v1 on v0

v1 whole, which is shorter than its diff:
```python
import functools

import jax
import jax.numpy as jnp
from jax import lax
from jax.experimental import pallas as pl
from jax.experimental.pallas import tpu as pltpu
from jax.sharding import PartitionSpec as P

HALO = 2
AHEAD = 9
LANES = 128
RADIX = 32
VMEM = pl.BlockSpec(memory_space=pltpu.VMEM)
SMEM = pl.BlockSpec(memory_space=pltpu.SMEM)
HBM = pl.BlockSpec(memory_space=pltpu.HBM)
ANY = pl.BlockSpec(memory_space=pl.ANY)
SLOTS = 2 * HALO + 1
TOKEN = jax.ShapeDtypeStruct((8, LANES), jnp.float32)
MIB = 1024 * 1024


def limit(mib):
    return pltpu.CompilerParams(vmem_limit_bytes=mib * MIB)


def in_hbm(value):
    return pltpu.with_memory_space_constraint(value, pltpu.HBM)


def gate_kernel(*refs):
    pass


def gate(value, *others):
    return pl.pallas_call(
        gate_kernel,
        out_shape=pltpu.HBM(value.shape, value.dtype),
        in_specs=[HBM] + [ANY] * len(others),
        out_specs=HBM,
        input_output_aliases={0: 0},
        compiler_params=limit(1),
        name="gate",
    )(in_hbm(value), *others)


def column_cuts(width):
    unit = width // 8
    return [[2 * unit], [3 * unit], [3 * unit]]


def pack_kernel(capacity, owner_ref, target_ref, rows_ref, out_ref):
    count, width = rows_ref.shape
    slots = out_ref.shape[0]
    owner = owner_ref[...]
    target = target_ref[...]
    named = lax.broadcasted_iota(jnp.int32, (LANES, count), 0) == owner
    tri = lax.broadcasted_iota(jnp.int32, (count, count), 0) < lax.broadcasted_iota(
        jnp.int32, (count, count), 1
    )
    earlier = jnp.dot(
        named.astype(jnp.bfloat16), tri.astype(jnp.bfloat16), preferred_element_type=jnp.float32
    )
    order = jnp.sum(jnp.where(named, earlier, 0.0), axis=0, keepdims=True).astype(jnp.int32)
    position = owner * capacity + order
    picker = (lax.broadcasted_iota(jnp.int32, (slots, count), 0) == position).astype(jnp.bfloat16)
    line = lax.broadcasted_iota(jnp.int32, (LANES, count), 0)
    tags = jnp.where(line == 0, target // RADIX + 1, jnp.where(line == 1, target % RADIX, 0))
    tags = tags.astype(jnp.float32).astype(jnp.bfloat16)
    out_ref[:, :width] = jnp.dot(
        picker, rows_ref[...], preferred_element_type=jnp.float32
    ).astype(jnp.bfloat16)
    out_ref[:, width:] = lax.dot_general(
        picker, tags, (((1,), (1,)), ((), ())), preferred_element_type=jnp.float32
    ).astype(jnp.bfloat16)


def inject_kernel(offset, base_ref, arrived_ref, wait_ref, *out_refs):
    seg_dev = base_ref.shape[0]
    slots = arrived_ref.shape[0]
    width = arrived_ref.shape[1] - LANES
    pick_lane = lax.broadcasted_iota(jnp.int32, (8, LANES), 1)
    weights = jnp.where(pick_lane == 0, float(RADIX), jnp.where(pick_lane == 1, 1.0, 0.0))
    segment = lax.dot_general(
        weights.astype(jnp.bfloat16),
        arrived_ref[:, width:],
        (((1,), (1,)), ((), ())),
        preferred_element_type=jnp.float32,
    )[0:1].astype(jnp.int32) - RADIX
    landing = (lax.broadcasted_iota(jnp.int32, (seg_dev, slots), 0) == segment).astype(jnp.bfloat16)
    for out_ref in out_refs:
        there = slice(offset, offset + out_ref.shape[1])
        injected = jnp.dot(landing, arrived_ref[:, there], preferred_element_type=jnp.float32)
        out_ref[...] = (base_ref[:, there].astype(jnp.float32) + injected).astype(jnp.bfloat16)
        offset += out_ref.shape[1]


def dense_kernel(cols_ref, slot_ref, blocks_ref, wait_ref, out_ref, token_ref, total_ref):
    row = pl.program_id(0)
    count = blocks_ref.shape[1]
    block = blocks_ref.shape[2]
    per_dev = cols_ref.shape[0]
    places = total_ref.shape[0]
    total_ref[...] = jnp.zeros_like(total_ref)
    token_ref[...] = jnp.zeros_like(token_ref)

    def add(k, carry):
        local = cols_ref[row, k] - slot_ref[SLOTS]
        at = slot_ref[local // per_dev] * per_dev + local % per_dev
        total_ref[at] = total_ref[at] + blocks_ref[0, k].astype(jnp.float32)
        return carry

    lax.fori_loop(0, count, add, 0)
    for at in range(places):
        out_ref[:, at * block : (at + 1) * block] = total_ref[at].astype(jnp.bfloat16)


def link_kernel(offset, sizes, flag_ref, dense_ref, *refs):
    parts = [refs[6 * i : 6 * i + 6] for i in range(len(sizes))]
    out_ref, token_ref, matrix, window, total, result, mat_sems, sems, out_sem = refs[-9:]
    token_ref[...] = jnp.zeros_like(token_ref)
    seg_dev = dense_ref.shape[0]
    width = sum(sizes)
    starts = [sum(sizes[:i]) for i in range(len(sizes))]

    def copies(slot, which):
        return [
            pltpu.make_async_copy(
                part[which], window.at[slot, :, pl.ds(start, size)], sems.at[slot, i]
            )
            for i, (part, start, size) in enumerate(zip(parts, starts, sizes))
        ]

    def columns(slot):
        return pltpu.make_async_copy(
            dense_ref.at[:, pl.ds(slot * seg_dev, seg_dev)], matrix.at[slot], mat_sems.at[slot]
        )

    for slot in range(SLOTS):
        columns(slot).start()
        if slot == 3:
            @pl.when(flag_ref[0] == 0)
            def _():
                for copy in copies(3, 3):
                    copy.start()

            @pl.when(flag_ref[0] == 1)
            def _():
                for copy in copies(3, 5):
                    copy.start()
        else:
            for copy in copies(slot, slot):
                copy.start()

    for slot in range(SLOTS):
        columns(slot).wait()
        for copy in copies(slot, 0):
            copy.wait()
        part = jnp.dot(matrix[slot], window[slot], preferred_element_type=jnp.float32)
        if slot == 0:
            total[...] = part
        elif slot < SLOTS - 1:
            total[...] += part
        else:
            result[...] = (total[...] + part).astype(jnp.bfloat16)
    out = pltpu.make_async_copy(result, out_ref.at[:, pl.ds(offset, width)], out_sem)
    out.start()
    out.wait()


def shards(base_currents, term_rows, term_owner, term_slot, inductance, block_cols):
    devices = lax.axis_size("row")
    me = lax.axis_index("row")
    seg_dev, width = base_currents.shape
    capacity = max(2, 2 * term_rows.shape[0] // devices)
    slots = devices * capacity
    rows_dev, count, block, _ = inductance.shape

    core, side = me % 2, (me // 2) % 2
    across = [(i, i ^ 2) for i in range(devices)]
    partner = [(i, i ^ 1) for i in range(devices)]
    relay = [(i, i + 4) for i in range(devices - 4) if not i & 2]
    relay += [(i + 4, i) for i in range(devices - 4) if i & 2]

    def send(value, pairs):
        return lax.ppermute(value, "row", pairs)

    near = jnp.where(core == 0, 3, 1)
    far = jnp.where(core == 0, 1, 3)
    slot_of = jnp.stack(
        [
            jnp.where(side == 0, 4, 2),
            near,
            jnp.zeros_like(near),
            far,
            jnp.where(side == 0, 2, 4),
            (me - HALO) * rows_dev,
        ]
    ).astype(jnp.int32)
    flag = jnp.where(core == side, 1, 0).astype(jnp.int32).reshape(1)

    outgoing = pl.pallas_call(
        functools.partial(pack_kernel, capacity),
        out_shape=jax.ShapeDtypeStruct((slots, width + LANES), jnp.bfloat16),
        in_specs=[VMEM] * 3,
        out_specs=VMEM,
        compiler_params=limit(16),
        name="pack_terms",
    )(term_owner.reshape(1, -1), term_slot.reshape(1, -1), term_rows)
    arrived = lax.all_to_all(
        outgoing.reshape(devices, capacity, width + LANES), "row", split_axis=0, concat_axis=0, tiled=True
    ).reshape(slots, width + LANES)

    dense, dense_token = pl.pallas_call(
        dense_kernel,
        out_shape=(pltpu.HBM((seg_dev, SLOTS * seg_dev), jnp.bfloat16), TOKEN),
        grid=(rows_dev,),
        in_specs=[SMEM, SMEM, pl.BlockSpec((1, count, block, block), lambda r: (r, 0, 0, 0)), HBM],
        out_specs=(pl.BlockSpec((block, SLOTS * seg_dev), lambda r: (r, 0)), pl.BlockSpec(TOKEN.shape, lambda r: (0, 0))),
        scratch_shapes=[pltpu.VMEM((SLOTS * rows_dev, block, block), jnp.float32)],
        compiler_params=limit(24),
        cost_estimate=pl.CostEstimate(flops=0, bytes_accessed=2 * inductance.size * 2, transcendentals=0),
        name="dense_blocks",
    )(block_cols, slot_of, in_hbm(inductance), in_hbm(outgoing))


    groups = column_cuts(width)
    flat = [size for sizes in groups for size in sizes]
    def inject(offset, sizes):
        return pl.pallas_call(
            functools.partial(inject_kernel, offset),
            out_shape=[jax.ShapeDtypeStruct((seg_dev, size), jnp.bfloat16) for size in sizes],
            in_specs=[VMEM, VMEM, ANY],
            out_specs=[VMEM] * len(sizes),
            compiler_params=limit(24),
            name="inject_terms",
        )(base_currents, arrived, dense_token)

    currents = [*inject(0, flat)]
    peers = []
    for k, current in enumerate(currents):
        if k >= AHEAD:
            current = currents[k] = gate(current, peers[k - AHEAD])
        peers.append(send(current, across))
    passed = [send(peer, relay) for peer in peers]

    def gather(k, token):
        beyond = passed[k]
        if token is not None:
            beyond = gate(beyond, token)
        return [
            currents[k],
            send(currents[k], partner),
            peers[k],
            send(peers[k], partner),
            beyond,
            send(beyond, partner),
        ]

    def link(out, offset, sizes, parts):
        given = [out] if out is not None else []
        total = sum(sizes)
        return pl.pallas_call(
            functools.partial(link_kernel, offset, sizes),
            out_shape=(pltpu.HBM((seg_dev, width), jnp.bfloat16), TOKEN),
            in_specs=[SMEM, HBM] + [HBM] * (len(parts) + len(given)),
            out_specs=(HBM, VMEM),
            scratch_shapes=[
                pltpu.VMEM((SLOTS, seg_dev, seg_dev), jnp.bfloat16),
                pltpu.VMEM((SLOTS, seg_dev, total), jnp.bfloat16),
                pltpu.VMEM((seg_dev, total), jnp.float32),
                pltpu.VMEM((seg_dev, total), jnp.bfloat16),
                pltpu.SemaphoreType.DMA((SLOTS,)),
                pltpu.SemaphoreType.DMA((SLOTS, len(sizes))),
                pltpu.SemaphoreType.DMA,
            ],
            input_output_aliases={2 + len(parts): 0} if given else {},
            compiler_params=limit(40),
            cost_estimate=pl.CostEstimate(
                flops=2 * seg_dev * SLOTS * seg_dev * total, bytes_accessed=0, transcendentals=0
            ),
            name="link_flux",
        )(
            flag,
            in_hbm(dense),
            *[in_hbm(part) for part in parts + given],
        )

    out, token, offset, at = None, None, 0, 0
    for sizes in groups:
        parts = sum([gather(at + i, token) for i in range(len(sizes))], [])
        at += len(sizes)
        out, token = link(out, offset, sizes, parts)
        offset += sum(sizes)
    return out


def solution(mesh):
    placed = (
        P(("group", "row"), None),
        P(("group", "row"), None),
        P(("group", "row"), None),
        P(("group", "row"), None),
        P("row", None, None, None),
        P("row", None),
    )
    return jax.shard_map(
        shards, mesh=mesh, in_specs=placed, out_specs=P(("group", "row"), None), check_vma=False
    )
```

time: 268 us -> 131 us (0.49)
  the two profiles are of different devices: /device:TPU:12 before, /device:TPU:7 now
where the time goes in v1:
time: 131 us; the launch traced here: 130 us
  waiting for transfers between devices  60 us (46%)
  Pallas kernels  41.2 us (31%)
  starting transfers between devices  20.9 us (16%)
  local copies, waits for them, and re-layouts  7.4 us (6%)
    ppermute x15, waiting for transfers between devices, send(): return lax.ppermute(value, 'row', pairs)  45.3 us
    pallas_call x3, Pallas kernels, link(): pl.pallas_call(functools.partial(link_kernel, offset, sizes), out_shape=(...  25.7 us
    all_to_all x1, waiting for transfers between devices, shards(): lax.all_to_all(outgoing.reshape(devices, capacity, width + LANES), 'row',...  14.7 us
    ppermute x15, starting transfers between devices, send(): return lax.ppermute(value, 'row', pairs)  14.2 us
    pallas_call x1, Pallas kernels, shards(): pl.pallas_call(dense_kernel, out_shape=(pltpu.HBM((seg_dev, SLOTS * seg_d...  11.2 us
    unnamed x36, local copies, waits for them, and re-layouts  7.32 us
    all_to_all x1, starting transfers between devices, shards(): lax.all_to_all(outgoing.reshape(devices, capacity, width + LANES), 'row',...  6.66 us
  transfers between devices with their start and end apart: 16, of which 7 were waited for; matrix products, arithmetic and copies ran while one was open for 0% of the time, Pallas kernels for 21%

profile of v1, /device:TPU:7, one launch (start us, length us, event | category | flops | bytes accessed | tf_op | source)
XLA Modules:
  0.0 129.8 jit_solution(333994408484226840)
XLA Ops:
  0.0 0.0 copy-start.2
  0.0 1.1 copy-done.2
  1.1 0.0 copy-start.4
  1.1 0.7 copy-done.4
  1.7 0.0 copy-start.5
  1.7 0.7 copy-done.5
  2.4 1.7 %pack_terms.1.wait_ref = bf16[512,1152]{1,0:T(8,128)(2,1)} custom-call(s32[1,256]{1,0:T(1,128)S(1)} %bitcast.11, s32[1,256]{1,0:T(1,128)S(1)} %bitcast.12, bf16[256,1024]{1,0:T(8,128)(2,1)S(1)} %copy-done.2), custom_call_target="tpu_custom_call" | custom-call | tf_op jit(solution)/shard_map/pack_terms/pallas_call | solution.py:202
  4.1 6.7 %all-to-all-start = ((bf16[16,32,1152]{2,1,0:T(8,128)(2,1)}), bf16[16,32,1152]{2,1,0:T(8,128)(2,1)S(1)}, u32[]{:S(2)}, u32[]{:S(2)}) async-start(bf16[16,32,1152]{2,1,0:T(8,128)(2,1)} %bitcast.8), calls=%async_computation | async-start | bytes 2359296 | tf_op jit(solution)/shard_map/all_to_all | solution.py:210
  10.8 0.1 stack.23.slot_ref
  10.9 0.0 copy-done.3
  10.9 0.0 copy-start
  10.9 11.2 %dense_blocks.1 = (bf16[1024,5120]{1,0:T(8,128)(2,1)}, f32[8,128]{1,0:T(8,128)S(1)}) custom-call(s32[4,20]{1,0:T(4,128)S(1)} %copy-done.3, s32[6]{0:T(128)S(1)} %stack.23.slot_ref, bf16[4,20,256,256]{3,2,1,0:T(8,128)(2,1)} %blocks_ref.1, bf16[512,1152]{1,0:T(8,128)(2,1)} %pack_terms.1.wait_ref), custom_call_target="tpu_custom_call" | custom-call | bytes 20971520 | tf_op jit(solution)/shard_map/dense_blocks/pallas_call | solution.py:214
  22.1 14.7 %all-to-all-done = bf16[16,32,1152]{2,1,0:T(8,128)(2,1)S(1)} async-done(((bf16[16,32,1152]{2,1,0:T(8,128)(2,1)}), bf16[16,32,1152]{2,1,0:T(8,128)(2,1)S(1)}, u32[]{:S(2)}, u32[]{:S(2)}) %all-to-all-start) | async-done | bytes 1179680 | tf_op jit(solution)/shard_map/all_to_all | solution.py:210
  36.8 0.0 copy-done
  36.8 2.6 %inject_terms.1 = (bf16[1024,256]{1,0:T(8,128)(2,1)}, bf16[1024,384]{1,0:T(8,128)(2,1)S(1)}, bf16[1024,384]{1,0:T(8,128)(2,1)}) custom-call(bf16[1024,1024]{1,0:T(8,128)(2,1)S(1)} %copy-done, bf16[512,1152]{1,0:T(8,128)(2,1)S(1)} %bitcast.10, f32[8,128]{1,0:T(8,128)S(1)} %get-tuple-element.16.wait_ref), custom_call_target="tpu_custom_call" | custom-call | tf_op jit(solution)/shard_map/inject_terms/pallas_call | solution.py:230
  39.3 0.0 copy-start.1
  39.3 0.0 collective-permute-start.9
  39.3 0.9 copy-done.1
  40.2 0.6 collective-permute-start.5
  40.8 12.5 %collective-permute-done.9.refs_2_ = bf16[1024,256]{1,0:T(8,128)(2,1)S(1)} collective-permute-done((bf16[1024,256]{1,0:T(8,128)(2,1)}, bf16[1024,256]{1,0:T(8,128)(2,1)S(1)}, u32[]{:S(2)}, u32[]{:S(2)}) %collective-permute-start.9) | collective-permute-done | bytes 524320 | tf_op jit(solution)/shard_map/ppermute | solution.py:186
  53.3 1.3 collective-permute-start.11
  54.6 15.6 %collective-permute-done.5.refs_2_ = bf16[1024,384]{1,0:T(8,128)(2,1)S(1)} collective-permute-done((bf16[1024,384]{1,0:T(8,128)(2,1)S(1)}, bf16[1024,384]{1,0:T(8,128)(2,1)S(1)}, u32[]{:S(2)}, u32[]{:S(2)}) %collective-permute-start.5) | collective-permute-done | bytes 786464 | tf_op jit(solution)/shard_map/ppermute | solution.py:186
  70.2 1.3 collective-permute-start.7
  71.4 0.7 collective-permute-start.8
  72.1 0.1 collective-permute-start.10
  72.2 0.0 collective-permute-done.11.refs_4_
  72.2 0.4 collective-permute-start.12
  72.6 4.0 %collective-permute-start.1 = (bf16[1024,384]{1,0:T(8,128)(2,1)}, bf16[1024,384]{1,0:T(8,128)(2,1)S(1)}, u32[]{:S(2)}, u32[]{:S(2)}) collective-permute-start(bf16[1024,384]{1,0:T(8,128)(2,1)} %get-tuple-element.17.refs_0_), channel_id=1, source_target_pairs={{0,2},{1,3},{2,0},{3,1},{4,6},{5,7},{6,4},{7,5},{8,10},{9,11},{10,... | collective-permute-start | bytes 2359304 | tf_op jit(solution)/shard_map/ppermute | solution.py:186
  76.6 0.0 collective-permute-done.8.refs_1_
  76.6 0.3 collective-permute-start.4
  77.0 0.0 collective-permute-done.10.refs_3_
  77.0 0.2 collective-permute-start.6
  77.1 0.0 collective-permute-done.12.refs_5_
  77.1 0.0 copy-done.16
  77.1 0.0 copy-done.17
  77.1 7.9 %link_flux.3 = (bf16[1024,1024]{1,0:T(8,128)(2,1)}, f32[8,128]{1,0:T(8,128)S(1)}) custom-call(s32[1]{0:T(128)} %bitcast.flag_ref, bf16[1024,5120]{1,0:T(8,128)(2,1)} %get-tuple-element.15.dense_ref, bf16[1024,256]{1,0:T(8,128)(2,1)} %get-tuple-element.19.refs_0_, bf16[1024,256]{1,0:T(8,128)(2,1)} %collective-permute-done.8.refs_1_, ...), custom_call_target="tpu_custom_call" | custom-call | flops 2684354560 | tf_op jit(solution)/shard_map/link_flux/pallas_call | solution.py:263
  85.1 0.0 copy-done.8
  85.1 6.4 %collective-permute-done.7.refs_0_ = bf16[1024,384]{1,0:T(8,128)(2,1)S(1)} collective-permute-done((bf16[1024,384]{1,0:T(8,128)(2,1)S(1)}, bf16[1024,384]{1,0:T(8,128)(2,1)S(1)}, u32[]{:S(2)}, u32[]{:S(2)}) %collective-permute-start.7) | collective-permute-done | bytes 786464 | tf_op jit(solution)/shard_map/ppermute | solution.py:186
  91.5 0.9 copy-done.6
  92.3 1.6 %collective-permute-start.13 = (bf16[1024,384]{1,0:T(8,128)(2,1)}, bf16[1024,384]{1,0:T(8,128)(2,1)S(1)}, u32[]{:S(2)}, u32[]{:S(2)}) collective-permute-start(bf16[1024,384]{1,0:T(8,128)(2,1)} %gate.2.refs_4_), channel_id=1, source_target_pairs={{0,1},{1,0},{2,3},{3,2},{4,5},{5,4},{6,7},{7,6},{8,9},{9,8},{10,11... | collective-permute-start | bytes 2359304 | tf_op jit(solution)/shard_map/ppermute | solution.py:186
  94.0 0.7 collective-permute-done.1.refs_2_
  94.6 1.5 %collective-permute-start.3 = (bf16[1024,384]{1,0:T(8,128)(2,1)S(1)}, bf16[1024,384]{1,0:T(8,128)(2,1)S(1)}, u32[]{:S(2)}, u32[]{:S(2)}) collective-permute-start(bf16[1024,384]{1,0:T(8,128)(2,1)S(1)} %collective-permute-done.1.refs_2_), channel_id=1, source_target_pairs={{0,4},{1,5},{4,8},{5,9},{8,12},{9,13},{6,2},{7,3},{10,6},{11,7},{1... | collective-permute-start | bytes 2359304 | tf_op jit(solution)/shard_map/ppermute | solution.py:186
  96.1 0.7 collective-permute-start
  96.8 0.0 collective-permute-done.4.refs_1_
  96.8 0.1 collective-permute-start.2
  96.9 0.0 collective-permute-done.6.refs_3_
  96.9 0.0 collective-permute-done.13.refs_5_
  96.9 0.0 copy-start.14
  96.9 0.8 copy-done.10
  97.7 0.2 copy-done.11
  98.0 0.2 copy-done.14
  98.2 8.6 %link_flux.4 = (bf16[1024,1024]{1,0:T(8,128)(2,1)}, f32[8,128]{1,0:T(8,128)S(1)}) custom-call(s32[1]{0:T(128)} %bitcast.flag_ref, bf16[1024,5120]{1,0:T(8,128)(2,1)} %get-tuple-element.15.dense_ref, bf16[1024,384]{1,0:T(8,128)(2,1)} %copy-done.1, bf16[1024,384]{1,0:T(8,128)(2,1)} %copy-done.10, ...), custom_call_target="tpu_custom_call", output_to_operand_aliasing={{0}: (8, {})} | custom-call | flops 4026531840 | tf_op jit(solution)/shard_map/link_flux/pallas_call | solution.py:263
  106.8 0.0 copy-done.9
  106.8 8.1 %collective-permute-done.3.refs_0_ = bf16[1024,384]{1,0:T(8,128)(2,1)S(1)} collective-permute-done((bf16[1024,384]{1,0:T(8,128)(2,1)S(1)}, bf16[1024,384]{1,0:T(8,128)(2,1)S(1)}, u32[]{:S(2)}, u32[]{:S(2)}) %collective-permute-start.3) | collective-permute-done | bytes 786464 | tf_op jit(solution)/shard_map/ppermute | solution.py:186
  114.9 0.9 copy-done.7
  115.9 1.5 %collective-permute-start.14 = (bf16[1024,384]{1,0:T(8,128)(2,1)}, bf16[1024,384]{1,0:T(8,128)(2,1)S(1)}, u32[]{:S(2)}, u32[]{:S(2)}) collective-permute-start(bf16[1024,384]{1,0:T(8,128)(2,1)} %gate.3.refs_4_), channel_id=1, source_target_pairs={{0,1},{1,0},{2,3},{3,2},{4,5},{5,4},{6,7},{7,6},{8,9},{9,8},{10,11... | collective-permute-start | bytes 2359304 | tf_op jit(solution)/shard_map/ppermute | solution.py:186
  117.4 0.0 collective-permute-done.refs_1_
  117.4 0.0 collective-permute-done.2.refs_3_
  117.4 0.0 copy-start.13
  117.4 2.1 %collective-permute-done.14.refs_5_ = bf16[1024,384]{1,0:T(8,128)(2,1)S(1)} collective-permute-done((bf16[1024,384]{1,0:T(8,128)(2,1)}, bf16[1024,384]{1,0:T(8,128)(2,1)S(1)}, u32[]{:S(2)}, u32[]{:S(2)}) %collective-permute-start.14) | collective-permute-done | bytes 786464 | tf_op jit(solution)/shard_map/ppermute | solution.py:186
  119.5 0.0 copy-done.12
  119.5 0.0 copy-done.13
  119.5 0.9 copy-done.15
  120.4 9.2 %link_flux.5 = (bf16[1024,1024]{1,0:T(8,128)(2,1)}, f32[8,128]{1,0:T(8,128)}) custom-call(s32[1]{0:T(128)} %bitcast.flag_ref, bf16[1024,5120]{1,0:T(8,128)(2,1)} %get-tuple-element.15.dense_ref, bf16[1024,384]{1,0:T(8,128)(2,1)} %get-tuple-element.17.refs_0_, bf16[1024,384]{1,0:T(8,128)(2,1)} %copy-done.12, ...), custom_call_target="tpu_custom_call", output_to_operand_aliasing={{0}: (8, {})} | custom-call | flops 4026531840 | tf_op jit(solution)/shard_map/link_flux/pallas_call | solution.py:263
  (13 shorter events, 0.0 us)
Async XLA Ops:
  0.0 10.9 %copy-start.3 = (s32[4,20]{1,0:T(4,128)S(1)}, s32[4,20]{1,0:T(4,128)}, u32[]{:S(2)}) copy-start(s32[4,20]{1,0:T(4,128)} %cols_ref.1) | copy-start | bytes 964
  0.0 1.1 copy-start.2
  1.1 0.7 copy-start.4
  1.7 0.7 copy-start.5
  4.1 32.6 %all-to-all-start = ((bf16[16,32,1152]{2,1,0:T(8,128)(2,1)}), bf16[16,32,1152]{2,1,0:T(8,128)(2,1)S(1)}, u32[]{:S(2)}, u32[]{:S(2)}) async-start(bf16[16,32,1152]{2,1,0:T(8,128)(2,1)} %bitcast.8), calls=%async_computation | async-start | bytes 2359296 | tf_op jit(solution)/shard_map/all_to_all | solution.py:210
  10.9 25.9 %copy-start = (bf16[1024,1024]{1,0:T(8,128)(2,1)S(1)}, bf16[1024,1024]{1,0:T(8,128)(2,1)}, u32[]{:S(2)}) copy-start(bf16[1024,1024]{1,0:T(8,128)(2,1)} %base_ref.1) | copy-start | bytes 6291460
  39.3 0.9 copy-start.1
  39.3 14.0 %collective-permute-start.9 = (bf16[1024,256]{1,0:T(8,128)(2,1)}, bf16[1024,256]{1,0:T(8,128)(2,1)S(1)}, u32[]{:S(2)}, u32[]{:S(2)}) collective-permute-start(bf16[1024,256]{1,0:T(8,128)(2,1)} %get-tuple-element.19.refs_0_), channel_id=1, source_target_pairs={{0,2},{1,3},{2,0},{3,1},{4,6},{5,7},{6,4},{7,5},{8,10},{9,11},{10,... | collective-permute-start | bytes 1572872 | tf_op jit(solution)/shard_map/ppermute | solution.py:186
  40.2 29.9 %collective-permute-start.5 = (bf16[1024,384]{1,0:T(8,128)(2,1)S(1)}, bf16[1024,384]{1,0:T(8,128)(2,1)S(1)}, u32[]{:S(2)}, u32[]{:S(2)}) collective-permute-start(bf16[1024,384]{1,0:T(8,128)(2,1)S(1)} %get-tuple-element.18.refs_0_), channel_id=1, source_target_pairs={{0,2},{1,3},{2,0},{3,1},{4,6},{5,7},{6,4},{7,5},{8,10},{9,11},{10,... | collective-permute-start | bytes 2359304 | tf_op jit(solution)/shard_map/ppermute | solution.py:186
  53.3 23.8 %copy-start.16 = (bf16[1024,256]{1,0:T(8,128)(2,1)}, bf16[1024,256]{1,0:T(8,128)(2,1)S(1)}, u32[]{:S(2)}) copy-start(bf16[1024,256]{1,0:T(8,128)(2,1)S(1)} %collective-permute-done.9.refs_2_) | copy-start | bytes 1572868
  53.3 18.9 %collective-permute-start.11 = (bf16[1024,256]{1,0:T(8,128)(2,1)S(1)}, bf16[1024,256]{1,0:T(8,128)(2,1)S(1)}, u32[]{:S(2)}, u32[]{:S(2)}) collective-permute-start(bf16[1024,256]{1,0:T(8,128)(2,1)S(1)} %collective-permute-done.9.refs_2_), channel_id=1, source_target_pairs={{0,4},{1,5},{4,8},{5,9},{8,12},{9,13},{6,2},{7,3},{10,6},{11,7},{1... | collective-permute-start | bytes 1572872 | tf_op jit(solution)/shard_map/ppermute | solution.py:186
  70.2 14.9 %copy-start.8 = (bf16[1024,384]{1,0:T(8,128)(2,1)}, bf16[1024,384]{1,0:T(8,128)(2,1)S(1)}, u32[]{:S(2)}) copy-start(bf16[1024,384]{1,0:T(8,128)(2,1)S(1)} %collective-permute-done.5.refs_2_) | copy-start | bytes 2359300
  70.2 21.3 %collective-permute-start.7 = (bf16[1024,384]{1,0:T(8,128)(2,1)S(1)}, bf16[1024,384]{1,0:T(8,128)(2,1)S(1)}, u32[]{:S(2)}, u32[]{:S(2)}) collective-permute-start(bf16[1024,384]{1,0:T(8,128)(2,1)S(1)} %collective-permute-done.5.refs_2_), channel_id=1, source_target_pairs={{0,4},{1,5},{4,8},{5,9},{8,12},{9,13},{6,2},{7,3},{10,6},{11,7},{1... | collective-permute-start | bytes 2359304 | tf_op jit(solution)/shard_map/ppermute | solution.py:186
  71.4 5.2 %collective-permute-start.8 = (bf16[1024,256]{1,0:T(8,128)(2,1)}, bf16[1024,256]{1,0:T(8,128)(2,1)}, u32[]{:S(2)}, u32[]{:S(2)}) collective-permute-start(bf16[1024,256]{1,0:T(8,128)(2,1)} %get-tuple-element.19.refs_0_), channel_id=1, source_target_pairs={{0,1},{1,0},{2,3},{3,2},{4,5},{5,4},{6,7},{7,6},{8,9},{9,8},{10,11... | collective-permute-start | bytes 1572872 | tf_op jit(solution)/shard_map/ppermute | solution.py:186
  72.1 4.9 %collective-permute-start.10 = (bf16[1024,256]{1,0:T(8,128)(2,1)S(1)}, bf16[1024,256]{1,0:T(8,128)(2,1)}, u32[]{:S(2)}, u32[]{:S(2)}) collective-permute-start(bf16[1024,256]{1,0:T(8,128)(2,1)S(1)} %collective-permute-done.9.refs_2_), channel_id=1, source_target_pairs={{0,1},{1,0},{2,3},{3,2},{4,5},{5,4},{6,7},{7,6},{8,9},{9,8},{10,11... | collective-permute-start | bytes 1572872 | tf_op jit(solution)/shard_map/ppermute | solution.py:186
  72.2 4.9 %copy-start.17 = (bf16[1024,256]{1,0:T(8,128)(2,1)}, bf16[1024,256]{1,0:T(8,128)(2,1)S(1)}, u32[]{:S(2)}) copy-start(bf16[1024,256]{1,0:T(8,128)(2,1)S(1)} %collective-permute-done.11.refs_4_) | copy-start | bytes 1572868
  72.2 4.9 %collective-permute-start.12 = (bf16[1024,256]{1,0:T(8,128)(2,1)S(1)}, bf16[1024,256]{1,0:T(8,128)(2,1)}, u32[]{:S(2)}, u32[]{:S(2)}) collective-permute-start(bf16[1024,256]{1,0:T(8,128)(2,1)S(1)} %collective-permute-done.11.refs_4_), channel_id=1, source_target_pairs={{0,1},{1,0},{2,3},{3,2},{4,5},{5,4},{6,7},{7,6},{8,9},{9,8},{10,11... | collective-permute-start | bytes 1572872 | tf_op jit(solution)/shard_map/ppermute | solution.py:186
  72.6 22.0 %collective-permute-start.1 = (bf16[1024,384]{1,0:T(8,128)(2,1)}, bf16[1024,384]{1,0:T(8,128)(2,1)S(1)}, u32[]{:S(2)}, u32[]{:S(2)}) collective-permute-start(bf16[1024,384]{1,0:T(8,128)(2,1)} %get-tuple-element.17.refs_0_), channel_id=1, source_target_pairs={{0,2},{1,3},{2,0},{3,1},{4,6},{5,7},{6,4},{7,5},{8,10},{9,11},{10,... | collective-permute-start | bytes 2359304 | tf_op jit(solution)/shard_map/ppermute | solution.py:186
  76.6 20.2 %collective-permute-start.4 = (bf16[1024,384]{1,0:T(8,128)(2,1)}, bf16[1024,384]{1,0:T(8,128)(2,1)S(1)}, u32[]{:S(2)}, u32[]{:S(2)}) collective-permute-start(bf16[1024,384]{1,0:T(8,128)(2,1)} %copy-done.1), channel_id=1, source_target_pairs={{0,1},{1,0},{2,3},{3,2},{4,5},{5,4},{6,7},{7,6},{8,9},{9,8},{10,11... | collective-permute-start | bytes 2359304 | tf_op jit(solution)/shard_map/ppermute | solution.py:186
  77.0 20.0 %collective-permute-start.6 = (bf16[1024,384]{1,0:T(8,128)(2,1)S(1)}, bf16[1024,384]{1,0:T(8,128)(2,1)S(1)}, u32[]{:S(2)}, u32[]{:S(2)}) collective-permute-start(bf16[1024,384]{1,0:T(8,128)(2,1)S(1)} %collective-permute-done.5.refs_2_), channel_id=1, source_target_pairs={{0,1},{1,0},{2,3},{3,2},{4,5},{5,4},{6,7},{7,6},{8,9},{9,8},{10,11... | collective-permute-start | bytes 2359304 | tf_op jit(solution)/shard_map/ppermute | solution.py:186
  91.4 0.9 copy-start.6
  92.3 4.6 %collective-permute-start.13 = (bf16[1024,384]{1,0:T(8,128)(2,1)}, bf16[1024,384]{1,0:T(8,128)(2,1)S(1)}, u32[]{:S(2)}, u32[]{:S(2)}) collective-permute-start(bf16[1024,384]{1,0:T(8,128)(2,1)} %gate.2.refs_4_), channel_id=1, source_target_pairs={{0,1},{1,0},{2,3},{3,2},{4,5},{5,4},{6,7},{7,6},{8,9},{9,8},{10,11... | collective-permute-start | bytes 2359304 | tf_op jit(solution)/shard_map/ppermute | solution.py:186
  94.6 12.2 %copy-start.9 = (bf16[1024,384]{1,0:T(8,128)(2,1)}, bf16[1024,384]{1,0:T(8,128)(2,1)S(1)}, u32[]{:S(2)}) copy-start(bf16[1024,384]{1,0:T(8,128)(2,1)S(1)} %collective-permute-done.1.refs_2_) | copy-start | bytes 2359300
  94.6 20.3 %collective-permute-start.3 = (bf16[1024,384]{1,0:T(8,128)(2,1)S(1)}, bf16[1024,384]{1,0:T(8,128)(2,1)S(1)}, u32[]{:S(2)}, u32[]{:S(2)}) collective-permute-start(bf16[1024,384]{1,0:T(8,128)(2,1)S(1)} %collective-permute-done.1.refs_2_), channel_id=1, source_target_pairs={{0,4},{1,5},{4,8},{5,9},{8,12},{9,13},{6,2},{7,3},{10,6},{11,7},{1... | collective-permute-start | bytes 2359304 | tf_op jit(solution)/shard_map/ppermute | solution.py:186
  96.1 21.3 %collective-permute-start = (bf16[1024,384]{1,0:T(8,128)(2,1)}, bf16[1024,384]{1,0:T(8,128)(2,1)S(1)}, u32[]{:S(2)}, u32[]{:S(2)}) collective-permute-start(bf16[1024,384]{1,0:T(8,128)(2,1)} %get-tuple-element.17.refs_0_), channel_id=1, source_target_pairs={{0,1},{1,0},{2,3},{3,2},{4,5},{5,4},{6,7},{7,6},{8,9},{9,8},{10,11... | collective-permute-start | bytes 2359304 | tf_op jit(solution)/shard_map/ppermute | solution.py:186
  96.8 0.9 copy-start.10
  96.8 20.6 %collective-permute-start.2 = (bf16[1024,384]{1,0:T(8,128)(2,1)S(1)}, bf16[1024,384]{1,0:T(8,128)(2,1)S(1)}, u32[]{:S(2)}, u32[]{:S(2)}) collective-permute-start(bf16[1024,384]{1,0:T(8,128)(2,1)S(1)} %collective-permute-done.1.refs_2_), channel_id=1, source_target_pairs={{0,1},{1,0},{2,3},{3,2},{4,5},{5,4},{6,7},{7,6},{8,9},{9,8},{10,11... | collective-permute-start | bytes 2359304 | tf_op jit(solution)/shard_map/ppermute | solution.py:186
  96.9 1.1 copy-start.11
  96.9 1.3 copy-start.14
  114.9 0.9 copy-start.7
  115.9 3.7 %collective-permute-start.14 = (bf16[1024,384]{1,0:T(8,128)(2,1)}, bf16[1024,384]{1,0:T(8,128)(2,1)S(1)}, u32[]{:S(2)}, u32[]{:S(2)}) collective-permute-start(bf16[1024,384]{1,0:T(8,128)(2,1)} %gate.3.refs_4_), channel_id=1, source_target_pairs={{0,1},{1,0},{2,3},{3,2},{4,5},{5,4},{6,7},{7,6},{8,9},{9,8},{10,11... | collective-permute-start | bytes 2359304 | tf_op jit(solution)/shard_map/ppermute | solution.py:186
  117.4 2.1 %copy-start.12 = (bf16[1024,384]{1,0:T(8,128)(2,1)}, bf16[1024,384]{1,0:T(8,128)(2,1)S(1)}, u32[]{:S(2)}) copy-start(bf16[1024,384]{1,0:T(8,128)(2,1)S(1)} %collective-permute-done.refs_1_) | copy-start | bytes 2359300
  117.4 2.1 %copy-start.13 = (bf16[1024,384]{1,0:T(8,128)(2,1)}, bf16[1024,384]{1,0:T(8,128)(2,1)S(1)}, u32[]{:S(2)}) copy-start(bf16[1024,384]{1,0:T(8,128)(2,1)S(1)} %collective-permute-done.2.refs_3_) | copy-start | bytes 2359300
  119.5 0.9 copy-start.15

commit v2 on v1

v2 whole, which is shorter than its diff:
```python
import functools

import jax
import jax.numpy as jnp
from jax import lax
from jax.experimental import pallas as pl
from jax.experimental.pallas import tpu as pltpu
from jax.sharding import PartitionSpec as P

HALO = 2
LANES = 128
RADIX = 32
VMEM = pl.BlockSpec(memory_space=pltpu.VMEM)
SMEM = pl.BlockSpec(memory_space=pltpu.SMEM)
HBM = pl.BlockSpec(memory_space=pltpu.HBM)
ANY = pl.BlockSpec(memory_space=pl.ANY)
SLOTS = 2 * HALO + 1
TOKEN = jax.ShapeDtypeStruct((8, LANES), jnp.float32)
HANDS = 3
LATE = 1
MIB = 1024 * 1024


def limit(mib):
    return pltpu.CompilerParams(vmem_limit_bytes=mib * MIB)


def in_hbm(value):
    return pltpu.with_memory_space_constraint(value, pltpu.HBM)


def gate_kernel(*refs):
    pass


def gate(value, *others):
    return pl.pallas_call(
        gate_kernel,
        out_shape=jax.ShapeDtypeStruct(value.shape, value.dtype),
        in_specs=[ANY] * (1 + len(others)),
        out_specs=ANY,
        input_output_aliases={0: 0},
        compiler_params=limit(1),
        name="gate",
    )(value, *others)


def chunk_sizes(width):
    unit = width // 8
    return [2 * unit] * 4


def pack_kernel(capacity, owner_ref, target_ref, rows_ref, out_ref):
    count, width = rows_ref.shape
    slots = out_ref.shape[0]
    owner = owner_ref[...]
    target = target_ref[...]
    named = lax.broadcasted_iota(jnp.int32, (LANES, count), 0) == owner
    tri = lax.broadcasted_iota(jnp.int32, (count, count), 0) < lax.broadcasted_iota(
        jnp.int32, (count, count), 1
    )
    earlier = jnp.dot(
        named.astype(jnp.bfloat16), tri.astype(jnp.bfloat16), preferred_element_type=jnp.float32
    )
    order = jnp.sum(jnp.where(named, earlier, 0.0), axis=0, keepdims=True).astype(jnp.int32)
    position = owner * capacity + order
    picker = (lax.broadcasted_iota(jnp.int32, (slots, count), 0) == position).astype(jnp.bfloat16)
    line = lax.broadcasted_iota(jnp.int32, (LANES, count), 0)
    tags = jnp.where(line == 0, target // RADIX + 1, jnp.where(line == 1, target % RADIX, 0))
    tags = tags.astype(jnp.float32).astype(jnp.bfloat16)
    out_ref[:, :width] = jnp.dot(
        picker, rows_ref[...], preferred_element_type=jnp.float32
    ).astype(jnp.bfloat16)
    out_ref[:, width:] = lax.dot_general(
        picker, tags, (((1,), (1,)), ((), ())), preferred_element_type=jnp.float32
    ).astype(jnp.bfloat16)


def inject_kernel(base_ref, arrived_ref, wait_ref, whole_ref, *out_refs):
    offset = 0
    seg_dev = base_ref.shape[0]
    slots = arrived_ref.shape[0]
    width = arrived_ref.shape[1] - LANES
    pick_lane = lax.broadcasted_iota(jnp.int32, (8, LANES), 1)
    weights = jnp.where(pick_lane == 0, float(RADIX), jnp.where(pick_lane == 1, 1.0, 0.0))
    segment = lax.dot_general(
        weights.astype(jnp.bfloat16),
        arrived_ref[:, width:],
        (((1,), (1,)), ((), ())),
        preferred_element_type=jnp.float32,
    )[0:1].astype(jnp.int32) - RADIX
    landing = (lax.broadcasted_iota(jnp.int32, (seg_dev, slots), 0) == segment).astype(jnp.bfloat16)
    for out_ref in out_refs:
        there = slice(offset, offset + out_ref.shape[1])
        injected = jnp.dot(landing, arrived_ref[:, there], preferred_element_type=jnp.float32)
        current = (base_ref[:, there].astype(jnp.float32) + injected).astype(jnp.bfloat16)
        out_ref[...] = current
        whole_ref[:, there] = current
        offset += out_ref.shape[1]


def dense_kernel(cols_ref, slot_ref, blocks_ref, wait_ref, out_ref, token_ref, total_ref):
    row = pl.program_id(0)
    count = blocks_ref.shape[1]
    block = blocks_ref.shape[2]
    per_dev = cols_ref.shape[0]
    places = total_ref.shape[0]
    total_ref[...] = jnp.zeros_like(total_ref)
    token_ref[...] = jnp.zeros_like(token_ref)

    def add(k, carry):
        local = cols_ref[row, k] - slot_ref[SLOTS]
        at = slot_ref[local // per_dev] * per_dev + local % per_dev
        total_ref[at] = total_ref[at] + blocks_ref[0, k].astype(jnp.float32)
        return carry

    lax.fori_loop(0, count, add, 0)
    for at in range(places):
        out_ref[:, at * block : (at + 1) * block] = total_ref[at].astype(jnp.bfloat16)


def hand_kernel(sizes, flag_ref, *refs):
    count = len(sizes)
    peers, passed = refs[:count], refs[count : 2 * count]
    out_ref, sems = refs[-2:]

    def copies(sources):
        return [
            pltpu.make_async_copy(
                source, out_ref.at[:, pl.ds(sum(sizes[:i]), sizes[i])], sems.at[i]
            )
            for i, source in enumerate(sources)
        ]

    @pl.when(flag_ref[1] == 0)
    def _():
        for copy in copies(peers):
            copy.start()

    @pl.when(flag_ref[1] == 1)
    def _():
        for copy in copies(passed):
            copy.start()

    for copy in copies(peers):
        copy.wait()


class Slots:
    def __init__(self, dense_ref, slots, matrix, window, mat_sems, sems):
        self.dense, self.slots = dense_ref, slots
        self.matrix, self.window, self.mat_sems, self.sems = matrix, window, mat_sems, sems

    def copies(self, slot):
        depth = self.dense.shape[0]
        columns = self.dense.at[:, pl.ds(slot * depth, depth)]
        made = [pltpu.make_async_copy(columns, self.matrix.at[slot], self.mat_sems.at[slot])]
        start = 0
        for i, piece in enumerate(self.slots[slot]):
            target = self.window.at[slot, :, pl.ds(start, piece.shape[1])]
            made.append(pltpu.make_async_copy(piece, target, self.sems.at[slot, i]))
            start += piece.shape[1]
        return made, start

    def begin(self, slot):
        for copy in self.copies(slot)[0]:
            copy.start()

    def sum_into(self, total_ref):
        self.begin(0)
        self.begin(1)
        for slot in range(len(self.slots)):
            made, wide = self.copies(slot)
            for copy in made:
                copy.wait()
            if slot + 2 < len(self.slots):
                self.begin(slot + 2)
            part = jnp.dot(
                self.matrix[slot], self.window[slot, :, :wide], preferred_element_type=jnp.float32
            )
            if slot == 0:
                total_ref[...] = part
            else:
                total_ref[:, :wide] += part


def part_kernel(offset, counts, dense_ref, own, beside, *refs):
    total_ref, token_ref, matrix, window, mat_sems, sems = refs[-6:]
    token_ref[...] = jnp.zeros_like(token_ref)
    there = pl.ds(offset, total_ref.shape[1])
    slots = [[own.at[:, there]], [beside.at[:, there]]]
    at = 0
    for count in counts:
        slots.append(refs[at : at + count])
        at += count
    Slots(dense_ref, slots, matrix, window, mat_sems, sems).sum_into(total_ref)


def last_kernel(plan, flag_ref, dense_ref, *refs):
    count = sum(len(item["inputs"]) for item in plan)
    inputs, outs = refs[:count], refs[count:]
    out_ref, matrix, window, extra, sums, result, mat_sems, row_sems, extra_sems, sum_sems, out_sems = outs
    seg_dev = dense_ref.shape[0]

    def columns(at, slot):
        there = dense_ref.at[:, pl.ds(slot * seg_dev, seg_dev)]
        return pltpu.make_async_copy(there, matrix.at[at], mat_sems.at[at])

    chunks, at = [], 0
    for i, item in enumerate(plan):
        chunk = dict(item, at=pl.ds(item["start"], item["size"]))
        chunk["given"] = inputs[at : at + len(item["inputs"])]
        at += len(item["inputs"])
        chunks.append(chunk)

    def into(target, sem, source):
        return pltpu.make_async_copy(source, target, sem)

    def sum_of(i, chunk):
        there = pl.ds(chunk["sum_start"], chunk["size"])
        return into(sums.at[:, chunk["at"]], sum_sems.at[i], chunk["given"][0].at[:, there])

    def rows_of(i, chunk, source):
        return into(window.at[:, chunk["at"]], row_sems.at[i], source)

    def extra_of(i, chunk):
        return into(extra.at[:, chunk["at"]], extra_sems.at[i], chunk["given"][-1])

    def result_of(i, chunk):
        return into(out_ref.at[:, chunk["at"]], out_sems.at[i], result.at[:, chunk["at"]])

    def begin(i, chunk):
        sum_of(i, chunk).start()
        if chunk["handed"]:
            rows_of(i, chunk, chunk["given"][1].at[:, chunk["at"]]).start()
        else:
            @pl.when(flag_ref[0] == 0)
            def _():
                rows_of(i, chunk, chunk["given"][1]).start()

            @pl.when(flag_ref[0] == 1)
            def _():
                rows_of(i, chunk, chunk["given"][2]).start()

        if chunk["relayed"]:
            extra_of(i, chunk).start()

    columns(0, SLOTS - 1).start()
    begin(0, chunks[0])
    begin(1, chunks[1])
    columns(1, SLOTS - 2).start()
    columns(0, SLOTS - 1).wait()
    waited = False
    for i, chunk in enumerate(chunks):
        if i + 2 < len(chunks):
            begin(i + 2, chunks[i + 2])
        rows_of(i, chunk, out_ref.at[:, chunk["at"]]).wait()
        sum_of(i, chunk).wait()
        there = chunk["at"]
        total = sums[:, there] + jnp.dot(matrix[0], window[:, there], preferred_element_type=jnp.float32)
        if chunk["relayed"]:
            if not waited:
                columns(1, SLOTS - 2).wait()
                waited = True
            extra_of(i, chunk).wait()
            total += jnp.dot(matrix[1], extra[:, there], preferred_element_type=jnp.float32)
        result[:, there] = total.astype(jnp.bfloat16)
        result_of(i, chunk).start()
    for i, chunk in enumerate(chunks):
        result_of(i, chunk).wait()


def shards(base_currents, term_rows, term_owner, term_slot, inductance, block_cols):
    devices = lax.axis_size("row")
    me = lax.axis_index("row")
    seg_dev, width = base_currents.shape
    capacity = max(2, 2 * term_rows.shape[0] // devices)
    slots = devices * capacity
    rows_dev, count, block, _ = inductance.shape

    core, side = me % 2, (me // 2) % 2
    across = [(i, i ^ 2) for i in range(devices)]
    partner = [(i, i ^ 1) for i in range(devices)]
    relay = [(i, i + 4) for i in range(devices - 4) if not i & 2]
    relay += [(i + 4, i) for i in range(devices - 4) if i & 2]

    def send(value, pairs):
        return lax.ppermute(value, "row", pairs)

    near = jnp.where(core == 0, 4, 1)
    far = jnp.where(core == 0, 1, 4)
    slot_of = jnp.stack(
        [
            jnp.where(side == 0, 3, 2),
            near,
            jnp.zeros_like(near),
            far,
            jnp.where(side == 0, 2, 3),
            (me - HALO) * rows_dev,
        ]
    ).astype(jnp.int32)
    flag = jnp.stack([core == side, core != side]).astype(jnp.int32)

    outgoing = pl.pallas_call(
        functools.partial(pack_kernel, capacity),
        out_shape=jax.ShapeDtypeStruct((slots, width + LANES), jnp.bfloat16),
        in_specs=[VMEM] * 3,
        out_specs=VMEM,
        compiler_params=limit(16),
        name="pack_terms",
    )(term_owner.reshape(1, -1), term_slot.reshape(1, -1), term_rows)
    arrived = lax.all_to_all(
        outgoing.reshape(devices, capacity, width + LANES), "row", split_axis=0, concat_axis=0, tiled=True
    ).reshape(slots, width + LANES)

    dense, dense_token = pl.pallas_call(
        dense_kernel,
        out_shape=(pltpu.HBM((seg_dev, SLOTS * seg_dev), jnp.bfloat16), TOKEN),
        grid=(rows_dev,),
        in_specs=[SMEM, SMEM, pl.BlockSpec((1, count, block, block), lambda r: (r, 0, 0, 0)), HBM],
        out_specs=(pl.BlockSpec((block, SLOTS * seg_dev), lambda r: (r, 0)), pl.BlockSpec(TOKEN.shape, lambda r: (0, 0))),
        scratch_shapes=[pltpu.VMEM((SLOTS * rows_dev, block, block), jnp.float32)],
        compiler_params=limit(24),
        cost_estimate=pl.CostEstimate(flops=0, bytes_accessed=0, transcendentals=0),
        name="dense_blocks",
    )(block_cols, slot_of, in_hbm(inductance), in_hbm(outgoing))


    sizes = chunk_sizes(width)
    starts = [sum(sizes[:k]) for k in range(len(sizes))]
    whole, *currents = pl.pallas_call(
        inject_kernel,
        out_shape=[
            jax.ShapeDtypeStruct((seg_dev, wide), jnp.bfloat16) for wide in [width] + sizes
        ],
        in_specs=[VMEM, VMEM, ANY],
        out_specs=[VMEM] * (1 + len(sizes)),
        compiler_params=limit(24),
        name="inject_terms",
    )(base_currents, arrived, dense_token)

    def cost():
        return pl.CostEstimate(flops=0, bytes_accessed=0, transcendentals=0)

    beside = send(whole, partner)
    peers = [send(current, across) for current in currents]

    passed = [send(peer, relay) for peer in peers]

    def part(start, slots, after):
        wide = sum(piece.shape[1] for piece in slots[0])
        given = [dense, whole, beside] + [piece for slot in slots for piece in slot]
        most = max(len(slot) for slot in slots)
        count = 2 + len(slots)
        return pl.pallas_call(
            functools.partial(part_kernel, start, [len(slot) for slot in slots]),
            out_shape=(pltpu.HBM((seg_dev, wide), jnp.float32), TOKEN),
            in_specs=[HBM] * len(given) + [ANY] * len(after),
            out_specs=(VMEM, VMEM),
            scratch_shapes=[
                pltpu.VMEM((count, seg_dev, seg_dev), jnp.bfloat16),
                pltpu.VMEM((count, seg_dev, wide), jnp.bfloat16),
                pltpu.SemaphoreType.DMA((count,)),
                pltpu.SemaphoreType.DMA((count, most)),
            ],
            compiler_params=limit(32),
            cost_estimate=cost(),
            name="part_flux",
        )(*[in_hbm(item) for item in given], *after)

    first, token = part(0, [peers[:2], passed[:2]], [])
    hands = HANDS
    mine = pl.pallas_call(
        functools.partial(hand_kernel, sizes[:hands]),
        out_shape=jax.ShapeDtypeStruct((seg_dev, sum(sizes[:hands])), jnp.bfloat16),
        in_specs=[SMEM] + [HBM] * (2 * hands) + [ANY],
        out_specs=VMEM,
        scratch_shapes=[pltpu.SemaphoreType.DMA((hands,))],
        compiler_params=limit(8),
        cost_estimate=cost(),
        name="hand_over",
    )(flag, *[in_hbm(item) for item in peers[:hands] + passed[:hands]], token)
    handed = send(mine, partner)
    second, token = part(starts[2], [peers[2:]] + ([passed[2:3]] if LATE else []), [mine])
    beyond = gate(passed[3], token)
    plan, parts = [], []
    for k, size in enumerate(sizes):
        item = dict(start=starts[k], size=size, handed=k < hands)
        item["sum_start"] = starts[k] if k < 2 else starts[k] - starts[2]
        item["relayed"] = k == 3 or (k == 2 and not LATE)
        last = beyond if k == 3 else passed[k]
        item["inputs"] = [first if k < 2 else second]
        if k < hands:
            item["inputs"] += [handed]
        else:
            item["inputs"] += [send(peers[k], partner), send(last, partner)]
        if item["relayed"]:
            item["inputs"] += [last]
        parts += item["inputs"]
        plan.append(item)
    plan = [dict(item, inputs=[0] * len(item["inputs"])) for item in plan]
    return pl.pallas_call(
        functools.partial(last_kernel, plan),
        out_shape=pltpu.HBM((seg_dev, width), jnp.bfloat16),
        in_specs=[SMEM, HBM] + [ANY] * len(parts),
        out_specs=HBM,
        scratch_shapes=[
            pltpu.VMEM((2, seg_dev, seg_dev), jnp.bfloat16),
            pltpu.VMEM((seg_dev, width), jnp.bfloat16),
            pltpu.VMEM((seg_dev, width), jnp.bfloat16),
            pltpu.VMEM((seg_dev, width), jnp.float32),
            pltpu.VMEM((seg_dev, width), jnp.bfloat16),
            pltpu.SemaphoreType.DMA((2,)),
            pltpu.SemaphoreType.DMA((len(sizes),)),
            pltpu.SemaphoreType.DMA((len(sizes),)),
            pltpu.SemaphoreType.DMA((len(sizes),)),
            pltpu.SemaphoreType.DMA((len(sizes),)),
        ],
        compiler_params=limit(32),
        cost_estimate=cost(),
        name="last_flux",
    )(flag, in_hbm(dense), *[in_hbm(p) if p is first or p is second or p is handed else p for p in parts])


def solution(mesh):
    placed = (
        P(("group", "row"), None),
        P(("group", "row"), None),
        P(("group", "row"), None),
        P(("group", "row"), None),
        P("row", None, None, None),
        P("row", None),
    )
    return jax.shard_map(
        shards, mesh=mesh, in_specs=placed, out_specs=P(("group", "row"), None), check_vma=False
    )
```

time: 131 us -> 126 us (0.962)
  waiting for transfers between devices: 60 us -> 56.3 us
  local copies, waits for them, and re-layouts: 7.4 us -> 6.03 us
    ppermute x15 -> x12, waiting for transfers between devices: 45.3 us -> 41.4 us  [send(): return lax.ppermute(value, 'row', pairs)]
    unnamed x36 -> x22, local copies, waits for them, and re-layouts: 7.32 us -> 5.95 us
    ppermute x15 -> x12, starting transfers between devices: 14.2 us -> 13.8 us  [send(): return lax.ppermute(value, 'row', pairs)]
  transfers between devices with their start and end apart: 16 -> 13, of which waited for: 7 -> 7; matrix products, arithmetic and copies ran while one was open for 0% -> 0% of each run, Pallas kernels for 21% -> 24%
where the time goes in v2:
time: 126 us; the launch traced here: 125 us
  waiting for transfers between devices  56.3 us (45%)
  Pallas kernels  41.8 us (33%)
  starting transfers between devices  20.5 us (16%)
  local copies, waits for them, and re-layouts  6.03 us (5%)
    ppermute x12, waiting for transfers between devices, send(): return lax.ppermute(value, 'row', pairs)  41.4 us
    pallas_call x2, Pallas kernels, part(): pl.pallas_call(functools.partial(part_kernel, start, [len(slot) for slot...  16.5 us
    all_to_all x1, waiting for transfers between devices, shards(): lax.all_to_all(outgoing.reshape(devices, capacity, width + LANES), 'row',...  14.8 us
    ppermute x12, starting transfers between devices, send(): return lax.ppermute(value, 'row', pairs)  13.8 us
    pallas_call x1, Pallas kernels, shards(): pl.pallas_call(dense_kernel, out_shape=(pltpu.HBM((seg_dev, SLOTS * seg_d...  11.1 us
    pallas_call x1, Pallas kernels, shards(): pl.pallas_call(functools.partial(last_kernel, plan), out_shape=pltpu.HBM(...  9.26 us
    all_to_all x1, starting transfers between devices, shards(): lax.all_to_all(outgoing.reshape(devices, capacity, width + LANES), 'row',...  6.67 us
    unnamed x22, local copies, waits for them, and re-layouts  5.95 us
  transfers between devices with their start and end apart: 13, of which 7 were waited for; matrix products, arithmetic and copies ran while one was open for 0% of the time, Pallas kernels for 24%

profile of v2, /device:TPU:7, one launch (start us, length us, event | category | flops | bytes accessed | tf_op | source)
XLA Modules:
  0.0 124.8 jit_solution(2979804591135254723)
XLA Ops:
  0.0 0.0 copy-start.3
  0.0 0.0 copy-start.2
  0.0 1.1 copy-done.2
  1.1 0.0 copy-start.4
  1.1 0.7 copy-done.4
  1.7 0.0 copy-start.5
  1.7 0.7 copy-done.5
  2.4 1.7 %pack_terms.1.wait_ref = bf16[512,1152]{1,0:T(8,128)(2,1)} custom-call(s32[1,256]{1,0:T(1,128)S(1)} %bitcast.12, s32[1,256]{1,0:T(1,128)S(1)} %bitcast.13, bf16[256,1024]{1,0:T(8,128)(2,1)S(1)} %copy-done.2), custom_call_target="tpu_custom_call" | custom-call | tf_op jit(solution)/shard_map/pack_terms/pallas_call | solution.py:304
  4.1 6.7 %all-to-all-start = ((bf16[16,32,1152]{2,1,0:T(8,128)(2,1)}), bf16[16,32,1152]{2,1,0:T(8,128)(2,1)S(1)}, u32[]{:S(2)}, u32[]{:S(2)}) async-start(bf16[16,32,1152]{2,1,0:T(8,128)(2,1)} %bitcast.9), calls=%async_computation | async-start | bytes 2359296 | tf_op jit(solution)/shard_map/all_to_all | solution.py:312
  10.8 0.1 stack.35.slot_ref
  10.9 0.0 copy-done.3
  10.9 11.1 %dense_blocks.1 = (bf16[1024,5120]{1,0:T(8,128)(2,1)}, f32[8,128]{1,0:T(8,128)S(1)}) custom-call(s32[4,20]{1,0:T(4,128)S(1)} %copy-done.3, s32[6]{0:T(128)S(1)} %stack.35.slot_ref, bf16[4,20,256,256]{3,2,1,0:T(8,128)(2,1)} %blocks_ref.1, bf16[512,1152]{1,0:T(8,128)(2,1)} %pack_terms.1.wait_ref), custom_call_target="tpu_custom_call" | custom-call | tf_op jit(solution)/shard_map/dense_blocks/pallas_call | solution.py:316
  21.9 14.8 %all-to-all-done = bf16[16,32,1152]{2,1,0:T(8,128)(2,1)S(1)} async-done(((bf16[16,32,1152]{2,1,0:T(8,128)(2,1)}), bf16[16,32,1152]{2,1,0:T(8,128)(2,1)S(1)}, u32[]{:S(2)}, u32[]{:S(2)}) %all-to-all-start) | async-done | bytes 1179680 | tf_op jit(solution)/shard_map/all_to_all | solution.py:312
  36.8 0.0 copy-start.1
  36.8 1.6 %copy-done.1 = bf16[1024,1024]{1,0:T(8,128)(2,1)S(1)} copy-done((bf16[1024,1024]{1,0:T(8,128)(2,1)S(1)}, bf16[1024,1024]{1,0:T(8,128)(2,1)}, u32[]{:S(2)}) %copy-start.1) | copy-done | bytes 2097176
  38.4 1.4 %inject_terms.1 = (bf16[1024,1024]{1,0:T(8,128)(2,1)S(1)}, bf16[1024,256]{1,0:T(8,128)(2,1)S(1)}, bf16[1024,256]{1,0:T(8,128)(2,1)S(1)}, bf16[1024,256]{1,0:T(8,128)(2,1)S(1)}, bf16[1024,256]{1,0:T(8,128)(2,1)S(1)}) custom-call(bf16[1024,1024]{1,0:T(8,128)(2,1)S(1)} %copy-done.1, bf16[512,1152]{1,0:T(8,128)(2,1)S(1)} %bitcast.11, ...), custom_call_target="tpu_custom_call" | custom-call | tf_op jit(solution)/shard_map/inject_terms/pallas_call | solution.py:331
  39.7 0.0 copy-start.6
  39.7 0.8 copy-done.6
  40.5 0.0 copy-start
  40.5 0.0 collective-permute-start
  40.6 0.0 collective-permute-start.1
  40.6 1.5 %collective-permute-start.2 = (bf16[1024,256]{1,0:T(8,128)(2,1)S(1)}, bf16[1024,256]{1,0:T(8,128)(2,1)}, u32[]{:S(2)}, u32[]{:S(2)}) collective-permute-start(bf16[1024,256]{1,0:T(8,128)(2,1)S(1)} %get-tuple-element.20), channel_id=1, source_target_pairs={{0,2},{1,3},{2,0},{3,1},{4,6},{5,7},{6,4},{7,5},{8,10},{9,11},{10,... | collective-permute-start | bytes 1572872 | tf_op jit(solution)/shard_map/ppermute | solution.py:288
  42.0 0.1 collective-permute-start.5
  42.1 11.4 %collective-permute-done.1.refs_0_ = bf16[1024,256]{1,0:T(8,128)(2,1)S(1)} collective-permute-done((bf16[1024,256]{1,0:T(8,128)(2,1)S(1)}, bf16[1024,256]{1,0:T(8,128)(2,1)S(1)}, u32[]{:S(2)}, u32[]{:S(2)}) %collective-permute-start.1) | collective-permute-done | bytes 524320 | tf_op jit(solution)/shard_map/ppermute | solution.py:288
  53.5 0.0 copy-start.9
  53.5 1.3 %collective-permute-start.3 = (bf16[1024,256]{1,0:T(8,128)(2,1)S(1)}, bf16[1024,256]{1,0:T(8,128)(2,1)}, u32[]{:S(2)}, u32[]{:S(2)}) collective-permute-start(bf16[1024,256]{1,0:T(8,128)(2,1)S(1)} %collective-permute-done.1.refs_0_), channel_id=1, source_target_pairs={{0,4},{1,5},{4,8},{5,9},{8,12},{9,13},{6,2},{7,3},{10,6},{11,7},{1... | collective-permute-start | bytes 1572872 | tf_op jit(solution)/shard_map/ppermute | solution.py:288
  54.8 10.0 %collective-permute-done.2.refs_1_ = bf16[1024,256]{1,0:T(8,128)(2,1)} collective-permute-done((bf16[1024,256]{1,0:T(8,128)(2,1)S(1)}, bf16[1024,256]{1,0:T(8,128)(2,1)}, u32[]{:S(2)}, u32[]{:S(2)}) %collective-permute-start.2) | collective-permute-done | bytes 524320 | tf_op jit(solution)/shard_map/ppermute | solution.py:288
  64.9 1.3 %collective-permute-start.4 = (bf16[1024,256]{1,0:T(8,128)(2,1)}, bf16[1024,256]{1,0:T(8,128)(2,1)}, u32[]{:S(2)}, u32[]{:S(2)}) collective-permute-start(bf16[1024,256]{1,0:T(8,128)(2,1)} %collective-permute-done.2.refs_1_), channel_id=1, source_target_pairs={{0,4},{1,5},{4,8},{5,9},{8,12},{9,13},{6,2},{7,3},{10,6},{11,7},{1... | collective-permute-start | bytes 1572872 | tf_op jit(solution)/shard_map/ppermute | solution.py:288
  66.2 9.9 %collective-permute-done.5.refs_2_.refs_0_ = bf16[1024,256]{1,0:T(8,128)(2,1)S(1)} collective-permute-done((bf16[1024,256]{1,0:T(8,128)(2,1)S(1)}, bf16[1024,256]{1,0:T(8,128)(2,1)S(1)}, u32[]{:S(2)}, u32[]{:S(2)}) %collective-permute-start.5) | collective-permute-done | bytes 524320 | tf_op jit(solution)/shard_map/ppermute | solution.py:288
  76.1 0.0 copy-start.8
  76.1 1.3 %collective-permute-start.6 = (bf16[1024,256]{1,0:T(8,128)(2,1)S(1)}, bf16[1024,256]{1,0:T(8,128)(2,1)}, u32[]{:S(2)}, u32[]{:S(2)}) collective-permute-start(bf16[1024,256]{1,0:T(8,128)(2,1)S(1)} %collective-permute-done.5.refs_2_.refs_0_), channel_id=1, source_target_pairs={{0,4},{1,5},{4,8},{5,9},{8,12},{9,13},{6,2},{7,3},{10,6},{11,7},{1... | collective-permute-start | bytes 1572872 | tf_op jit(solution)/shard_map/ppermute | solution.py:288
  77.4 0.1 add_convert_fusion.flag_ref
  77.5 4.8 %collective-permute-start.8 = (bf16[1024,256]{1,0:T(8,128)(2,1)}, bf16[1024,256]{1,0:T(8,128)(2,1)S(1)}, u32[]{:S(2)}, u32[]{:S(2)}) collective-permute-start(bf16[1024,256]{1,0:T(8,128)(2,1)} %copy-done.6), channel_id=1, source_target_pairs={{0,2},{1,3},{2,0},{3,1},{4,6},{5,7},{6,4},{7,5},{8,10},{9,11},{10,... | collective-permute-start | bytes 1572872 | tf_op jit(solution)/shard_map/ppermute | solution.py:288
  82.2 0.0 collective-permute-done.3.refs_2_.refs_3_
  82.3 0.0 collective-permute-done.4.refs_3_.refs_4_
  82.3 0.0 collective-permute-done.beside
  82.3 0.0 copy-done
  82.3 0.0 copy-done.9
  82.3 7.9 %part_flux.2 = (f32[1024,512]{1,0:T(8,128)}, f32[8,128]{1,0:T(8,128)S(1)}) custom-call(bf16[1024,5120]{1,0:T(8,128)(2,1)} %get-tuple-element.16.dense_ref, bf16[1024,1024]{1,0:T(8,128)(2,1)} %copy-done, bf16[1024,1024]{1,0:T(8,128)(2,1)} %collective-permute-done.beside, bf16[1024,256]{1,0:T(8,128)(2,1)} %copy-done.9, ...), custom_call_target="tpu_custom_call" | custom-call | tf_op jit(solution)/shard_map/part_flux/pallas_call | solution.py:355
  90.2 0.0 copy-done.8
  90.2 3.0 %collective-permute-done.6.refs_5_.refs_2_ = bf16[1024,256]{1,0:T(8,128)(2,1)} collective-permute-done((bf16[1024,256]{1,0:T(8,128)(2,1)S(1)}, bf16[1024,256]{1,0:T(8,128)(2,1)}, u32[]{:S(2)}, u32[]{:S(2)}) %collective-permute-start.6) | collective-permute-done | bytes 524320 | tf_op jit(solution)/shard_map/ppermute | solution.py:288
  93.2 1.9 %hand_over.1.refs_3_ = bf16[1024,768]{1,0:T(8,128)(2,1)S(1)} custom-call(s32[2]{0:T(128)S(1)} %add_convert_fusion.flag_ref, bf16[1024,256]{1,0:T(8,128)(2,1)} %copy-done.9, bf16[1024,256]{1,0:T(8,128)(2,1)} %collective-permute-done.2.refs_1_, bf16[1024,256]{1,0:T(8,128)(2,1)} %copy-done.8, bf16[1024,256]{1,0:T(8,128)(2,1)} %collective-permute-done.3.refs_2_.refs_3_, ...), custom_call_target="tpu_custom_call" | custom-call | tf_op jit(solution)/shard_map/hand_over/pallas_call | solution.py:373
  95.1 1.5 %collective-permute-start.7 = (bf16[1024,768]{1,0:T(8,128)(2,1)S(1)}, bf16[1024,768]{1,0:T(8,128)(2,1)S(1)}, u32[]{:S(2)}, u32[]{:S(2)}) collective-permute-start(bf16[1024,768]{1,0:T(8,128)(2,1)S(1)} %hand_over.1.refs_3_), channel_id=1, source_target_pairs={{0,1},{1,0},{2,3},{3,2},{4,5},{5,4},{6,7},{7,6},{8,9},{9,8},{10,11... | collective-permute-start | bytes 4718600 | tf_op jit(solution)/shard_map/ppermute | solution.py:288
  96.6 0.0 collective-permute-done.8.refs_1_
  96.6 0.0 copy-start.10
  96.6 1.3 %collective-permute-start.10 = (bf16[1024,256]{1,0:T(8,128)(2,1)S(1)}, bf16[1024,256]{1,0:T(8,128)(2,1)S(1)}, u32[]{:S(2)}, u32[]{:S(2)}) collective-permute-start(bf16[1024,256]{1,0:T(8,128)(2,1)S(1)} %collective-permute-done.8.refs_1_), channel_id=1, source_target_pairs={{0,4},{1,5},{4,8},{5,9},{8,12},{9,13},{6,2},{7,3},{10,6},{11,7},{1... | collective-permute-start | bytes 1572872 | tf_op jit(solution)/shard_map/ppermute | solution.py:288
  97.9 0.1 collective-permute-start.9
  98.0 0.0 copy-done.10
  98.0 8.5 %part_flux.3 = (f32[1024,512]{1,0:T(8,128)}, f32[8,128]{1,0:T(8,128)S(1)}) custom-call(bf16[1024,5120]{1,0:T(8,128)(2,1)} %get-tuple-element.16.dense_ref, bf16[1024,1024]{1,0:T(8,128)(2,1)} %copy-done, bf16[1024,1024]{1,0:T(8,128)(2,1)} %collective-permute-done.beside, bf16[1024,256]{1,0:T(8,128)(2,1)} %copy-done.8, bf16[1024,256]{1,0:T(8,128)(2,1)} %copy-done.10, ...), custom_call_target="tpu_custom_call" | custom-call | tf_op jit(solution)/shard_map/part_flux/pallas_call | solution.py:355
  106.6 5.4 %collective-permute-done.10.refs_0_ = bf16[1024,256]{1,0:T(8,128)(2,1)S(1)} collective-permute-done((bf16[1024,256]{1,0:T(8,128)(2,1)S(1)}, bf16[1024,256]{1,0:T(8,128)(2,1)S(1)}, u32[]{:S(2)}, u32[]{:S(2)}) %collective-permute-start.10) | collective-permute-done | bytes 524320 | tf_op jit(solution)/shard_map/ppermute | solution.py:288
  112.0 0.8 collective-permute-start.11
  112.8 0.0 collective-permute-done.9.refs_7_
  112.8 1.5 %collective-permute-done.11.refs_8_ = bf16[1024,256]{1,0:T(8,128)(2,1)S(1)} collective-permute-done((bf16[1024,256]{1,0:T(8,128)(2,1)S(1)}, bf16[1024,256]{1,0:T(8,128)(2,1)S(1)}, u32[]{:S(2)}, u32[]{:S(2)}) %collective-permute-start.11) | collective-permute-done | bytes 524320 | tf_op jit(solution)/shard_map/ppermute | solution.py:288
  114.4 0.0 collective-permute-done.7.refs_1_.refs_3_.refs_5_
  114.4 0.0 copy-start.7
  114.4 1.1 copy-done.7
  115.5 9.3 %last_flux.1 = bf16[1024,1024]{1,0:T(8,128)(2,1)} custom-call(s32[2]{0:T(128)S(1)} %add_convert_fusion.flag_ref, bf16[1024,5120]{1,0:T(8,128)(2,1)} %get-tuple-element.16.dense_ref, f32[1024,512]{1,0:T(8,128)} %get-tuple-element.21.refs_0_.refs_2_, bf16[1024,768]{1,0:T(8,128)(2,1)} %copy-done.7, f32[1024,512]{1,0:T(8,128)} %get-tuple-element.21.refs_0_.refs_2_, ...), custom_call_target="tpu_custom_call" | custom-call | tf_op jit(solution)/shard_map/last_flux/pallas_call | solution.py:402
  (1 shorter events, 0.0 us)
Async XLA Ops:
  0.0 10.9 %copy-start.3 = (s32[4,20]{1,0:T(4,128)S(1)}, s32[4,20]{1,0:T(4,128)}, u32[]{:S(2)}) copy-start(s32[4,20]{1,0:T(4,128)} %cols_ref.1) | copy-start | bytes 964
  0.0 1.1 copy-start.2
  1.1 0.7 copy-start.4
  1.7 0.7 copy-start.5
  4.1 32.6 %all-to-all-start = ((bf16[16,32,1152]{2,1,0:T(8,128)(2,1)}), bf16[16,32,1152]{2,1,0:T(8,128)(2,1)S(1)}, u32[]{:S(2)}, u32[]{:S(2)}) async-start(bf16[16,32,1152]{2,1,0:T(8,128)(2,1)} %bitcast.9), calls=%async_computation | async-start | bytes 2359296 | tf_op jit(solution)/shard_map/all_to_all | solution.py:312
  36.8 1.6 %copy-start.1 = (bf16[1024,1024]{1,0:T(8,128)(2,1)S(1)}, bf16[1024,1024]{1,0:T(8,128)(2,1)}, u32[]{:S(2)}) copy-start(bf16[1024,1024]{1,0:T(8,128)(2,1)} %base_ref.1) | copy-start | bytes 6291460
  39.7 0.8 copy-start.6
  40.5 41.7 %copy-start = (bf16[1024,1024]{1,0:T(8,128)(2,1)}, bf16[1024,1024]{1,0:T(8,128)(2,1)S(1)}, u32[]{:S(2)}) copy-start(bf16[1024,1024]{1,0:T(8,128)(2,1)S(1)} %get-tuple-element.18.own) | copy-start | bytes 6291460
  40.5 41.7 %collective-permute-start = (bf16[1024,1024]{1,0:T(8,128)(2,1)S(1)}, bf16[1024,1024]{1,0:T(8,128)(2,1)}, u32[]{:S(2)}, u32[]{:S(2)}) collective-permute-start(bf16[1024,1024]{1,0:T(8,128)(2,1)S(1)} %get-tuple-element.18.own), channel_id=1, source_target_pairs={{0,1},{1,0},{2,3},{3,2},{4,5},{5,4},{6,7},{7,6},{8,9},{9,8},{10,11... | collective-permute-start | bytes 6291464 | tf_op jit(solution)/shard_map/ppermute | solution.py:288
  40.6 13.0 %collective-permute-start.1 = (bf16[1024,256]{1,0:T(8,128)(2,1)S(1)}, bf16[1024,256]{1,0:T(8,128)(2,1)S(1)}, u32[]{:S(2)}, u32[]{:S(2)}) collective-permute-start(bf16[1024,256]{1,0:T(8,128)(2,1)S(1)} %get-tuple-element.19), channel_id=1, source_target_pairs={{0,2},{1,3},{2,0},{3,1},{4,6},{5,7},{6,4},{7,5},{8,10},{9,11},{10,... | collective-permute-start | bytes 1572872 | tf_op jit(solution)/shard_map/ppermute | solution.py:288
  40.6 24.3 %collective-permute-start.2 = (bf16[1024,256]{1,0:T(8,128)(2,1)S(1)}, bf16[1024,256]{1,0:T(8,128)(2,1)}, u32[]{:S(2)}, u32[]{:S(2)}) collective-permute-start(bf16[1024,256]{1,0:T(8,128)(2,1)S(1)} %get-tuple-element.20), channel_id=1, source_target_pairs={{0,2},{1,3},{2,0},{3,1},{4,6},{5,7},{6,4},{7,5},{8,10},{9,11},{10,... | collective-permute-start | bytes 1572872 | tf_op jit(solution)/shard_map/ppermute | solution.py:288
  42.0 34.1 %collective-permute-start.5 = (bf16[1024,256]{1,0:T(8,128)(2,1)S(1)}, bf16[1024,256]{1,0:T(8,128)(2,1)S(1)}, u32[]{:S(2)}, u32[]{:S(2)}) collective-permute-start(bf16[1024,256]{1,0:T(8,128)(2,1)S(1)} %get-tuple-element.22), channel_id=1, source_target_pairs={{0,2},{1,3},{2,0},{3,1},{4,6},{5,7},{6,4},{7,5},{8,10},{9,11},{10,... | collective-permute-start | bytes 1572872 | tf_op jit(solution)/shard_map/ppermute | solution.py:288
  53.5 28.7 %copy-start.9 = (bf16[1024,256]{1,0:T(8,128)(2,1)}, bf16[1024,256]{1,0:T(8,128)(2,1)S(1)}, u32[]{:S(2)}) copy-start(bf16[1024,256]{1,0:T(8,128)(2,1)S(1)} %collective-permute-done.1.refs_0_) | copy-start | bytes 1572868
  53.5 28.7 %collective-permute-start.3 = (bf16[1024,256]{1,0:T(8,128)(2,1)S(1)}, bf16[1024,256]{1,0:T(8,128)(2,1)}, u32[]{:S(2)}, u32[]{:S(2)}) collective-permute-start(bf16[1024,256]{1,0:T(8,128)(2,1)S(1)} %collective-permute-done.1.refs_0_), channel_id=1, source_target_pairs={{0,4},{1,5},{4,8},{5,9},{8,12},{9,13},{6,2},{7,3},{10,6},{11,7},{1... | collective-permute-start | bytes 1572872 | tf_op jit(solution)/shard_map/ppermute | solution.py:288
  64.9 17.4 %collective-permute-start.4 = (bf16[1024,256]{1,0:T(8,128)(2,1)}, bf16[1024,256]{1,0:T(8,128)(2,1)}, u32[]{:S(2)}, u32[]{:S(2)}) collective-permute-start(bf16[1024,256]{1,0:T(8,128)(2,1)} %collective-permute-done.2.refs_1_), channel_id=1, source_target_pairs={{0,4},{1,5},{4,8},{5,9},{8,12},{9,13},{6,2},{7,3},{10,6},{11,7},{1... | collective-permute-start | bytes 1572872 | tf_op jit(solution)/shard_map/ppermute | solution.py:288
  76.1 14.1 %copy-start.8 = (bf16[1024,256]{1,0:T(8,128)(2,1)}, bf16[1024,256]{1,0:T(8,128)(2,1)S(1)}, u32[]{:S(2)}) copy-start(bf16[1024,256]{1,0:T(8,128)(2,1)S(1)} %collective-permute-done.5.refs_2_.refs_0_) | copy-start | bytes 1572868
  76.1 17.1 %collective-permute-start.6 = (bf16[1024,256]{1,0:T(8,128)(2,1)S(1)}, bf16[1024,256]{1,0:T(8,128)(2,1)}, u32[]{:S(2)}, u32[]{:S(2)}) collective-permute-start(bf16[1024,256]{1,0:T(8,128)(2,1)S(1)} %collective-permute-done.5.refs_2_.refs_0_), channel_id=1, source_target_pairs={{0,4},{1,5},{4,8},{5,9},{8,12},{9,13},{6,2},{7,3},{10,6},{11,7},{1... | collective-permute-start | bytes 1572872 | tf_op jit(solution)/shard_map/ppermute | solution.py:288
  77.5 19.1 %collective-permute-start.8 = (bf16[1024,256]{1,0:T(8,128)(2,1)}, bf16[1024,256]{1,0:T(8,128)(2,1)S(1)}, u32[]{:S(2)}, u32[]{:S(2)}) collective-permute-start(bf16[1024,256]{1,0:T(8,128)(2,1)} %copy-done.6), channel_id=1, source_target_pairs={{0,2},{1,3},{2,0},{3,1},{4,6},{5,7},{6,4},{7,5},{8,10},{9,11},{10,... | collective-permute-start | bytes 1572872 | tf_op jit(solution)/shard_map/ppermute | solution.py:288
  95.1 19.2 %collective-permute-start.7 = (bf16[1024,768]{1,0:T(8,128)(2,1)S(1)}, bf16[1024,768]{1,0:T(8,128)(2,1)S(1)}, u32[]{:S(2)}, u32[]{:S(2)}) collective-permute-start(bf16[1024,768]{1,0:T(8,128)(2,1)S(1)} %hand_over.1.refs_3_), channel_id=1, source_target_pairs={{0,1},{1,0},{2,3},{3,2},{4,5},{5,4},{6,7},{7,6},{8,9},{9,8},{10,11... | collective-permute-start | bytes 4718600 | tf_op jit(solution)/shard_map/ppermute | solution.py:288
  96.6 1.4 %copy-start.10 = (bf16[1024,256]{1,0:T(8,128)(2,1)}, bf16[1024,256]{1,0:T(8,128)(2,1)S(1)}, u32[]{:S(2)}) copy-start(bf16[1024,256]{1,0:T(8,128)(2,1)S(1)} %collective-permute-done.8.refs_1_) | copy-start | bytes 1572868
  96.6 15.4 %collective-permute-start.10 = (bf16[1024,256]{1,0:T(8,128)(2,1)S(1)}, bf16[1024,256]{1,0:T(8,128)(2,1)S(1)}, u32[]{:S(2)}, u32[]{:S(2)}) collective-permute-start(bf16[1024,256]{1,0:T(8,128)(2,1)S(1)} %collective-permute-done.8.refs_1_), channel_id=1, source_target_pairs={{0,4},{1,5},{4,8},{5,9},{8,12},{9,13},{6,2},{7,3},{10,6},{11,7},{1... | collective-permute-start | bytes 1572872 | tf_op jit(solution)/shard_map/ppermute | solution.py:288
  97.9 14.9 %collective-permute-start.9 = (bf16[1024,256]{1,0:T(8,128)(2,1)S(1)}, bf16[1024,256]{1,0:T(8,128)(2,1)S(1)}, u32[]{:S(2)}, u32[]{:S(2)}) collective-permute-start(bf16[1024,256]{1,0:T(8,128)(2,1)S(1)} %collective-permute-done.8.refs_1_), channel_id=1, source_target_pairs={{0,1},{1,0},{2,3},{3,2},{4,5},{5,4},{6,7},{7,6},{8,9},{9,8},{10,11... | collective-permute-start | bytes 1572872 | tf_op jit(solution)/shard_map/ppermute | solution.py:288
  112.0 2.4 %collective-permute-start.11 = (bf16[1024,256]{1,0:T(8,128)(2,1)S(1)}, bf16[1024,256]{1,0:T(8,128)(2,1)S(1)}, u32[]{:S(2)}, u32[]{:S(2)}) collective-permute-start(bf16[1024,256]{1,0:T(8,128)(2,1)S(1)} %gate.1.refs_9_), channel_id=1, source_target_pairs={{0,1},{1,0},{2,3},{3,2},{4,5},{5,4},{6,7},{7,6},{8,9},{9,8},{10,11... | collective-permute-start | bytes 1572872 | tf_op jit(solution)/shard_map/ppermute | solution.py:288
  114.4 1.1 copy-start.7

commit v3 on v1

v3 whole, which is shorter than its diff:
```python
import functools

import jax
import jax.numpy as jnp
from jax import lax
from jax.experimental import pallas as pl
from jax.experimental.pallas import tpu as pltpu
from jax.sharding import PartitionSpec as P

HALO = 2
PIECES = 1
AHEAD = 3
LANES = 128
RADIX = 32
VMEM = pl.BlockSpec(memory_space=pltpu.VMEM)
SMEM = pl.BlockSpec(memory_space=pltpu.SMEM)
HBM = pl.BlockSpec(memory_space=pltpu.HBM)
ANY = pl.BlockSpec(memory_space=pl.ANY)
SLOTS = 2 * HALO + 1
TOKEN = jax.ShapeDtypeStruct((8, LANES), jnp.float32)
WAIT = ('y3', 'z2')
GATE = True
MIB = 1024 * 1024


def limit(mib):
    return pltpu.CompilerParams(vmem_limit_bytes=mib * MIB)


def in_hbm(value):
    return pltpu.with_memory_space_constraint(value, pltpu.HBM)


def gate_kernel(*refs):
    pass


def gate(value, *others):
    return pl.pallas_call(
        gate_kernel,
        out_shape=jax.ShapeDtypeStruct(value.shape, value.dtype),
        in_specs=[ANY] * (1 + len(others)),
        out_specs=ANY,
        input_output_aliases={0: 0},
        compiler_params=limit(1),
        name="gate",
    )(value, *others)


def chunk_sizes(width):
    unit = width // 8
    return [2 * unit] * 4


def pack_kernel(capacity, owner_hbm, target_hbm, rows_hbm, out_ref, owner_ref, target_ref, rows_ref, sems):
    copies = [
        pltpu.make_async_copy(source, target, sems.at[i])
        for i, (source, target) in enumerate(
            [(owner_hbm, owner_ref), (target_hbm, target_ref), (rows_hbm, rows_ref)]
        )
    ]
    for copy in copies:
        copy.start()
    count, width = rows_ref.shape
    slots = out_ref.shape[0]
    tri = lax.broadcasted_iota(jnp.int32, (count, count), 0) < lax.broadcasted_iota(
        jnp.int32, (count, count), 1
    )
    line = lax.broadcasted_iota(jnp.int32, (LANES, count), 0)
    copies[0].wait()
    copies[1].wait()
    owner = owner_ref[...]
    target = target_ref[...]
    named = line == owner
    earlier = jnp.dot(
        named.astype(jnp.bfloat16), tri.astype(jnp.bfloat16), preferred_element_type=jnp.float32
    )
    order = jnp.sum(jnp.where(named, earlier, 0.0), axis=0, keepdims=True).astype(jnp.int32)
    position = owner * capacity + order
    picker = (lax.broadcasted_iota(jnp.int32, (slots, count), 0) == position).astype(jnp.bfloat16)
    tags = jnp.where(line == 0, target // RADIX + 1, jnp.where(line == 1, target % RADIX, 0))
    tags = tags.astype(jnp.float32).astype(jnp.bfloat16)
    out_ref[:, width:] = lax.dot_general(
        picker, tags, (((1,), (1,)), ((), ())), preferred_element_type=jnp.float32
    ).astype(jnp.bfloat16)
    copies[2].wait()
    out_ref[:, :width] = jnp.dot(
        picker, rows_ref[...], preferred_element_type=jnp.float32
    ).astype(jnp.bfloat16)


def inject_kernel(base_ref, arrived_ref, wait_ref, whole_ref, *out_refs):
    offset = 0
    seg_dev = base_ref.shape[0]
    slots = arrived_ref.shape[0]
    width = arrived_ref.shape[1] - LANES
    pick_lane = lax.broadcasted_iota(jnp.int32, (8, LANES), 1)
    weights = jnp.where(pick_lane == 0, float(RADIX), jnp.where(pick_lane == 1, 1.0, 0.0))
    segment = lax.dot_general(
        weights.astype(jnp.bfloat16),
        arrived_ref[:, width:],
        (((1,), (1,)), ((), ())),
        preferred_element_type=jnp.float32,
    )[0:1].astype(jnp.int32) - RADIX
    landing = (lax.broadcasted_iota(jnp.int32, (seg_dev, slots), 0) == segment).astype(jnp.bfloat16)
    for out_ref in out_refs:
        there = slice(offset, offset + out_ref.shape[1])
        injected = jnp.dot(landing, arrived_ref[:, there], preferred_element_type=jnp.float32)
        current = (base_ref[:, there].astype(jnp.float32) + injected).astype(jnp.bfloat16)
        out_ref[...] = current
        whole_ref[:, there] = current
        offset += out_ref.shape[1]


def dense_kernel(cols_ref, slot_ref, blocks_ref, wait_ref, out_ref, token_ref, total_ref):
    row = pl.program_id(0)
    count = blocks_ref.shape[1]
    block = blocks_ref.shape[2]
    per_dev = cols_ref.shape[0]
    places = total_ref.shape[0]
    total_ref[...] = jnp.zeros_like(total_ref)
    token_ref[...] = jnp.zeros_like(token_ref)

    def add(k, carry):
        local = cols_ref[row, k] - slot_ref[SLOTS]
        at = slot_ref[local // per_dev] * per_dev + local % per_dev
        total_ref[at] = total_ref[at] + blocks_ref[0, k].astype(jnp.float32)
        return carry

    lax.fori_loop(0, count, add, 0)
    for at in range(places):
        out_ref[:, at * block : (at + 1) * block] = total_ref[at].astype(jnp.bfloat16)


def hand_kernel(count, flag_ref, *refs):
    peers, passed = refs[:count], refs[count : 2 * count]
    out_refs, sems = refs[-1 - count * PIECES : -1], refs[-1]

    def copies(sources):
        made = []
        for i, out_ref in enumerate(out_refs):
            size = out_ref.shape[1]
            source = sources[i // PIECES].at[:, pl.ds(i % PIECES * size, size)]
            made.append(pltpu.make_async_copy(source, out_ref, sems.at[i]))
        return made

    @pl.when(flag_ref[1] == 0)
    def _():
        for copy in copies(peers):
            copy.start()

    @pl.when(flag_ref[1] == 1)
    def _():
        for copy in copies(passed):
            copy.start()

    for copy in copies(peers):
        copy.wait()


class Slots:
    def __init__(self, flag, dense_ref, slots, matrix, window, mat_sems, sems):
        self.flag, self.dense, self.slots = flag, dense_ref, slots
        self.matrix, self.window, self.mat_sems, self.sems = matrix, window, mat_sems, sems

    def columns(self, slot):
        depth = self.dense.shape[0]
        there = self.dense.at[:, pl.ds(slot * depth, depth)]
        return pltpu.make_async_copy(there, self.matrix.at[slot], self.mat_sems.at[slot])

    def rows(self, slot, i, piece):
        size = piece.shape[1]
        target = self.window.at[slot, :, pl.ds(i * size, size)]
        return pltpu.make_async_copy(piece, target, self.sems.at[slot, i])

    def begin(self, slot):
        self.columns(slot).start()
        for i, piece in enumerate(self.slots[slot]):
            if not isinstance(piece, tuple):
                self.rows(slot, i, piece).start()
                continue
            for value in range(2):
                @pl.when(self.flag == value)
                def _(value=value):
                    self.rows(slot, i, piece[value]).start()

    def sum_into(self, total_ref):
        for slot in range(AHEAD):
            self.begin(slot)
        last = len(self.slots) - 1
        for slot, pieces in enumerate(self.slots):
            self.columns(slot).wait()
            for i, piece in enumerate(pieces):
                self.rows(slot, i, piece[0] if isinstance(piece, tuple) else piece).wait()
            if slot + AHEAD <= last:
                self.begin(slot + AHEAD)
            part = jnp.dot(self.matrix[slot], self.window[slot], preferred_element_type=jnp.float32)
            if slot == 0:
                total_ref[...] = part
            elif slot < last:
                total_ref[...] += part
        return total_ref[...] + part


def flux_kernel(offset, count, paired, flag_ref, dense_ref, own, beside, *refs):
    out_ref, token_ref, matrix, window, total, result, mat_sems, sems, out_sem = refs[-9:]
    token_ref[...] = jnp.zeros_like(token_ref)
    there = pl.ds(offset, total.shape[1])
    peers, passed = refs[:count], refs[count : 2 * count]
    slots = [[own.at[:, there]], [beside.at[:, there]], peers, passed]
    if paired:
        slots.append(list(zip(refs[2 * count : 3 * count], refs[3 * count : 4 * count])))
    else:
        slots.append(refs[2 * count : 2 * count + count * PIECES])
    parts = Slots(flag_ref[0], dense_ref, slots, matrix, window, mat_sems, sems).sum_into(total)
    result[...] = parts.astype(jnp.bfloat16)
    out = pltpu.make_async_copy(result, out_ref.at[:, there], out_sem)
    out.start()
    out.wait()


def shards(base_currents, term_rows, term_owner, term_slot, inductance, block_cols):
    devices = lax.axis_size("row")
    me = lax.axis_index("row")
    seg_dev, width = base_currents.shape
    capacity = max(2, 2 * term_rows.shape[0] // devices)
    slots = devices * capacity
    rows_dev, count, block, _ = inductance.shape

    core, side = me % 2, (me // 2) % 2
    across = [(i, i ^ 2) for i in range(devices)]
    partner = [(i, i ^ 1) for i in range(devices)]
    relay = [(i, i + 4) for i in range(devices - 4) if not i & 2]
    relay += [(i + 4, i) for i in range(devices - 4) if i & 2]

    def send(value, pairs):
        return lax.ppermute(value, "row", pairs)

    near = jnp.where(core == 0, 4, 1)
    far = jnp.where(core == 0, 1, 4)
    slot_of = jnp.stack(
        [
            jnp.where(side == 0, 3, 2),
            near,
            jnp.zeros_like(near),
            far,
            jnp.where(side == 0, 2, 3),
            (me - HALO) * rows_dev,
        ]
    ).astype(jnp.int32)
    flag = jnp.stack([core == side, core != side]).astype(jnp.int32)

    outgoing = pl.pallas_call(
        functools.partial(pack_kernel, capacity),
        out_shape=jax.ShapeDtypeStruct((slots, width + LANES), jnp.bfloat16),
        in_specs=[HBM] * 3,
        out_specs=VMEM,
        scratch_shapes=[
            pltpu.VMEM((1, term_rows.shape[0]), jnp.int32),
            pltpu.VMEM((1, term_rows.shape[0]), jnp.int32),
            pltpu.VMEM(term_rows.shape, jnp.bfloat16),
            pltpu.SemaphoreType.DMA((3,)),
        ],
        compiler_params=limit(16),
        name="pack_terms",
    )(*[in_hbm(item) for item in (term_owner.reshape(1, -1), term_slot.reshape(1, -1), term_rows)])
    arrived = lax.all_to_all(
        outgoing.reshape(devices, capacity, width + LANES), "row", split_axis=0, concat_axis=0, tiled=True
    ).reshape(slots, width + LANES)

    dense, dense_token = pl.pallas_call(
        dense_kernel,
        out_shape=(pltpu.HBM((seg_dev, SLOTS * seg_dev), jnp.bfloat16), TOKEN),
        grid=(rows_dev,),
        in_specs=[SMEM, SMEM, pl.BlockSpec((1, count, block, block), lambda r: (r, 0, 0, 0)), HBM],
        out_specs=(pl.BlockSpec((block, SLOTS * seg_dev), lambda r: (r, 0)), pl.BlockSpec(TOKEN.shape, lambda r: (0, 0))),
        scratch_shapes=[pltpu.VMEM((SLOTS * rows_dev, block, block), jnp.float32)],
        compiler_params=limit(24),
        cost_estimate=pl.CostEstimate(flops=0, bytes_accessed=0, transcendentals=0),
        name="dense_blocks",
    )(block_cols, slot_of, in_hbm(inductance), in_hbm(outgoing))


    sizes = chunk_sizes(width)
    starts = [sum(sizes[:k]) for k in range(len(sizes))]
    whole, *currents = pl.pallas_call(
        inject_kernel,
        out_shape=[
            jax.ShapeDtypeStruct((seg_dev, wide), jnp.bfloat16) for wide in [width] + sizes
        ],
        in_specs=[VMEM, VMEM, ANY],
        out_specs=[VMEM] * (1 + len(sizes)),
        compiler_params=limit(24),
        name="inject_terms",
    )(base_currents, arrived, dense_token)

    def cost():
        return pl.CostEstimate(flops=0, bytes_accessed=0, transcendentals=0)

    beside = send(whole, partner)
    peers = [send(current, across) for current in currents]

    passed = [send(peer, relay) for peer in peers]

    size = sizes[0]
    half = len(sizes) // 2
    out_type = pltpu.HBM((seg_dev, width), jnp.bfloat16)

    def flux(start, chunks, others, paired, out, after=()):
        given = [dense, whole, beside] + peers[chunks] + passed[chunks] + others + out
        return pl.pallas_call(
            functools.partial(flux_kernel, start, half, paired),
            out_shape=(out_type, TOKEN),
            in_specs=[SMEM]
            + [ANY if start and any(item is other for other in others) else HBM for item in given]
            + [HBM] * len(after),
            out_specs=(HBM, VMEM),
            scratch_shapes=[
                pltpu.VMEM((SLOTS, seg_dev, seg_dev), jnp.bfloat16),
                pltpu.VMEM((SLOTS, seg_dev, half * size), jnp.bfloat16),
                pltpu.VMEM((seg_dev, half * size), jnp.float32),
                pltpu.VMEM((seg_dev, half * size), jnp.bfloat16),
                pltpu.SemaphoreType.DMA((SLOTS,)),
                pltpu.SemaphoreType.DMA((SLOTS, half * PIECES)),
                pltpu.SemaphoreType.DMA,
            ],
            input_output_aliases={len(given): 0} if out else {},
            compiler_params=limit(36),
            cost_estimate=cost(),
            name="flux",
        )(flag, *[in_hbm(item) if start == 0 or not any(item is other for other in others) else item for item in (*given, *after)])

    across_beside = [send(peer, partner) for peer in peers]
    passed_beside = [send(item, partner) for item in passed[:3]]
    others = across_beside[:half] + passed_beside[:half]
    out, token = flux(0, slice(0, half), others, True, [], [passed_beside[2]])
    passed[3] = gate(passed[3], token)
    passed_beside.append(send(passed[3], partner))
    others = across_beside[half:] + passed_beside[half:]
    out, _ = flux(half * size, slice(half, 2 * half), others, True, [out])
    return out


def solution(mesh):
    placed = (
        P(("group", "row"), None),
        P(("group", "row"), None),
        P(("group", "row"), None),
        P(("group", "row"), None),
        P("row", None, None, None),
        P("row", None),
    )
    return jax.shard_map(
        shards, mesh=mesh, in_specs=placed, out_specs=P(("group", "row"), None), check_vma=False
    )
```

time: 131 us -> 124 us (0.947)
  Pallas kernels: 41.2 us -> 34.3 us
  waiting for transfers between devices: 60 us -> 62.8 us
  local copies, waits for them, and re-layouts: 7.4 us -> 5.02 us
    pallas_call x6 -> x4, Pallas kernels: 28.2 us -> 20.7 us  [the longest x2 19.3 us: flux(): pl.pallas_call(functools.partial(flux_kernel, start, half, paired), out_s...]
    ppermute x15 -> x17, waiting for transfers between devices: 45.3 us -> 48 us  [send(): return lax.ppermute(value, 'row', pairs)]
    unnamed x36 -> x22, local copies, waits for them, and re-layouts: 7.32 us -> 4.94 us
    ppermute x15 -> x17, starting transfers between devices: 14.2 us -> 13.7 us  [send(): return lax.ppermute(value, 'row', pairs)]
  transfers between devices with their start and end apart: 16 -> 18, of which waited for: 7 -> 8; matrix products, arithmetic and copies ran while one was open for 0% -> 0% of each run, Pallas kernels for 21% -> 17%
where the time goes in v3:
time: 124 us; the launch traced here: 123 us
  waiting for transfers between devices  62.8 us (51%)
  Pallas kernels  34.3 us (28%)
  starting transfers between devices  20.4 us (16%)
  local copies, waits for them, and re-layouts  5.02 us (4%)
    ppermute x17, waiting for transfers between devices, send(): return lax.ppermute(value, 'row', pairs)  48 us
    pallas_call x2, Pallas kernels, flux(): pl.pallas_call(functools.partial(flux_kernel, start, half, paired), out_s...  19.3 us
    all_to_all x1, waiting for transfers between devices, shards(): lax.all_to_all(outgoing.reshape(devices, capacity, width + LANES), 'row',...  14.9 us
    ppermute x17, starting transfers between devices, send(): return lax.ppermute(value, 'row', pairs)  13.7 us
    pallas_call x1, Pallas kernels, shards(): pl.pallas_call(dense_kernel, out_shape=(pltpu.HBM((seg_dev, SLOTS * seg_d...  11 us
    all_to_all x1, starting transfers between devices, shards(): lax.all_to_all(outgoing.reshape(devices, capacity, width + LANES), 'row',...  6.68 us
    unnamed x22, local copies, waits for them, and re-layouts  4.94 us
    pallas_call x1, Pallas kernels, shards(): pl.pallas_call(functools.partial(pack_kernel, capacity), out_shape=jax.Sh...  2.61 us
  transfers between devices with their start and end apart: 18, of which 8 were waited for; matrix products, arithmetic and copies ran while one was open for 0% of the time, Pallas kernels for 17%

profile of v3, /device:TPU:7, one launch (start us, length us, event | category | flops | bytes accessed | tf_op | source)
XLA Modules:
  0.0 122.8 jit_solution(2630526574276077526)
XLA Ops:
  0.0 0.0 copy-start.5
  0.0 2.6 %pack_terms.1.wait_ref = bf16[512,1152]{1,0:T(8,128)(2,1)} custom-call(s32[1,256]{1,0:T(1,128)} %bitcast.12, s32[1,256]{1,0:T(1,128)} %bitcast.13, bf16[256,1024]{1,0:T(8,128)(2,1)} %rows_hbm.1), custom_call_target="tpu_custom_call" | custom-call | tf_op jit(solution)/shard_map/pack_terms/pallas_call | solution.py:253
  2.6 6.7 %all-to-all-start = ((bf16[16,32,1152]{2,1,0:T(8,128)(2,1)}), bf16[16,32,1152]{2,1,0:T(8,128)(2,1)S(1)}, u32[]{:S(2)}, u32[]{:S(2)}) async-start(bf16[16,32,1152]{2,1,0:T(8,128)(2,1)} %bitcast.9), calls=%async_computation | async-start | bytes 2359296 | tf_op jit(solution)/shard_map/all_to_all | solution.py:267
  9.3 0.1 stack.35.slot_ref
  9.4 0.0 copy-done.5
  9.4 11.0 %dense_blocks.1 = (bf16[1024,5120]{1,0:T(8,128)(2,1)}, f32[8,128]{1,0:T(8,128)S(1)}) custom-call(s32[4,20]{1,0:T(4,128)S(1)} %copy-done.5, s32[6]{0:T(128)S(1)} %stack.35.slot_ref, bf16[4,20,256,256]{3,2,1,0:T(8,128)(2,1)} %blocks_ref.1, bf16[512,1152]{1,0:T(8,128)(2,1)} %pack_terms.1.wait_ref), custom_call_target="tpu_custom_call" | custom-call | tf_op jit(solution)/shard_map/dense_blocks/pallas_call | solution.py:271
  20.4 14.9 %all-to-all-done = bf16[16,32,1152]{2,1,0:T(8,128)(2,1)S(1)} async-done(((bf16[16,32,1152]{2,1,0:T(8,128)(2,1)}), bf16[16,32,1152]{2,1,0:T(8,128)(2,1)S(1)}, u32[]{:S(2)}, u32[]{:S(2)}) %all-to-all-start) | async-done | bytes 1179680 | tf_op jit(solution)/shard_map/all_to_all | solution.py:267
  35.3 0.0 copy-start.3
  35.3 1.6 %copy-done.3 = bf16[1024,1024]{1,0:T(8,128)(2,1)S(1)} copy-done((bf16[1024,1024]{1,0:T(8,128)(2,1)S(1)}, bf16[1024,1024]{1,0:T(8,128)(2,1)}, u32[]{:S(2)}) %copy-start.3) | copy-done | bytes 2097176
  36.9 1.4 %inject_terms.1 = (bf16[1024,1024]{1,0:T(8,128)(2,1)S(1)}, bf16[1024,256]{1,0:T(8,128)(2,1)S(1)}, bf16[1024,256]{1,0:T(8,128)(2,1)S(1)}, bf16[1024,256]{1,0:T(8,128)(2,1)S(1)}, bf16[1024,256]{1,0:T(8,128)(2,1)S(1)}) custom-call(bf16[1024,1024]{1,0:T(8,128)(2,1)S(1)} %copy-done.3, bf16[512,1152]{1,0:T(8,128)(2,1)S(1)} %bitcast.11, ...), custom_call_target="tpu_custom_call" | custom-call | tf_op jit(solution)/shard_map/inject_terms/pallas_call | solution.py:286
  38.2 0.0 copy-start
  38.3 0.1 collective-permute-start
  38.3 0.1 collective-permute-start.5
  38.4 1.5 %collective-permute-start.6 = (bf16[1024,256]{1,0:T(8,128)(2,1)S(1)}, bf16[1024,256]{1,0:T(8,128)(2,1)S(1)}, u32[]{:S(2)}, u32[]{:S(2)}) collective-permute-start(bf16[1024,256]{1,0:T(8,128)(2,1)S(1)} %get-tuple-element.21), channel_id=1, source_target_pairs={{0,2},{1,3},{2,0},{3,1},{4,6},{5,7},{6,4},{7,5},{8,10},{9,11},{10,... | collective-permute-start | bytes 1572872 | tf_op jit(solution)/shard_map/ppermute | solution.py:237
  39.9 0.1 collective-permute-start.1
  39.9 1.4 %collective-permute-start.2 = (bf16[1024,256]{1,0:T(8,128)(2,1)S(1)}, bf16[1024,256]{1,0:T(8,128)(2,1)}, u32[]{:S(2)}, u32[]{:S(2)}) collective-permute-start(bf16[1024,256]{1,0:T(8,128)(2,1)S(1)} %get-tuple-element.19), channel_id=1, source_target_pairs={{0,2},{1,3},{2,0},{3,1},{4,6},{5,7},{6,4},{7,5},{8,10},{9,11},{10,... | collective-permute-start | bytes 1572872 | tf_op jit(solution)/shard_map/ppermute | solution.py:237
  41.3 10.1 %collective-permute-done.5.refs_0_ = bf16[1024,256]{1,0:T(8,128)(2,1)S(1)} collective-permute-done((bf16[1024,256]{1,0:T(8,128)(2,1)S(1)}, bf16[1024,256]{1,0:T(8,128)(2,1)S(1)}, u32[]{:S(2)}, u32[]{:S(2)}) %collective-permute-start.5) | collective-permute-done | bytes 524320 | tf_op jit(solution)/shard_map/ppermute | solution.py:237
  51.5 0.0 copy-start.7
  51.5 1.3 %collective-permute-start.7 = (bf16[1024,256]{1,0:T(8,128)(2,1)S(1)}, bf16[1024,256]{1,0:T(8,128)(2,1)}, u32[]{:S(2)}, u32[]{:S(2)}) collective-permute-start(bf16[1024,256]{1,0:T(8,128)(2,1)S(1)} %collective-permute-done.5.refs_0_), channel_id=1, source_target_pairs={{0,4},{1,5},{4,8},{5,9},{8,12},{9,13},{6,2},{7,3},{10,6},{11,7},{1... | collective-permute-start | bytes 1572872 | tf_op jit(solution)/shard_map/ppermute | solution.py:237
  52.8 10.0 %collective-permute-done.6.refs_1_ = bf16[1024,256]{1,0:T(8,128)(2,1)S(1)} collective-permute-done((bf16[1024,256]{1,0:T(8,128)(2,1)S(1)}, bf16[1024,256]{1,0:T(8,128)(2,1)S(1)}, u32[]{:S(2)}, u32[]{:S(2)}) %collective-permute-start.6) | collective-permute-done | bytes 524320 | tf_op jit(solution)/shard_map/ppermute | solution.py:237
  62.8 0.0 copy-start.8
  62.8 1.3 %collective-permute-start.8 = (bf16[1024,256]{1,0:T(8,128)(2,1)S(1)}, bf16[1024,256]{1,0:T(8,128)(2,1)}, u32[]{:S(2)}, u32[]{:S(2)}) collective-permute-start(bf16[1024,256]{1,0:T(8,128)(2,1)S(1)} %collective-permute-done.6.refs_1_), channel_id=1, source_target_pairs={{0,4},{1,5},{4,8},{5,9},{8,12},{9,13},{6,2},{7,3},{10,6},{11,7},{1... | collective-permute-start | bytes 1572872 | tf_op jit(solution)/shard_map/ppermute | solution.py:237
  64.1 9.9 %collective-permute-done.1.refs_0_ = bf16[1024,256]{1,0:T(8,128)(2,1)S(1)} collective-permute-done((bf16[1024,256]{1,0:T(8,128)(2,1)S(1)}, bf16[1024,256]{1,0:T(8,128)(2,1)S(1)}, u32[]{:S(2)}, u32[]{:S(2)}) %collective-permute-start.1) | collective-permute-done | bytes 524320 | tf_op jit(solution)/shard_map/ppermute | solution.py:237
  74.0 0.0 copy-start.6
  74.0 1.3 %collective-permute-start.3 = (bf16[1024,256]{1,0:T(8,128)(2,1)S(1)}, bf16[1024,256]{1,0:T(8,128)(2,1)}, u32[]{:S(2)}, u32[]{:S(2)}) collective-permute-start(bf16[1024,256]{1,0:T(8,128)(2,1)S(1)} %collective-permute-done.1.refs_0_), channel_id=1, source_target_pairs={{0,4},{1,5},{4,8},{5,9},{8,12},{9,13},{6,2},{7,3},{10,6},{11,7},{1... | collective-permute-start | bytes 1572872 | tf_op jit(solution)/shard_map/ppermute | solution.py:237
  75.3 9.9 %collective-permute-done.2.refs_1_ = bf16[1024,256]{1,0:T(8,128)(2,1)} collective-permute-done((bf16[1024,256]{1,0:T(8,128)(2,1)S(1)}, bf16[1024,256]{1,0:T(8,128)(2,1)}, u32[]{:S(2)}, u32[]{:S(2)}) %collective-permute-start.2) | collective-permute-done | bytes 524320 | tf_op jit(solution)/shard_map/ppermute | solution.py:237
  85.3 1.3 %collective-permute-start.10 = (bf16[1024,256]{1,0:T(8,128)(2,1)S(1)}, bf16[1024,256]{1,0:T(8,128)(2,1)S(1)}, u32[]{:S(2)}, u32[]{:S(2)}) collective-permute-start(bf16[1024,256]{1,0:T(8,128)(2,1)S(1)} %collective-permute-done.6.refs_1_), channel_id=1, source_target_pairs={{0,1},{1,0},{2,3},{3,2},{4,5},{5,4},{6,7},{7,6},{8,9},{9,8},{10,11... | collective-permute-start | bytes 1572872 | tf_op jit(solution)/shard_map/ppermute | solution.py:237
  86.5 0.0 collective-permute-done.7.refs_2_
  86.6 0.0 collective-permute-start.9
  86.6 0.0 collective-permute-done.8.refs_3_
  86.6 0.5 collective-permute-start.11
  87.1 2.7 %collective-permute-done.3.refs_2_ = bf16[1024,256]{1,0:T(8,128)(2,1)} collective-permute-done((bf16[1024,256]{1,0:T(8,128)(2,1)S(1)}, bf16[1024,256]{1,0:T(8,128)(2,1)}, u32[]{:S(2)}, u32[]{:S(2)}) %collective-permute-start.3) | collective-permute-done | bytes 524320 | tf_op jit(solution)/shard_map/ppermute | solution.py:237
  89.8 2.4 %collective-permute-start.12 = (bf16[1024,256]{1,0:T(8,128)(2,1)}, bf16[1024,256]{1,0:T(8,128)(2,1)}, u32[]{:S(2)}, u32[]{:S(2)}) collective-permute-start(bf16[1024,256]{1,0:T(8,128)(2,1)} %collective-permute-done.8.refs_3_), channel_id=1, source_target_pairs={{0,1},{1,0},{2,3},{3,2},{4,5},{5,4},{6,7},{7,6},{8,9},{9,8},{10,11... | collective-permute-start | bytes 1572872 | tf_op jit(solution)/shard_map/ppermute | solution.py:237
  92.2 0.0 collective-permute-done.10.refs_5_
  92.2 0.0 copy-start.9
  92.2 0.1 collective-permute-start.13
  92.3 0.0 copy-done.6
  92.3 0.0 collective-permute-done.9.refs_4_
  92.3 0.0 copy-done.7
  92.3 0.0 copy-done.8
  92.3 0.7 copy-done.9
  93.0 0.0 copy-start.10
  93.0 0.8 copy-done.10
  93.8 1.3 %collective-permute-start.4 = (bf16[1024,256]{1,0:T(8,128)(2,1)}, bf16[1024,256]{1,0:T(8,128)(2,1)S(1)}, u32[]{:S(2)}, u32[]{:S(2)}) collective-permute-start(bf16[1024,256]{1,0:T(8,128)(2,1)} %collective-permute-done.2.refs_1_), channel_id=1, source_target_pairs={{0,4},{1,5},{4,8},{5,9},{8,12},{9,13},{6,2},{7,3},{10,6},{11,7},{1... | collective-permute-start | bytes 1572872 | tf_op jit(solution)/shard_map/ppermute | solution.py:237
  95.1 0.1 add_convert_fusion.flag_ref
  95.2 0.0 collective-permute-done.11.refs_6_
  95.2 0.0 collective-permute-start.14
  95.2 0.0 collective-permute-done.12.refs_7_
  95.2 0.5 collective-permute-start.15
  95.7 0.0 collective-permute-done.13.refs_8_.refs_6_
  95.7 0.0 copy-start.1
  95.7 0.0 collective-permute-done.beside
  95.7 0.0 copy-done
  95.7 0.8 copy-done.1
  96.5 9.3 %flux.2 = (bf16[1024,1024]{1,0:T(8,128)(2,1)}, f32[8,128]{1,0:T(8,128)S(1)}) custom-call(s32[2]{0:T(128)S(1)} %add_convert_fusion.flag_ref, bf16[1024,5120]{1,0:T(8,128)(2,1)} %get-tuple-element.15.dense_ref, bf16[1024,1024]{1,0:T(8,128)(2,1)} %copy-done, bf16[1024,1024]{1,0:T(8,128)(2,1)} %collective-permute-done.beside, bf16[1024,256]{1,0:T(8,128)(2,1)} %copy-done.7, ...), custom_call_target="tpu_custom_call" | custom-call | tf_op jit(solution)/shard_map/flux/pallas_call | solution.py:311
  105.8 3.6 %collective-permute-done.4.refs_0_ = bf16[1024,256]{1,0:T(8,128)(2,1)S(1)} collective-permute-done((bf16[1024,256]{1,0:T(8,128)(2,1)}, bf16[1024,256]{1,0:T(8,128)(2,1)S(1)}, u32[]{:S(2)}, u32[]{:S(2)}) %collective-permute-start.4) | collective-permute-done | bytes 524320 | tf_op jit(solution)/shard_map/ppermute | solution.py:237
  109.4 0.0 copy-start.4
  109.4 0.8 collective-permute-start.16
  110.2 0.0 collective-permute-done.14.refs_4_
  110.2 0.0 collective-permute-done.15.refs_5_
  110.2 1.5 %collective-permute-done.16.refs_7_ = bf16[1024,256]{1,0:T(8,128)(2,1)S(1)} collective-permute-done((bf16[1024,256]{1,0:T(8,128)(2,1)S(1)}, bf16[1024,256]{1,0:T(8,128)(2,1)S(1)}, u32[]{:S(2)}, u32[]{:S(2)}) %collective-permute-start.16) | collective-permute-done | bytes 524320 | tf_op jit(solution)/shard_map/ppermute | solution.py:237
  111.8 0.0 copy-done.4
  111.8 1.0 copy-done.2
  112.8 10.0 %flux.3 = (bf16[1024,1024]{1,0:T(8,128)(2,1)}, f32[8,128]{1,0:T(8,128)}) custom-call(s32[2]{0:T(128)S(1)} %add_convert_fusion.flag_ref, bf16[1024,5120]{1,0:T(8,128)(2,1)} %get-tuple-element.15.dense_ref, bf16[1024,1024]{1,0:T(8,128)(2,1)} %copy-done, bf16[1024,1024]{1,0:T(8,128)(2,1)} %collective-permute-done.beside, ...), custom_call_target="tpu_custom_call", output_to_operand_aliasing={{0}: (12, {})} | custom-call | tf_op jit(solution)/shard_map/flux/pallas_call | solution.py:311
  (2 shorter events, 0.0 us)
Async XLA Ops:
  0.0 9.4 %copy-start.5 = (s32[4,20]{1,0:T(4,128)S(1)}, s32[4,20]{1,0:T(4,128)}, u32[]{:S(2)}) copy-start(s32[4,20]{1,0:T(4,128)} %cols_ref.1) | copy-start | bytes 964
  2.6 32.6 %all-to-all-start = ((bf16[16,32,1152]{2,1,0:T(8,128)(2,1)}), bf16[16,32,1152]{2,1,0:T(8,128)(2,1)S(1)}, u32[]{:S(2)}, u32[]{:S(2)}) async-start(bf16[16,32,1152]{2,1,0:T(8,128)(2,1)} %bitcast.9), calls=%async_computation | async-start | bytes 2359296 | tf_op jit(solution)/shard_map/all_to_all | solution.py:267
  35.3 1.6 %copy-start.3 = (bf16[1024,1024]{1,0:T(8,128)(2,1)S(1)}, bf16[1024,1024]{1,0:T(8,128)(2,1)}, u32[]{:S(2)}) copy-start(bf16[1024,1024]{1,0:T(8,128)(2,1)} %base_ref.1) | copy-start | bytes 6291460
  38.2 57.5 %copy-start = (bf16[1024,1024]{1,0:T(8,128)(2,1)}, bf16[1024,1024]{1,0:T(8,128)(2,1)S(1)}, u32[]{:S(2)}) copy-start(bf16[1024,1024]{1,0:T(8,128)(2,1)S(1)} %get-tuple-element.17.own) | copy-start | bytes 6291460
  38.3 57.4 %collective-permute-start = (bf16[1024,1024]{1,0:T(8,128)(2,1)S(1)}, bf16[1024,1024]{1,0:T(8,128)(2,1)}, u32[]{:S(2)}, u32[]{:S(2)}) collective-permute-start(bf16[1024,1024]{1,0:T(8,128)(2,1)S(1)} %get-tuple-element.17.own), channel_id=1, source_target_pairs={{0,1},{1,0},{2,3},{3,2},{4,5},{5,4},{6,7},{7,6},{8,9},{9,8},{10,11... | collective-permute-start | bytes 6291464 | tf_op jit(solution)/shard_map/ppermute | solution.py:237
  38.3 13.1 %collective-permute-start.5 = (bf16[1024,256]{1,0:T(8,128)(2,1)S(1)}, bf16[1024,256]{1,0:T(8,128)(2,1)S(1)}, u32[]{:S(2)}, u32[]{:S(2)}) collective-permute-start(bf16[1024,256]{1,0:T(8,128)(2,1)S(1)} %get-tuple-element.20), channel_id=1, source_target_pairs={{0,2},{1,3},{2,0},{3,1},{4,6},{5,7},{6,4},{7,5},{8,10},{9,11},{10,... | collective-permute-start | bytes 1572872 | tf_op jit(solution)/shard_map/ppermute | solution.py:237
  38.4 24.4 %collective-permute-start.6 = (bf16[1024,256]{1,0:T(8,128)(2,1)S(1)}, bf16[1024,256]{1,0:T(8,128)(2,1)S(1)}, u32[]{:S(2)}, u32[]{:S(2)}) collective-permute-start(bf16[1024,256]{1,0:T(8,128)(2,1)S(1)} %get-tuple-element.21), channel_id=1, source_target_pairs={{0,2},{1,3},{2,0},{3,1},{4,6},{5,7},{6,4},{7,5},{8,10},{9,11},{10,... | collective-permute-start | bytes 1572872 | tf_op jit(solution)/shard_map/ppermute | solution.py:237
  39.9 34.2 %collective-permute-start.1 = (bf16[1024,256]{1,0:T(8,128)(2,1)S(1)}, bf16[1024,256]{1,0:T(8,128)(2,1)S(1)}, u32[]{:S(2)}, u32[]{:S(2)}) collective-permute-start(bf16[1024,256]{1,0:T(8,128)(2,1)S(1)} %get-tuple-element.18), channel_id=1, source_target_pairs={{0,2},{1,3},{2,0},{3,1},{4,6},{5,7},{6,4},{7,5},{8,10},{9,11},{10,... | collective-permute-start | bytes 1572872 | tf_op jit(solution)/shard_map/ppermute | solution.py:237
  39.9 45.3 %collective-permute-start.2 = (bf16[1024,256]{1,0:T(8,128)(2,1)S(1)}, bf16[1024,256]{1,0:T(8,128)(2,1)}, u32[]{:S(2)}, u32[]{:S(2)}) collective-permute-start(bf16[1024,256]{1,0:T(8,128)(2,1)S(1)} %get-tuple-element.19), channel_id=1, source_target_pairs={{0,2},{1,3},{2,0},{3,1},{4,6},{5,7},{6,4},{7,5},{8,10},{9,11},{10,... | collective-permute-start | bytes 1572872 | tf_op jit(solution)/shard_map/ppermute | solution.py:237
  51.5 40.8 %copy-start.7 = (bf16[1024,256]{1,0:T(8,128)(2,1)}, bf16[1024,256]{1,0:T(8,128)(2,1)S(1)}, u32[]{:S(2)}) copy-start(bf16[1024,256]{1,0:T(8,128)(2,1)S(1)} %collective-permute-done.5.refs_0_) | copy-start | bytes 1572868
  51.5 35.1 %collective-permute-start.7 = (bf16[1024,256]{1,0:T(8,128)(2,1)S(1)}, bf16[1024,256]{1,0:T(8,128)(2,1)}, u32[]{:S(2)}, u32[]{:S(2)}) collective-permute-start(bf16[1024,256]{1,0:T(8,128)(2,1)S(1)} %collective-permute-done.5.refs_0_), channel_id=1, source_target_pairs={{0,4},{1,5},{4,8},{5,9},{8,12},{9,13},{6,2},{7,3},{10,6},{11,7},{1... | collective-permute-start | bytes 1572872 | tf_op jit(solution)/shard_map/ppermute | solution.py:237
  62.8 29.5 %copy-start.8 = (bf16[1024,256]{1,0:T(8,128)(2,1)}, bf16[1024,256]{1,0:T(8,128)(2,1)S(1)}, u32[]{:S(2)}) copy-start(bf16[1024,256]{1,0:T(8,128)(2,1)S(1)} %collective-permute-done.6.refs_1_) | copy-start | bytes 1572868
  62.8 23.8 %collective-permute-start.8 = (bf16[1024,256]{1,0:T(8,128)(2,1)S(1)}, bf16[1024,256]{1,0:T(8,128)(2,1)}, u32[]{:S(2)}, u32[]{:S(2)}) collective-permute-start(bf16[1024,256]{1,0:T(8,128)(2,1)S(1)} %collective-permute-done.6.refs_1_), channel_id=1, source_target_pairs={{0,4},{1,5},{4,8},{5,9},{8,12},{9,13},{6,2},{7,3},{10,6},{11,7},{1... | collective-permute-start | bytes 1572872 | tf_op jit(solution)/shard_map/ppermute | solution.py:237
  74.0 18.2 %copy-start.6 = (bf16[1024,256]{1,0:T(8,128)(2,1)}, bf16[1024,256]{1,0:T(8,128)(2,1)S(1)}, u32[]{:S(2)}) copy-start(bf16[1024,256]{1,0:T(8,128)(2,1)S(1)} %collective-permute-done.1.refs_0_) | copy-start | bytes 1572868
  74.0 15.8 %collective-permute-start.3 = (bf16[1024,256]{1,0:T(8,128)(2,1)S(1)}, bf16[1024,256]{1,0:T(8,128)(2,1)}, u32[]{:S(2)}, u32[]{:S(2)}) collective-permute-start(bf16[1024,256]{1,0:T(8,128)(2,1)S(1)} %collective-permute-done.1.refs_0_), channel_id=1, source_target_pairs={{0,4},{1,5},{4,8},{5,9},{8,12},{9,13},{6,2},{7,3},{10,6},{11,7},{1... | collective-permute-start | bytes 1572872 | tf_op jit(solution)/shard_map/ppermute | solution.py:237
  85.3 6.9 %collective-permute-start.10 = (bf16[1024,256]{1,0:T(8,128)(2,1)S(1)}, bf16[1024,256]{1,0:T(8,128)(2,1)S(1)}, u32[]{:S(2)}, u32[]{:S(2)}) collective-permute-start(bf16[1024,256]{1,0:T(8,128)(2,1)S(1)} %collective-permute-done.6.refs_1_), channel_id=1, source_target_pairs={{0,1},{1,0},{2,3},{3,2},{4,5},{5,4},{6,7},{7,6},{8,9},{9,8},{10,11... | collective-permute-start | bytes 1572872 | tf_op jit(solution)/shard_map/ppermute | solution.py:237
  86.6 5.7 %collective-permute-start.9 = (bf16[1024,256]{1,0:T(8,128)(2,1)S(1)}, bf16[1024,256]{1,0:T(8,128)(2,1)S(1)}, u32[]{:S(2)}, u32[]{:S(2)}) collective-permute-start(bf16[1024,256]{1,0:T(8,128)(2,1)S(1)} %collective-permute-done.5.refs_0_), channel_id=1, source_target_pairs={{0,1},{1,0},{2,3},{3,2},{4,5},{5,4},{6,7},{7,6},{8,9},{9,8},{10,11... | collective-permute-start | bytes 1572872 | tf_op jit(solution)/shard_map/ppermute | solution.py:237
  86.6 8.6 %collective-permute-start.11 = (bf16[1024,256]{1,0:T(8,128)(2,1)}, bf16[1024,256]{1,0:T(8,128)(2,1)}, u32[]{:S(2)}, u32[]{:S(2)}) collective-permute-start(bf16[1024,256]{1,0:T(8,128)(2,1)} %collective-permute-done.7.refs_2_), channel_id=1, source_target_pairs={{0,1},{1,0},{2,3},{3,2},{4,5},{5,4},{6,7},{7,6},{8,9},{9,8},{10,11... | collective-permute-start | bytes 1572872 | tf_op jit(solution)/shard_map/ppermute | solution.py:237
  89.8 5.4 %collective-permute-start.12 = (bf16[1024,256]{1,0:T(8,128)(2,1)}, bf16[1024,256]{1,0:T(8,128)(2,1)}, u32[]{:S(2)}, u32[]{:S(2)}) collective-permute-start(bf16[1024,256]{1,0:T(8,128)(2,1)} %collective-permute-done.8.refs_3_), channel_id=1, source_target_pairs={{0,1},{1,0},{2,3},{3,2},{4,5},{5,4},{6,7},{7,6},{8,9},{9,8},{10,11... | collective-permute-start | bytes 1572872 | tf_op jit(solution)/shard_map/ppermute | solution.py:237
  92.2 0.8 copy-start.9
  92.2 3.5 %collective-permute-start.13 = (bf16[1024,256]{1,0:T(8,128)(2,1)}, bf16[1024,256]{1,0:T(8,128)(2,1)S(1)}, u32[]{:S(2)}, u32[]{:S(2)}) collective-permute-start(bf16[1024,256]{1,0:T(8,128)(2,1)} %collective-permute-done.3.refs_2_), channel_id=1, source_target_pairs={{0,1},{1,0},{2,3},{3,2},{4,5},{5,4},{6,7},{7,6},{8,9},{9,8},{10,11... | collective-permute-start | bytes 1572872 | tf_op jit(solution)/shard_map/ppermute | solution.py:237
  93.0 0.8 copy-start.10
  93.8 15.6 %collective-permute-start.4 = (bf16[1024,256]{1,0:T(8,128)(2,1)}, bf16[1024,256]{1,0:T(8,128)(2,1)S(1)}, u32[]{:S(2)}, u32[]{:S(2)}) collective-permute-start(bf16[1024,256]{1,0:T(8,128)(2,1)} %collective-permute-done.2.refs_1_), channel_id=1, source_target_pairs={{0,4},{1,5},{4,8},{5,9},{8,12},{9,13},{6,2},{7,3},{10,6},{11,7},{1... | collective-permute-start | bytes 1572872 | tf_op jit(solution)/shard_map/ppermute | solution.py:237
  95.2 15.1 %collective-permute-start.14 = (bf16[1024,256]{1,0:T(8,128)(2,1)}, bf16[1024,256]{1,0:T(8,128)(2,1)S(1)}, u32[]{:S(2)}, u32[]{:S(2)}) collective-permute-start(bf16[1024,256]{1,0:T(8,128)(2,1)} %copy-done.6), channel_id=1, source_target_pairs={{0,1},{1,0},{2,3},{3,2},{4,5},{5,4},{6,7},{7,6},{8,9},{9,8},{10,11... | collective-permute-start | bytes 1572872 | tf_op jit(solution)/shard_map/ppermute | solution.py:237
  95.2 15.0 %collective-permute-start.15 = (bf16[1024,256]{1,0:T(8,128)(2,1)}, bf16[1024,256]{1,0:T(8,128)(2,1)S(1)}, u32[]{:S(2)}, u32[]{:S(2)}) collective-permute-start(bf16[1024,256]{1,0:T(8,128)(2,1)} %collective-permute-done.2.refs_1_), channel_id=1, source_target_pairs={{0,1},{1,0},{2,3},{3,2},{4,5},{5,4},{6,7},{7,6},{8,9},{9,8},{10,11... | collective-permute-start | bytes 1572872 | tf_op jit(solution)/shard_map/ppermute | solution.py:237
  95.7 0.8 copy-start.1
  109.4 2.3 %copy-start.4 = (bf16[1024,256]{1,0:T(8,128)(2,1)}, bf16[1024,256]{1,0:T(8,128)(2,1)S(1)}, u32[]{:S(2)}) copy-start(bf16[1024,256]{1,0:T(8,128)(2,1)S(1)} %gate.1.refs_3_) | copy-start | bytes 1572868
  109.4 2.3 %collective-permute-start.16 = (bf16[1024,256]{1,0:T(8,128)(2,1)S(1)}, bf16[1024,256]{1,0:T(8,128)(2,1)S(1)}, u32[]{:S(2)}, u32[]{:S(2)}) collective-permute-start(bf16[1024,256]{1,0:T(8,128)(2,1)S(1)} %gate.1.refs_3_), channel_id=1, source_target_pairs={{0,1},{1,0},{2,3},{3,2},{4,5},{5,4},{6,7},{7,6},{8,9},{9,8},{10,11... | collective-permute-start | bytes 1572872 | tf_op jit(solution)/shard_map/ppermute | solution.py:237
  111.8 1.0 copy-start.2

commit v4 on v3

--- a/solution.py
+++ b/solution.py
@@ -10,6 +10,7 @@
 HALO = 2
 PIECES = 1
 AHEAD = 3
+SIGN = 2
 LANES = 128
 RADIX = 32
 VMEM = pl.BlockSpec(memory_space=pltpu.VMEM)
@@ -49,7 +50,7 @@
 
 def chunk_sizes(width):
     unit = width // 8
-    return [2 * unit] * 4
+    return [2 * unit, 2 * unit, 2 * unit, 2 * unit]
 
 
 def pack_kernel(capacity, owner_hbm, target_hbm, rows_hbm, out_ref, owner_ref, target_ref, rows_ref, sems):
@@ -163,18 +164,27 @@
         self.flag, self.dense, self.slots = flag, dense_ref, slots
         self.matrix, self.window, self.mat_sems, self.sems = matrix, window, mat_sems, sems
 
+    def block(self, slot):
+        depth = self.dense.shape[0]
+        if self.matrix is None:
+            return self.dense[:, slot * depth : (slot + 1) * depth]
+        self.columns(slot).wait()
+        return self.matrix[slot]
+
     def columns(self, slot):
         depth = self.dense.shape[0]
         there = self.dense.at[:, pl.ds(slot * depth, depth)]
         return pltpu.make_async_copy(there, self.matrix.at[slot], self.mat_sems.at[slot])
 
     def rows(self, slot, i, piece):
-        size = piece.shape[1]
-        target = self.window.at[slot, :, pl.ds(i * size, size)]
+        before = [item[0] if isinstance(item, tuple) else item for item in self.slots[slot][:i]]
+        start = sum(item.shape[1] for item in before)
+        target = self.window.at[slot, :, pl.ds(start, piece.shape[1])]
         return pltpu.make_async_copy(piece, target, self.sems.at[slot, i])
 
     def begin(self, slot):
-        self.columns(slot).start()
+        if self.matrix is not None:
+            self.columns(slot).start()
         for i, piece in enumerate(self.slots[slot]):
             if not isinstance(piece, tuple):
                 self.rows(slot, i, piece).start()
@@ -189,12 +199,11 @@
             self.begin(slot)
         last = len(self.slots) - 1
         for slot, pieces in enumerate(self.slots):
-            self.columns(slot).wait()
             for i, piece in enumerate(pieces):
                 self.rows(slot, i, piece[0] if isinstance(piece, tuple) else piece).wait()
             if slot + AHEAD <= last:
                 self.begin(slot + AHEAD)
-            part = jnp.dot(self.matrix[slot], self.window[slot], preferred_element_type=jnp.float32)
+            part = jnp.dot(self.block(slot), self.window[slot], preferred_element_type=jnp.float32)
             if slot == 0:
                 total_ref[...] = part
             elif slot < last:
@@ -205,6 +214,8 @@
 def flux_kernel(offset, count, paired, flag_ref, dense_ref, own, beside, *refs):
     out_ref, token_ref, matrix, window, total, result, mat_sems, sems, out_sem = refs[-9:]
     token_ref[...] = jnp.zeros_like(token_ref)
+    if offset:
+        matrix = None
     there = pl.ds(offset, total.shape[1])
     peers, passed = refs[:count], refs[count : 2 * count]
     slots = [[own.at[:, there]], [beside.at[:, there]], peers, passed]
@@ -302,42 +313,52 @@
 
     passed = [send(peer, relay) for peer in peers]
 
-    size = sizes[0]
-    half = len(sizes) // 2
+    half = 2
     out_type = pltpu.HBM((seg_dev, width), jnp.bfloat16)
 
-    def flux(start, chunks, others, paired, out, after=()):
+    def flux(chunks, others, out, after=()):
         given = [dense, whole, beside] + peers[chunks] + passed[chunks] + others + out
+        wide, many = sum(sizes[chunks]), len(sizes[chunks])
+        start = starts[chunks][0]
+        loose = [item for item in others if start]
         return pl.pallas_call(
-            functools.partial(flux_kernel, start, half, paired),
+            functools.partial(flux_kernel, start, many, True),
             out_shape=(out_type, TOKEN),
             in_specs=[SMEM]
-            + [ANY if start and any(item is other for other in others) else HBM for item in given]
-            + [HBM] * len(after),
+            + [VMEM if start and item is dense else ANY if any(item is other for other in loose) else HBM for item in given]
+            + [ANY] * len(after),
             out_specs=(HBM, VMEM),
             scratch_shapes=[
-                pltpu.VMEM((SLOTS, seg_dev, seg_dev), jnp.bfloat16),
-                pltpu.VMEM((SLOTS, seg_dev, half * size), jnp.bfloat16),
-                pltpu.VMEM((seg_dev, half * size), jnp.float32),
-                pltpu.VMEM((seg_dev, half * size), jnp.bfloat16),
+                pltpu.VMEM((1, 8, LANES) if start else (SLOTS, seg_dev, seg_dev), jnp.bfloat16),
+                pltpu.VMEM((SLOTS, seg_dev, wide), jnp.bfloat16),
+                pltpu.VMEM((seg_dev, wide), jnp.float32),
+                pltpu.VMEM((seg_dev, wide), jnp.bfloat16),
                 pltpu.SemaphoreType.DMA((SLOTS,)),
-                pltpu.SemaphoreType.DMA((SLOTS, half * PIECES)),
+                pltpu.SemaphoreType.DMA((SLOTS, many)),
                 pltpu.SemaphoreType.DMA,
             ],
             input_output_aliases={len(given): 0} if out else {},
-            compiler_params=limit(36),
+            compiler_params=limit(20 if start else 36),
             cost_estimate=cost(),
             name="flux",
-        )(flag, *[in_hbm(item) if start == 0 or not any(item is other for other in others) else item for item in (*given, *after)])
+        )(
+            flag,
+            *[item if any(item is other for other in loose + [dense] * (start > 0)) else in_hbm(item) for item in given],
+            *after,
+        )
 
     across_beside = [send(peer, partner) for peer in peers]
-    passed_beside = [send(item, partner) for item in passed[:3]]
+    passed_beside = [send(item, partner) for item in passed[:-1]]
+    sign = passed[SIGN][:16, :LANES]
+    for _ in range(3):
+        sign = gate(sign, flag)
+    after = [sign]
     others = across_beside[:half] + passed_beside[:half]
-    out, token = flux(0, slice(0, half), others, True, [], [passed_beside[2]])
-    passed[3] = gate(passed[3], token)
-    passed_beside.append(send(passed[3], partner))
+    out, token = flux(slice(0, half), others, [], after)
+    passed[-1] = gate(passed[-1], token)
+    passed_beside.append(send(passed[-1], partner))
     others = across_beside[half:] + passed_beside[half:]
-    out, _ = flux(half * size, slice(half, 2 * half), others, True, [out])
+    out, _ = flux(slice(half, len(sizes)), others, [out])
     return out
 
 

time: 124 us -> 122 us (0.984)
  local copies, waits for them, and re-layouts: 5.02 us -> 2.49 us
    unnamed x22, local copies, waits for them, and re-layouts: 4.94 us -> 2.4 us
where the time goes in v4:
time: 122 us; the launch traced here: 120 us
  waiting for transfers between devices  63.4 us (52%)
  Pallas kernels  33.9 us (28%)
  starting transfers between devices  20.3 us (17%)
  local copies, waits for them, and re-layouts  2.49 us (2%)
    ppermute x17, waiting for transfers between devices, send(): return lax.ppermute(value, 'row', pairs)  48.6 us
    pallas_call x2, Pallas kernels, flux(): pl.pallas_call(functools.partial(flux_kernel, start, many, True), out_sha...  18.9 us
    all_to_all x1, waiting for transfers between devices, shards(): lax.all_to_all(outgoing.reshape(devices, capacity, width + LANES), 'row',...  14.8 us
    ppermute x17, starting transfers between devices, send(): return lax.ppermute(value, 'row', pairs)  13.6 us
    pallas_call x1, Pallas kernels, shards(): pl.pallas_call(dense_kernel, out_shape=(pltpu.HBM((seg_dev, SLOTS * seg_d...  11 us
    all_to_all x1, starting transfers between devices, shards(): lax.all_to_all(outgoing.reshape(devices, capacity, width + LANES), 'row',...  6.68 us
    pallas_call x1, Pallas kernels, shards(): pl.pallas_call(functools.partial(pack_kernel, capacity), out_shape=jax.Sh...  2.61 us
  transfers between devices with their start and end apart: 18, of which 8 were waited for; matrix products, arithmetic and copies ran while one was open for 0% of the time, Pallas kernels for 17%

profile of v4, /device:TPU:7, one launch (start us, length us, event | category | flops | bytes accessed | tf_op | source)
XLA Modules:
  0.0 120.4 jit_solution(15667883193049696611)
XLA Ops:
  0.0 0.0 copy-start.3
  0.0 2.6 %pack_terms.1.wait_ref = bf16[512,1152]{1,0:T(8,128)(2,1)} custom-call(s32[1,256]{1,0:T(1,128)} %bitcast.14, s32[1,256]{1,0:T(1,128)} %bitcast.15, bf16[256,1024]{1,0:T(8,128)(2,1)} %rows_hbm.1), custom_call_target="tpu_custom_call" | custom-call | tf_op jit(solution)/shard_map/pack_terms/pallas_call | solution.py:264
  2.6 6.7 %all-to-all-start = ((bf16[16,32,1152]{2,1,0:T(8,128)(2,1)}), bf16[16,32,1152]{2,1,0:T(8,128)(2,1)S(1)}, u32[]{:S(2)}, u32[]{:S(2)}) async-start(bf16[16,32,1152]{2,1,0:T(8,128)(2,1)} %bitcast.9), calls=%async_computation | async-start | bytes 2359296 | tf_op jit(solution)/shard_map/all_to_all | solution.py:278
  9.3 0.1 stack.35.slot_ref
  9.4 0.0 copy-done.3
  9.4 11.0 %dense_blocks.1 = (bf16[1024,5120]{1,0:T(8,128)(2,1)}, f32[8,128]{1,0:T(8,128)S(1)}) custom-call(s32[4,20]{1,0:T(4,128)S(1)} %copy-done.3, s32[6]{0:T(128)S(1)} %stack.35.slot_ref, bf16[4,20,256,256]{3,2,1,0:T(8,128)(2,1)} %blocks_ref.1, bf16[512,1152]{1,0:T(8,128)(2,1)} %pack_terms.1.wait_ref), custom_call_target="tpu_custom_call" | custom-call | tf_op jit(solution)/shard_map/dense_blocks/pallas_call | solution.py:282
  20.4 14.8 %all-to-all-done = bf16[16,32,1152]{2,1,0:T(8,128)(2,1)S(1)} async-done(((bf16[16,32,1152]{2,1,0:T(8,128)(2,1)}), bf16[16,32,1152]{2,1,0:T(8,128)(2,1)S(1)}, u32[]{:S(2)}, u32[]{:S(2)}) %all-to-all-start) | async-done | bytes 1179680 | tf_op jit(solution)/shard_map/all_to_all | solution.py:278
  35.3 0.0 copy-start.1
  35.3 1.6 %copy-done.1 = bf16[1024,1024]{1,0:T(8,128)(2,1)S(1)} copy-done((bf16[1024,1024]{1,0:T(8,128)(2,1)S(1)}, bf16[1024,1024]{1,0:T(8,128)(2,1)}, u32[]{:S(2)}) %copy-start.1) | copy-done | bytes 2097176
  36.9 1.4 %inject_terms.1 = (bf16[1024,1024]{1,0:T(8,128)(2,1)S(1)}, bf16[1024,256]{1,0:T(8,128)(2,1)S(1)}, bf16[1024,256]{1,0:T(8,128)(2,1)S(1)}, bf16[1024,256]{1,0:T(8,128)(2,1)S(1)}, bf16[1024,256]{1,0:T(8,128)(2,1)S(1)}) custom-call(bf16[1024,1024]{1,0:T(8,128)(2,1)S(1)} %copy-done.1, bf16[512,1152]{1,0:T(8,128)(2,1)S(1)} %bitcast.13, ...), custom_call_target="tpu_custom_call" | custom-call | tf_op jit(solution)/shard_map/inject_terms/pallas_call | solution.py:297
  38.2 0.0 copy-start
  38.3 0.1 collective-permute-start
  38.3 0.1 collective-permute-start.5
  38.4 1.5 %collective-permute-start.6 = (bf16[1024,256]{1,0:T(8,128)(2,1)S(1)}, bf16[1024,256]{1,0:T(8,128)(2,1)S(1)}, u32[]{:S(2)}, u32[]{:S(2)}) collective-permute-start(bf16[1024,256]{1,0:T(8,128)(2,1)S(1)} %get-tuple-element.21), channel_id=1, source_target_pairs={{0,2},{1,3},{2,0},{3,1},{4,6},{5,7},{6,4},{7,5},{8,10},{9,11},{10,... | collective-permute-start | bytes 1572872 | tf_op jit(solution)/shard_map/ppermute | solution.py:248
  39.9 0.1 collective-permute-start.1
  39.9 1.4 %collective-permute-start.2 = (bf16[1024,256]{1,0:T(8,128)(2,1)S(1)}, bf16[1024,256]{1,0:T(8,128)(2,1)}, u32[]{:S(2)}, u32[]{:S(2)}) collective-permute-start(bf16[1024,256]{1,0:T(8,128)(2,1)S(1)} %get-tuple-element.19), channel_id=1, source_target_pairs={{0,2},{1,3},{2,0},{3,1},{4,6},{5,7},{6,4},{7,5},{8,10},{9,11},{10,... | collective-permute-start | bytes 1572872 | tf_op jit(solution)/shard_map/ppermute | solution.py:248
  41.3 10.2 %collective-permute-done.5.refs_0_ = bf16[1024,256]{1,0:T(8,128)(2,1)} collective-permute-done((bf16[1024,256]{1,0:T(8,128)(2,1)S(1)}, bf16[1024,256]{1,0:T(8,128)(2,1)}, u32[]{:S(2)}, u32[]{:S(2)}) %collective-permute-start.5) | collective-permute-done | bytes 524320 | tf_op jit(solution)/shard_map/ppermute | solution.py:248
  51.6 1.3 %collective-permute-start.7 = (bf16[1024,256]{1,0:T(8,128)(2,1)}, bf16[1024,256]{1,0:T(8,128)(2,1)}, u32[]{:S(2)}, u32[]{:S(2)}) collective-permute-start(bf16[1024,256]{1,0:T(8,128)(2,1)} %collective-permute-done.5.refs_0_), channel_id=1, source_target_pairs={{0,4},{1,5},{4,8},{5,9},{8,12},{9,13},{6,2},{7,3},{10,6},{11,7},{1... | collective-permute-start | bytes 1572872 | tf_op jit(solution)/shard_map/ppermute | solution.py:248
  52.9 9.9 %collective-permute-done.6.refs_1_ = bf16[1024,256]{1,0:T(8,128)(2,1)S(1)} collective-permute-done((bf16[1024,256]{1,0:T(8,128)(2,1)S(1)}, bf16[1024,256]{1,0:T(8,128)(2,1)S(1)}, u32[]{:S(2)}, u32[]{:S(2)}) %collective-permute-start.6) | collective-permute-done | bytes 524320 | tf_op jit(solution)/shard_map/ppermute | solution.py:248
  62.8 0.0 copy-start.6
  62.8 1.3 %collective-permute-start.8 = (bf16[1024,256]{1,0:T(8,128)(2,1)S(1)}, bf16[1024,256]{1,0:T(8,128)(2,1)}, u32[]{:S(2)}, u32[]{:S(2)}) collective-permute-start(bf16[1024,256]{1,0:T(8,128)(2,1)S(1)} %collective-permute-done.6.refs_1_), channel_id=1, source_target_pairs={{0,4},{1,5},{4,8},{5,9},{8,12},{9,13},{6,2},{7,3},{10,6},{11,7},{1... | collective-permute-start | bytes 1572872 | tf_op jit(solution)/shard_map/ppermute | solution.py:248
  64.1 9.9 %collective-permute-done.1.refs_0_ = bf16[1024,256]{1,0:T(8,128)(2,1)S(1)} collective-permute-done((bf16[1024,256]{1,0:T(8,128)(2,1)S(1)}, bf16[1024,256]{1,0:T(8,128)(2,1)S(1)}, u32[]{:S(2)}, u32[]{:S(2)}) %collective-permute-start.1) | collective-permute-done | bytes 524320 | tf_op jit(solution)/shard_map/ppermute | solution.py:248
  74.0 0.0 copy-start.5
  74.0 1.3 %collective-permute-start.3 = (bf16[1024,256]{1,0:T(8,128)(2,1)S(1)}, bf16[1024,256]{1,0:T(8,128)(2,1)S(1)}, u32[]{:S(2)}, u32[]{:S(2)}) collective-permute-start(bf16[1024,256]{1,0:T(8,128)(2,1)S(1)} %collective-permute-done.1.refs_0_), channel_id=1, source_target_pairs={{0,4},{1,5},{4,8},{5,9},{8,12},{9,13},{6,2},{7,3},{10,6},{11,7},{1... | collective-permute-start | bytes 1572872 | tf_op jit(solution)/shard_map/ppermute | solution.py:248
  75.3 9.9 %collective-permute-done.2.refs_1_ = bf16[1024,256]{1,0:T(8,128)(2,1)} collective-permute-done((bf16[1024,256]{1,0:T(8,128)(2,1)S(1)}, bf16[1024,256]{1,0:T(8,128)(2,1)}, u32[]{:S(2)}, u32[]{:S(2)}) %collective-permute-start.2) | collective-permute-done | bytes 524320 | tf_op jit(solution)/shard_map/ppermute | solution.py:248
  85.3 1.3 %collective-permute-start.10 = (bf16[1024,256]{1,0:T(8,128)(2,1)S(1)}, bf16[1024,256]{1,0:T(8,128)(2,1)S(1)}, u32[]{:S(2)}, u32[]{:S(2)}) collective-permute-start(bf16[1024,256]{1,0:T(8,128)(2,1)S(1)} %collective-permute-done.6.refs_1_), channel_id=1, source_target_pairs={{0,1},{1,0},{2,3},{3,2},{4,5},{5,4},{6,7},{7,6},{8,9},{9,8},{10,11... | collective-permute-start | bytes 1572872 | tf_op jit(solution)/shard_map/ppermute | solution.py:248
  86.5 0.0 collective-permute-done.7.refs_2_
  86.6 0.0 collective-permute-start.9
  86.6 0.0 collective-permute-done.8.refs_3_
  86.6 0.5 collective-permute-start.11
  87.1 3.0 %collective-permute-done.3.refs_2_ = bf16[1024,256]{1,0:T(8,128)(2,1)S(1)} collective-permute-done((bf16[1024,256]{1,0:T(8,128)(2,1)S(1)}, bf16[1024,256]{1,0:T(8,128)(2,1)S(1)}, u32[]{:S(2)}, u32[]{:S(2)}) %collective-permute-start.3) | collective-permute-done | bytes 524320 | tf_op jit(solution)/shard_map/ppermute | solution.py:248
  90.1 0.0 copy-start.4
  90.1 2.2 %collective-permute-start.12 = (bf16[1024,256]{1,0:T(8,128)(2,1)}, bf16[1024,256]{1,0:T(8,128)(2,1)}, u32[]{:S(2)}, u32[]{:S(2)}) collective-permute-start(bf16[1024,256]{1,0:T(8,128)(2,1)} %collective-permute-done.8.refs_3_), channel_id=1, source_target_pairs={{0,1},{1,0},{2,3},{3,2},{4,5},{5,4},{6,7},{7,6},{8,9},{9,8},{10,11... | collective-permute-start | bytes 1572872 | tf_op jit(solution)/shard_map/ppermute | solution.py:248
  92.3 0.0 copy-done.5
  92.3 0.0 collective-permute-done.10.refs_5_
  92.3 0.0 copy-done.6
  92.3 0.0 copy-start.7
  92.3 0.8 copy-done.7
  93.1 1.3 %collective-permute-start.4 = (bf16[1024,256]{1,0:T(8,128)(2,1)}, bf16[1024,256]{1,0:T(8,128)(2,1)S(1)}, u32[]{:S(2)}, u32[]{:S(2)}) collective-permute-start(bf16[1024,256]{1,0:T(8,128)(2,1)} %collective-permute-done.2.refs_1_), channel_id=1, source_target_pairs={{0,4},{1,5},{4,8},{5,9},{8,12},{9,13},{6,2},{7,3},{10,6},{11,7},{1... | collective-permute-start | bytes 1572872 | tf_op jit(solution)/shard_map/ppermute | solution.py:248
  94.4 0.1 add_convert_fusion.refs_1_.flag_ref
  94.5 0.0 collective-permute-done.9.refs_4_
  94.5 0.1 collective-permute-start.13
  94.6 0.0 collective-permute-done.11.refs_6_
  94.6 0.5 collective-permute-start.14
  95.0 0.0 collective-permute-done.12.refs_7_
  95.0 0.1 collective-permute-start.15
  95.1 0.0 collective-permute-done.beside
  95.1 0.0 slice-start
  95.1 0.0 copy-done
  95.1 0.0 slice-start.2
  95.1 9.6 %flux.2 = (bf16[1024,1024]{1,0:T(8,128)(2,1)}, f32[8,128]{1,0:T(8,128)S(1)}) custom-call(s32[2]{0:T(128)S(1)} %add_convert_fusion.refs_1_.flag_ref, bf16[1024,5120]{1,0:T(8,128)(2,1)} %get-tuple-element.15.dense_ref, bf16[1024,1024]{1,0:T(8,128)(2,1)} %copy-done, bf16[1024,1024]{1,0:T(8,128)(2,1)} %collective-permute-done.beside, ...), custom_call_target="tpu_custom_call" | custom-call | tf_op jit(solution)/shard_map/flux/pallas_call | solution.py:324
  104.7 0.0 copy-done.4
  104.8 3.9 %collective-permute-done.4.refs_0_ = bf16[1024,256]{1,0:T(8,128)(2,1)S(1)} collective-permute-done((bf16[1024,256]{1,0:T(8,128)(2,1)}, bf16[1024,256]{1,0:T(8,128)(2,1)S(1)}, u32[]{:S(2)}, u32[]{:S(2)}) %collective-permute-start.4) | collective-permute-done | bytes 524320 | tf_op jit(solution)/shard_map/ppermute | solution.py:248
  108.7 0.0 copy-start.2
  108.7 0.8 collective-permute-start.16
  109.5 0.0 collective-permute-done.13.refs_4_
  109.5 0.0 collective-permute-done.14.refs_5_
  109.5 0.0 collective-permute-done.15.refs_6_
  109.5 1.5 %collective-permute-done.16.refs_7_ = bf16[1024,256]{1,0:T(8,128)(2,1)S(1)} collective-permute-done((bf16[1024,256]{1,0:T(8,128)(2,1)S(1)}, bf16[1024,256]{1,0:T(8,128)(2,1)S(1)}, u32[]{:S(2)}, u32[]{:S(2)}) %collective-permute-start.16) | collective-permute-done | bytes 524320 | tf_op jit(solution)/shard_map/ppermute | solution.py:248
  111.0 0.0 copy-done.2
  111.0 0.0 slice-done
  111.1 0.0 slice-done.1
  111.1 0.0 slice-done.2
  111.1 9.3 %flux.3 = (bf16[1024,1024]{1,0:T(8,128)(2,1)}, f32[8,128]{1,0:T(8,128)}) custom-call(s32[2]{0:T(128)S(1)} %add_convert_fusion.refs_1_.flag_ref, bf16[1024,5120]{1,0:T(8,128)(2,1)S(1)} %bitcast.12, bf16[1024,1024]{1,0:T(8,128)(2,1)} %copy-done, bf16[1024,1024]{1,0:T(8,128)(2,1)} %collective-permute-done.beside, ...), custom_call_target="tpu_custom_call", output_to_operand_aliasing={{0}: (12, {})} | custom-call | tf_op jit(solution)/shard_map/flux/pallas_call | solution.py:324
  (7 shorter events, 0.0 us)
Async XLA Ops:
  0.0 9.4 %copy-start.3 = (s32[4,20]{1,0:T(4,128)S(1)}, s32[4,20]{1,0:T(4,128)}, u32[]{:S(2)}) copy-start(s32[4,20]{1,0:T(4,128)} %cols_ref.1) | copy-start | bytes 964
  2.6 32.6 %all-to-all-start = ((bf16[16,32,1152]{2,1,0:T(8,128)(2,1)}), bf16[16,32,1152]{2,1,0:T(8,128)(2,1)S(1)}, u32[]{:S(2)}, u32[]{:S(2)}) async-start(bf16[16,32,1152]{2,1,0:T(8,128)(2,1)} %bitcast.9), calls=%async_computation | async-start | bytes 2359296 | tf_op jit(solution)/shard_map/all_to_all | solution.py:278
  35.3 1.6 %copy-start.1 = (bf16[1024,1024]{1,0:T(8,128)(2,1)S(1)}, bf16[1024,1024]{1,0:T(8,128)(2,1)}, u32[]{:S(2)}) copy-start(bf16[1024,1024]{1,0:T(8,128)(2,1)} %base_ref.1) | copy-start | bytes 6291460
  38.2 56.9 %copy-start = (bf16[1024,1024]{1,0:T(8,128)(2,1)}, bf16[1024,1024]{1,0:T(8,128)(2,1)S(1)}, u32[]{:S(2)}) copy-start(bf16[1024,1024]{1,0:T(8,128)(2,1)S(1)} %get-tuple-element.17.own) | copy-start | bytes 6291460
  38.3 56.9 %collective-permute-start = (bf16[1024,1024]{1,0:T(8,128)(2,1)S(1)}, bf16[1024,1024]{1,0:T(8,128)(2,1)}, u32[]{:S(2)}, u32[]{:S(2)}) collective-permute-start(bf16[1024,1024]{1,0:T(8,128)(2,1)S(1)} %get-tuple-element.17.own), channel_id=1, source_target_pairs={{0,1},{1,0},{2,3},{3,2},{4,5},{5,4},{6,7},{7,6},{8,9},{9,8},{10,11... | collective-permute-start | bytes 6291464 | tf_op jit(solution)/shard_map/ppermute | solution.py:248
  38.3 13.2 %collective-permute-start.5 = (bf16[1024,256]{1,0:T(8,128)(2,1)S(1)}, bf16[1024,256]{1,0:T(8,128)(2,1)}, u32[]{:S(2)}, u32[]{:S(2)}) collective-permute-start(bf16[1024,256]{1,0:T(8,128)(2,1)S(1)} %get-tuple-element.20), channel_id=1, source_target_pairs={{0,2},{1,3},{2,0},{3,1},{4,6},{5,7},{6,4},{7,5},{8,10},{9,11},{10,... | collective-permute-start | bytes 1572872 | tf_op jit(solution)/shard_map/ppermute | solution.py:248
  38.4 24.4 %collective-permute-start.6 = (bf16[1024,256]{1,0:T(8,128)(2,1)S(1)}, bf16[1024,256]{1,0:T(8,128)(2,1)S(1)}, u32[]{:S(2)}, u32[]{:S(2)}) collective-permute-start(bf16[1024,256]{1,0:T(8,128)(2,1)S(1)} %get-tuple-element.21), channel_id=1, source_target_pairs={{0,2},{1,3},{2,0},{3,1},{4,6},{5,7},{6,4},{7,5},{8,10},{9,11},{10,... | collective-permute-start | bytes 1572872 | tf_op jit(solution)/shard_map/ppermute | solution.py:248
  39.9 34.2 %collective-permute-start.1 = (bf16[1024,256]{1,0:T(8,128)(2,1)S(1)}, bf16[1024,256]{1,0:T(8,128)(2,1)S(1)}, u32[]{:S(2)}, u32[]{:S(2)}) collective-permute-start(bf16[1024,256]{1,0:T(8,128)(2,1)S(1)} %get-tuple-element.18), channel_id=1, source_target_pairs={{0,2},{1,3},{2,0},{3,1},{4,6},{5,7},{6,4},{7,5},{8,10},{9,11},{10,... | collective-permute-start | bytes 1572872 | tf_op jit(solution)/shard_map/ppermute | solution.py:248
  39.9 45.3 %collective-permute-start.2 = (bf16[1024,256]{1,0:T(8,128)(2,1)S(1)}, bf16[1024,256]{1,0:T(8,128)(2,1)}, u32[]{:S(2)}, u32[]{:S(2)}) collective-permute-start(bf16[1024,256]{1,0:T(8,128)(2,1)S(1)} %get-tuple-element.19), channel_id=1, source_target_pairs={{0,2},{1,3},{2,0},{3,1},{4,6},{5,7},{6,4},{7,5},{8,10},{9,11},{10,... | collective-permute-start | bytes 1572872 | tf_op jit(solution)/shard_map/ppermute | solution.py:248
  51.6 35.0 %collective-permute-start.7 = (bf16[1024,256]{1,0:T(8,128)(2,1)}, bf16[1024,256]{1,0:T(8,128)(2,1)}, u32[]{:S(2)}, u32[]{:S(2)}) collective-permute-start(bf16[1024,256]{1,0:T(8,128)(2,1)} %collective-permute-done.5.refs_0_), channel_id=1, source_target_pairs={{0,4},{1,5},{4,8},{5,9},{8,12},{9,13},{6,2},{7,3},{10,6},{11,7},{1... | collective-permute-start | bytes 1572872 | tf_op jit(solution)/shard_map/ppermute | solution.py:248
  62.8 29.5 %copy-start.6 = (bf16[1024,256]{1,0:T(8,128)(2,1)}, bf16[1024,256]{1,0:T(8,128)(2,1)S(1)}, u32[]{:S(2)}) copy-start(bf16[1024,256]{1,0:T(8,128)(2,1)S(1)} %collective-permute-done.6.refs_1_) | copy-start | bytes 1572868
  62.8 23.8 %collective-permute-start.8 = (bf16[1024,256]{1,0:T(8,128)(2,1)S(1)}, bf16[1024,256]{1,0:T(8,128)(2,1)}, u32[]{:S(2)}, u32[]{:S(2)}) collective-permute-start(bf16[1024,256]{1,0:T(8,128)(2,1)S(1)} %collective-permute-done.6.refs_1_), channel_id=1, source_target_pairs={{0,4},{1,5},{4,8},{5,9},{8,12},{9,13},{6,2},{7,3},{10,6},{11,7},{1... | collective-permute-start | bytes 1572872 | tf_op jit(solution)/shard_map/ppermute | solution.py:248
  74.0 18.2 %copy-start.5 = (bf16[1024,256]{1,0:T(8,128)(2,1)}, bf16[1024,256]{1,0:T(8,128)(2,1)S(1)}, u32[]{:S(2)}) copy-start(bf16[1024,256]{1,0:T(8,128)(2,1)S(1)} %collective-permute-done.1.refs_0_) | copy-start | bytes 1572868
  74.0 16.1 %collective-permute-start.3 = (bf16[1024,256]{1,0:T(8,128)(2,1)S(1)}, bf16[1024,256]{1,0:T(8,128)(2,1)S(1)}, u32[]{:S(2)}, u32[]{:S(2)}) collective-permute-start(bf16[1024,256]{1,0:T(8,128)(2,1)S(1)} %collective-permute-done.1.refs_0_), channel_id=1, source_target_pairs={{0,4},{1,5},{4,8},{5,9},{8,12},{9,13},{6,2},{7,3},{10,6},{11,7},{1... | collective-permute-start | bytes 1572872 | tf_op jit(solution)/shard_map/ppermute | solution.py:248
  85.3 7.0 %collective-permute-start.10 = (bf16[1024,256]{1,0:T(8,128)(2,1)S(1)}, bf16[1024,256]{1,0:T(8,128)(2,1)S(1)}, u32[]{:S(2)}, u32[]{:S(2)}) collective-permute-start(bf16[1024,256]{1,0:T(8,128)(2,1)S(1)} %collective-permute-done.6.refs_1_), channel_id=1, source_target_pairs={{0,1},{1,0},{2,3},{3,2},{4,5},{5,4},{6,7},{7,6},{8,9},{9,8},{10,11... | collective-permute-start | bytes 1572872 | tf_op jit(solution)/shard_map/ppermute | solution.py:248
  86.6 7.9 %collective-permute-start.9 = (bf16[1024,256]{1,0:T(8,128)(2,1)}, bf16[1024,256]{1,0:T(8,128)(2,1)}, u32[]{:S(2)}, u32[]{:S(2)}) collective-permute-start(bf16[1024,256]{1,0:T(8,128)(2,1)} %collective-permute-done.5.refs_0_), channel_id=1, source_target_pairs={{0,1},{1,0},{2,3},{3,2},{4,5},{5,4},{6,7},{7,6},{8,9},{9,8},{10,11... | collective-permute-start | bytes 1572872 | tf_op jit(solution)/shard_map/ppermute | solution.py:248
  86.6 8.0 %collective-permute-start.11 = (bf16[1024,256]{1,0:T(8,128)(2,1)}, bf16[1024,256]{1,0:T(8,128)(2,1)}, u32[]{:S(2)}, u32[]{:S(2)}) collective-permute-start(bf16[1024,256]{1,0:T(8,128)(2,1)} %collective-permute-done.7.refs_2_), channel_id=1, source_target_pairs={{0,1},{1,0},{2,3},{3,2},{4,5},{5,4},{6,7},{7,6},{8,9},{9,8},{10,11... | collective-permute-start | bytes 1572872 | tf_op jit(solution)/shard_map/ppermute | solution.py:248
  90.1 14.6 %copy-start.4 = (bf16[1024,256]{1,0:T(8,128)(2,1)}, bf16[1024,256]{1,0:T(8,128)(2,1)S(1)}, u32[]{:S(2)}) copy-start(bf16[1024,256]{1,0:T(8,128)(2,1)S(1)} %collective-permute-done.3.refs_2_) | copy-start | bytes 1572868
  90.1 4.9 %collective-permute-start.12 = (bf16[1024,256]{1,0:T(8,128)(2,1)}, bf16[1024,256]{1,0:T(8,128)(2,1)}, u32[]{:S(2)}, u32[]{:S(2)}) collective-permute-start(bf16[1024,256]{1,0:T(8,128)(2,1)} %collective-permute-done.8.refs_3_), channel_id=1, source_target_pairs={{0,1},{1,0},{2,3},{3,2},{4,5},{5,4},{6,7},{7,6},{8,9},{9,8},{10,11... | collective-permute-start | bytes 1572872 | tf_op jit(solution)/shard_map/ppermute | solution.py:248
  92.3 0.8 copy-start.7
  93.1 15.6 %collective-permute-start.4 = (bf16[1024,256]{1,0:T(8,128)(2,1)}, bf16[1024,256]{1,0:T(8,128)(2,1)S(1)}, u32[]{:S(2)}, u32[]{:S(2)}) collective-permute-start(bf16[1024,256]{1,0:T(8,128)(2,1)} %collective-permute-done.2.refs_1_), channel_id=1, source_target_pairs={{0,4},{1,5},{4,8},{5,9},{8,12},{9,13},{6,2},{7,3},{10,6},{11,7},{1... | collective-permute-start | bytes 1572872 | tf_op jit(solution)/shard_map/ppermute | solution.py:248
  94.5 15.1 %collective-permute-start.13 = (bf16[1024,256]{1,0:T(8,128)(2,1)}, bf16[1024,256]{1,0:T(8,128)(2,1)S(1)}, u32[]{:S(2)}, u32[]{:S(2)}) collective-permute-start(bf16[1024,256]{1,0:T(8,128)(2,1)} %copy-done.5), channel_id=1, source_target_pairs={{0,1},{1,0},{2,3},{3,2},{4,5},{5,4},{6,7},{7,6},{8,9},{9,8},{10,11... | collective-permute-start | bytes 1572872 | tf_op jit(solution)/shard_map/ppermute | solution.py:248
  94.6 14.9 %collective-permute-start.14 = (bf16[1024,256]{1,0:T(8,128)(2,1)}, bf16[1024,256]{1,0:T(8,128)(2,1)S(1)}, u32[]{:S(2)}, u32[]{:S(2)}) collective-permute-start(bf16[1024,256]{1,0:T(8,128)(2,1)} %collective-permute-done.2.refs_1_), channel_id=1, source_target_pairs={{0,1},{1,0},{2,3},{3,2},{4,5},{5,4},{6,7},{7,6},{8,9},{9,8},{10,11... | collective-permute-start | bytes 1572872 | tf_op jit(solution)/shard_map/ppermute | solution.py:248
  95.0 14.5 %collective-permute-start.15 = (bf16[1024,256]{1,0:T(8,128)(2,1)S(1)}, bf16[1024,256]{1,0:T(8,128)(2,1)S(1)}, u32[]{:S(2)}, u32[]{:S(2)}) collective-permute-start(bf16[1024,256]{1,0:T(8,128)(2,1)S(1)} %collective-permute-done.3.refs_2_), channel_id=1, source_target_pairs={{0,1},{1,0},{2,3},{3,2},{4,5},{5,4},{6,7},{7,6},{8,9},{9,8},{10,11... | collective-permute-start | bytes 1572872 | tf_op jit(solution)/shard_map/ppermute | solution.py:248
  95.1 15.9 %slice-start = ((s8[10485760]{0:T(1024)(128)(4,1)}), s8[4194304]{0:T(1024)(128)(4,1)S(1)}, s32[]{:S(2)}) async-start(s8[10485760]{0:T(1024)(128)(4,1)} %bitcast.11), calls=%async_computation.1 | async-start | bytes 8388608
  95.1 15.9 %slice-start.1 = ((s8[10485760]{0:T(1024)(128)(4,1)}), s8[4194304]{0:T(1024)(128)(4,1)S(1)}, s32[]{:S(2)}) async-start(s8[10485760]{0:T(1024)(128)(4,1)} %bitcast.11), calls=%async_computation.2 | async-start | bytes 8388608
  95.1 15.9 %slice-start.2 = ((s8[10485760]{0:T(1024)(128)(4,1)}), s8[2097152]{0:T(1024)(128)(4,1)S(1)}, s32[]{:S(2)}) async-start(s8[10485760]{0:T(1024)(128)(4,1)} %bitcast.11), calls=%async_computation.3 | async-start | bytes 4194304
  108.7 2.4 %copy-start.2 = (bf16[1024,256]{1,0:T(8,128)(2,1)}, bf16[1024,256]{1,0:T(8,128)(2,1)S(1)}, u32[]{:S(2)}) copy-start(bf16[1024,256]{1,0:T(8,128)(2,1)S(1)} %gate.7.refs_3_) | copy-start | bytes 1572868
  108.7 2.4 %collective-permute-start.16 = (bf16[1024,256]{1,0:T(8,128)(2,1)S(1)}, bf16[1024,256]{1,0:T(8,128)(2,1)S(1)}, u32[]{:S(2)}, u32[]{:S(2)}) collective-permute-start(bf16[1024,256]{1,0:T(8,128)(2,1)S(1)} %gate.7.refs_3_), channel_id=1, source_target_pairs={{0,1},{1,0},{2,3},{3,2},{4,5},{5,4},{6,7},{7,6},{8,9},{9,8},{10,11... | collective-permute-start | bytes 1572872 | tf_op jit(solution)/shard_map/ppermute | solution.py:248

commit v5 on v4

--- a/solution.py
+++ b/solution.py
@@ -10,7 +10,6 @@
 HALO = 2
 PIECES = 1
 AHEAD = 3
-SIGN = 2
 LANES = 128
 RADIX = 32
 VMEM = pl.BlockSpec(memory_space=pltpu.VMEM)
@@ -160,13 +159,15 @@
 
 
 class Slots:
-    def __init__(self, flag, dense_ref, slots, matrix, window, mat_sems, sems):
+    def __init__(self, flag, dense_ref, slots, matrix, window, mat_sems, sems, first=0):
+        self.first = first
         self.flag, self.dense, self.slots = flag, dense_ref, slots
         self.matrix, self.window, self.mat_sems, self.sems = matrix, window, mat_sems, sems
 
     def block(self, slot):
         depth = self.dense.shape[0]
         if self.matrix is None:
+            slot += self.first
             return self.dense[:, slot * depth : (slot + 1) * depth]
         self.columns(slot).wait()
         return self.matrix[slot]
@@ -194,37 +195,56 @@
                 def _(value=value):
                     self.rows(slot, i, piece[value]).start()
 
-    def sum_into(self, total_ref):
-        for slot in range(AHEAD):
+    def sum_into(self, total_ref, prior=None):
+        last = len(self.slots) - 1
+        for slot in range(min(AHEAD, last + 1)):
             self.begin(slot)
-        last = len(self.slots) - 1
         for slot, pieces in enumerate(self.slots):
             for i, piece in enumerate(pieces):
                 self.rows(slot, i, piece[0] if isinstance(piece, tuple) else piece).wait()
             if slot + AHEAD <= last:
                 self.begin(slot + AHEAD)
             part = jnp.dot(self.block(slot), self.window[slot], preferred_element_type=jnp.float32)
-            if slot == 0:
+            if slot == 0 and prior is not None:
+                prior.wait()
+                total_ref[...] += part
+            elif slot == 0:
                 total_ref[...] = part
             elif slot < last:
                 total_ref[...] += part
         return total_ref[...] + part
 
 
-def flux_kernel(offset, count, paired, flag_ref, dense_ref, own, beside, *refs):
+def near_kernel(offset, dense_ref, own, beside, wait_ref, total_ref, token_ref, window, sems):
+    token_ref[...] = jnp.zeros_like(token_ref)
+    there = pl.ds(offset, total_ref.shape[1])
+    slots = [[own.at[:, there]], [beside.at[:, there]]]
+    total_ref[...] = Slots(0, dense_ref, slots, None, window, None, sems).sum_into(total_ref)
+
+
+def flux_kernel(offset, count, flag_ref, dense_ref, own, beside, *refs):
     out_ref, token_ref, matrix, window, total, result, mat_sems, sems, out_sem = refs[-9:]
     token_ref[...] = jnp.zeros_like(token_ref)
-    if offset:
-        matrix = None
     there = pl.ds(offset, total.shape[1])
     peers, passed = refs[:count], refs[count : 2 * count]
-    slots = [[own.at[:, there]], [beside.at[:, there]], peers, passed]
-    if paired:
-        slots.append(list(zip(refs[2 * count : 3 * count], refs[3 * count : 4 * count])))
-    else:
-        slots.append(refs[2 * count : 2 * count + count * PIECES])
+    pairs = list(zip(refs[2 * count : 3 * count], refs[3 * count : 4 * count]))
+    slots = [[own.at[:, there]], [beside.at[:, there]], peers, passed, pairs]
     parts = Slots(flag_ref[0], dense_ref, slots, matrix, window, mat_sems, sems).sum_into(total)
     result[...] = parts.astype(jnp.bfloat16)
+    out = pltpu.make_async_copy(result, out_ref.at[:, there], out_sem)
+    out.start()
+    out.wait()
+
+
+def far_kernel(offset, count, flag_ref, dense_ref, prior_ref, *refs):
+    out_ref, window, total, result, sems, prior_sem, out_sem = refs[-7:]
+    there = pl.ds(offset, total.shape[1])
+    prior = pltpu.make_async_copy(prior_ref, total, prior_sem)
+    peers, passed = refs[:count], refs[count : 2 * count]
+    pairs = list(zip(refs[2 * count : 3 * count], refs[3 * count : 4 * count]))
+    slots = Slots(flag_ref[0], dense_ref, [peers, passed, pairs], None, window, None, sems, first=2)
+    prior.start()
+    result[...] = slots.sum_into(total, prior).astype(jnp.bfloat16)
     out = pltpu.make_async_copy(result, out_ref.at[:, there], out_sem)
     out.start()
     out.wait()
@@ -241,8 +261,7 @@
     core, side = me % 2, (me // 2) % 2
     across = [(i, i ^ 2) for i in range(devices)]
     partner = [(i, i ^ 1) for i in range(devices)]
-    relay = [(i, i + 4) for i in range(devices - 4) if not i & 2]
-    relay += [(i + 4, i) for i in range(devices - 4) if i & 2]
+    relay = [(i, (i - 4 if i & 2 else i + 4) % devices) for i in range(devices)]
 
     def send(value, pairs):
         return lax.ppermute(value, "row", pairs)
@@ -316,50 +335,69 @@
     half = 2
     out_type = pltpu.HBM((seg_dev, width), jnp.bfloat16)
 
-    def flux(chunks, others, out, after=()):
-        given = [dense, whole, beside] + peers[chunks] + passed[chunks] + others + out
-        wide, many = sum(sizes[chunks]), len(sizes[chunks])
-        start = starts[chunks][0]
-        loose = [item for item in others if start]
-        return pl.pallas_call(
-            functools.partial(flux_kernel, start, many, True),
-            out_shape=(out_type, TOKEN),
-            in_specs=[SMEM]
-            + [VMEM if start and item is dense else ANY if any(item is other for other in loose) else HBM for item in given]
-            + [ANY] * len(after),
-            out_specs=(HBM, VMEM),
-            scratch_shapes=[
-                pltpu.VMEM((1, 8, LANES) if start else (SLOTS, seg_dev, seg_dev), jnp.bfloat16),
-                pltpu.VMEM((SLOTS, seg_dev, wide), jnp.bfloat16),
-                pltpu.VMEM((seg_dev, wide), jnp.float32),
-                pltpu.VMEM((seg_dev, wide), jnp.bfloat16),
-                pltpu.SemaphoreType.DMA((SLOTS,)),
-                pltpu.SemaphoreType.DMA((SLOTS, many)),
-                pltpu.SemaphoreType.DMA,
-            ],
-            input_output_aliases={len(given): 0} if out else {},
-            compiler_params=limit(20 if start else 36),
-            cost_estimate=cost(),
-            name="flux",
-        )(
-            flag,
-            *[item if any(item is other for other in loose + [dense] * (start > 0)) else in_hbm(item) for item in given],
-            *after,
-        )
-
     across_beside = [send(peer, partner) for peer in peers]
     passed_beside = [send(item, partner) for item in passed[:-1]]
-    sign = passed[SIGN][:16, :LANES]
+    sign = passed[half][:16, :LANES]
     for _ in range(3):
         sign = gate(sign, flag)
-    after = [sign]
-    others = across_beside[:half] + passed_beside[:half]
-    out, token = flux(slice(0, half), others, [], after)
+
+    wide = sum(sizes[:half])
+    given = [dense, whole, beside] + peers[:half] + passed[:half]
+    given += across_beside[:half] + passed_beside[:half]
+    out, token = pl.pallas_call(
+        functools.partial(flux_kernel, 0, half),
+        out_shape=(out_type, TOKEN),
+        in_specs=[SMEM] + [HBM] * len(given) + [ANY],
+        out_specs=(HBM, VMEM),
+        scratch_shapes=[
+            pltpu.VMEM((SLOTS, seg_dev, seg_dev), jnp.bfloat16),
+            pltpu.VMEM((SLOTS, seg_dev, wide), jnp.bfloat16),
+            pltpu.VMEM((seg_dev, wide), jnp.float32),
+            pltpu.VMEM((seg_dev, wide), jnp.bfloat16),
+            pltpu.SemaphoreType.DMA((SLOTS,)),
+            pltpu.SemaphoreType.DMA((SLOTS, half)),
+            pltpu.SemaphoreType.DMA,
+        ],
+        compiler_params=limit(36),
+        cost_estimate=cost(),
+        name="flux",
+    )(flag, *[in_hbm(item) for item in given], sign)
+
+    rest, left = width - wide, len(sizes) - half
+    sums, token = pl.pallas_call(
+        functools.partial(near_kernel, wide),
+        out_shape=(jax.ShapeDtypeStruct((seg_dev, rest), jnp.float32), TOKEN),
+        in_specs=[VMEM, HBM, HBM, ANY],
+        out_specs=(VMEM, VMEM),
+        scratch_shapes=[
+            pltpu.VMEM((2, seg_dev, rest), jnp.bfloat16),
+            pltpu.SemaphoreType.DMA((2, 1)),
+        ],
+        compiler_params=limit(16),
+        cost_estimate=cost(),
+        name="near_flux",
+    )(dense, in_hbm(whole), in_hbm(beside), token)
     passed[-1] = gate(passed[-1], token)
     passed_beside.append(send(passed[-1], partner))
-    others = across_beside[half:] + passed_beside[half:]
-    out, _ = flux(slice(half, len(sizes)), others, [out])
-    return out
+    given = peers[half:] + passed[half:] + across_beside[half:] + passed_beside[half:]
+    return pl.pallas_call(
+        functools.partial(far_kernel, wide, left),
+        out_shape=out_type,
+        in_specs=[SMEM, VMEM] + [ANY] * (1 + len(given)) + [HBM],
+        out_specs=HBM,
+        scratch_shapes=[
+            pltpu.VMEM((3, seg_dev, rest), jnp.bfloat16),
+            pltpu.VMEM((seg_dev, rest), jnp.float32),
+            pltpu.VMEM((seg_dev, rest), jnp.bfloat16),
+            pltpu.SemaphoreType.DMA((3, left)),
+            pltpu.SemaphoreType.DMA,
+            pltpu.SemaphoreType.DMA,
+        ],
+        input_output_aliases={3 + len(given): 0},
+        compiler_params=limit(16),
+        cost_estimate=cost(),
+        name="far_flux",
+    )(flag, dense, sums, *given, in_hbm(out))
 
 
 def solution(mesh):

time: 122 us -> 120 us (0.984)
  waiting for transfers between devices: 63.4 us -> 49 us
  starting transfers between devices: 20.3 us -> 31.5 us
  Pallas kernels: 33.9 us -> 36.1 us
    ppermute x17, waiting for transfers between devices: 48.6 us -> 34.1 us  [send(): return lax.ppermute(value, 'row', pairs)]
    ppermute x17, starting transfers between devices: 13.6 us -> 24.8 us  [send(): return lax.ppermute(value, 'row', pairs)]
    pallas_call x1, Pallas kernels: 1.38 us -> 2.73 us  [shards(): pl.pallas_call(inject_kernel, out_shape=[jax.ShapeDtypeStruct((seg_dev, w...]
    pallas_call x2 -> x3, Pallas kernels: 18.9 us -> 19.7 us  [the longest x1 9.58 us: shards(): pl.pallas_call(functools.partial(flux_kernel, 0, half), out_shape=(out_ty...]
  transfers between devices with their start and end apart: 18 -> 18, of which waited for: 8 -> 7; matrix products, arithmetic and copies ran while one was open for 0% -> 0% of each run, Pallas kernels for 17% -> 20%
where the time goes in v5:
time: 120 us; the launch traced here: 119 us
  waiting for transfers between devices  49 us (41%)
  Pallas kernels  36.1 us (30%)
  starting transfers between devices  31.5 us (26%)
  local copies, waits for them, and re-layouts  2.5 us (2%)
    ppermute x17, waiting for transfers between devices, send(): return lax.ppermute(value, 'row', pairs)  34.1 us
    ppermute x17, starting transfers between devices, send(): return lax.ppermute(value, 'row', pairs)  24.8 us
    all_to_all x1, waiting for transfers between devices, shards(): lax.all_to_all(outgoing.reshape(devices, capacity, width + LANES), 'row',...  14.8 us
    pallas_call x1, Pallas kernels, shards(): pl.pallas_call(dense_kernel, out_shape=(pltpu.HBM((seg_dev, SLOTS * seg_d...  11 us
    pallas_call x1, Pallas kernels, shards(): pl.pallas_call(functools.partial(flux_kernel, 0, half), out_shape=(out_ty...  9.58 us
    all_to_all x1, starting transfers between devices, shards(): lax.all_to_all(outgoing.reshape(devices, capacity, width + LANES), 'row',...  6.68 us
    pallas_call x1, Pallas kernels, shards(): pl.pallas_call(functools.partial(far_kernel, wide, left), out_shape=out_t...  6.42 us
    pallas_call x1, Pallas kernels, shards(): pl.pallas_call(functools.partial(near_kernel, wide), out_shape=(jax.Shape...  3.67 us
  transfers between devices with their start and end apart: 18, of which 7 were waited for; matrix products, arithmetic and copies ran while one was open for 0% of the time, Pallas kernels for 20%

profile of v5, /device:TPU:7, one launch (start us, length us, event | category | flops | bytes accessed | tf_op | source)
XLA Modules:
  0.0 119.2 jit_solution(10883271203861378744)
XLA Ops:
  0.0 0.0 copy-start.3
  0.0 2.6 %pack_terms.1.wait_ref = bf16[512,1152]{1,0:T(8,128)(2,1)} custom-call(s32[1,256]{1,0:T(1,128)} %bitcast.14, s32[1,256]{1,0:T(1,128)} %bitcast.15, bf16[256,1024]{1,0:T(8,128)(2,1)} %rows_hbm.1), custom_call_target="tpu_custom_call" | custom-call | tf_op jit(solution)/shard_map/pack_terms/pallas_call | solution.py:283
  2.6 6.7 %all-to-all-start = ((bf16[16,32,1152]{2,1,0:T(8,128)(2,1)}), bf16[16,32,1152]{2,1,0:T(8,128)(2,1)S(1)}, u32[]{:S(2)}, u32[]{:S(2)}) async-start(bf16[16,32,1152]{2,1,0:T(8,128)(2,1)} %bitcast.9), calls=%async_computation | async-start | bytes 2359296 | tf_op jit(solution)/shard_map/all_to_all | solution.py:297
  9.3 0.1 stack.35.slot_ref
  9.4 0.0 copy-done.3
  9.4 11.0 %dense_blocks.1 = (bf16[1024,5120]{1,0:T(8,128)(2,1)}, f32[8,128]{1,0:T(8,128)S(1)}) custom-call(s32[4,20]{1,0:T(4,128)S(1)} %copy-done.3, s32[6]{0:T(128)S(1)} %stack.35.slot_ref, bf16[4,20,256,256]{3,2,1,0:T(8,128)(2,1)} %blocks_ref.1, bf16[512,1152]{1,0:T(8,128)(2,1)} %pack_terms.1.wait_ref), custom_call_target="tpu_custom_call" | custom-call | tf_op jit(solution)/shard_map/dense_blocks/pallas_call | solution.py:301
  20.4 14.8 %all-to-all-done = bf16[16,32,1152]{2,1,0:T(8,128)(2,1)S(1)} async-done(((bf16[16,32,1152]{2,1,0:T(8,128)(2,1)}), bf16[16,32,1152]{2,1,0:T(8,128)(2,1)S(1)}, u32[]{:S(2)}, u32[]{:S(2)}) %all-to-all-start) | async-done | bytes 1179680 | tf_op jit(solution)/shard_map/all_to_all | solution.py:297
  35.3 0.0 copy-start
  35.3 1.6 %copy-done = bf16[1024,1024]{1,0:T(8,128)(2,1)S(1)} copy-done((bf16[1024,1024]{1,0:T(8,128)(2,1)S(1)}, bf16[1024,1024]{1,0:T(8,128)(2,1)}, u32[]{:S(2)}) %copy-start) | copy-done | bytes 2097176
  36.9 0.0 slice-start
  36.9 2.7 %inject_terms.1 = (bf16[1024,1024]{1,0:T(8,128)(2,1)}, bf16[1024,256]{1,0:T(8,128)(2,1)S(1)}, bf16[1024,256]{1,0:T(8,128)(2,1)S(1)}, bf16[1024,256]{1,0:T(8,128)(2,1)S(1)}, bf16[1024,256]{1,0:T(8,128)(2,1)S(1)}) custom-call(bf16[1024,1024]{1,0:T(8,128)(2,1)S(1)} %copy-done, bf16[512,1152]{1,0:T(8,128)(2,1)S(1)} %bitcast.13, ...), custom_call_target="tpu_custom_call" | custom-call | tf_op jit(solution)/shard_map/inject_terms/pallas_call | solution.py:316
  39.6 0.0 collective-permute-start
  39.6 0.0 collective-permute-start.1
  39.6 1.5 %collective-permute-start.2 = (bf16[1024,256]{1,0:T(8,128)(2,1)S(1)}, bf16[1024,256]{1,0:T(8,128)(2,1)}, u32[]{:S(2)}, u32[]{:S(2)}) collective-permute-start(bf16[1024,256]{1,0:T(8,128)(2,1)S(1)} %get-tuple-element.20), channel_id=1, source_target_pairs={{0,2},{1,3},{2,0},{3,1},{4,6},{5,7},{6,4},{7,5},{8,10},{9,11},{10,... | collective-permute-start | bytes 1572872 | tf_op jit(solution)/shard_map/ppermute | solution.py:267
  41.1 0.0 collective-permute-start.9
  41.1 1.4 %collective-permute-start.11 = (bf16[1024,256]{1,0:T(8,128)(2,1)S(1)}, bf16[1024,256]{1,0:T(8,128)(2,1)}, u32[]{:S(2)}, u32[]{:S(2)}) collective-permute-start(bf16[1024,256]{1,0:T(8,128)(2,1)S(1)} %get-tuple-element.24), channel_id=1, source_target_pairs={{0,2},{1,3},{2,0},{3,1},{4,6},{5,7},{6,4},{7,5},{8,10},{9,11},{10,... | collective-permute-start | bytes 1572872 | tf_op jit(solution)/shard_map/ppermute | solution.py:267
  42.5 10.0 %collective-permute-done.1.refs_0_ = bf16[1024,256]{1,0:T(8,128)(2,1)S(1)} collective-permute-done((bf16[1024,256]{1,0:T(8,128)(2,1)S(1)}, bf16[1024,256]{1,0:T(8,128)(2,1)S(1)}, u32[]{:S(2)}, u32[]{:S(2)}) %collective-permute-start.1) | collective-permute-done | bytes 524320 | tf_op jit(solution)/shard_map/ppermute | solution.py:267
  52.6 0.0 copy-start.4
  52.6 4.2 %collective-permute-start.3 = (bf16[1024,256]{1,0:T(8,128)(2,1)S(1)}, bf16[1024,256]{1,0:T(8,128)(2,1)}, u32[]{:S(2)}, u32[]{:S(2)}) collective-permute-start(bf16[1024,256]{1,0:T(8,128)(2,1)S(1)} %collective-permute-done.1.refs_0_), channel_id=1, source_target_pairs={{0,4},{1,5},{2,14},{3,15},{4,8},{5,9},{6,2},{7,3},{8,12},{9,13},{1... | collective-permute-start | bytes 1572872 | tf_op jit(solution)/shard_map/ppermute | solution.py:267
  56.8 7.1 %collective-permute-done.2.refs_1_ = bf16[1024,256]{1,0:T(8,128)(2,1)} collective-permute-done((bf16[1024,256]{1,0:T(8,128)(2,1)S(1)}, bf16[1024,256]{1,0:T(8,128)(2,1)}, u32[]{:S(2)}, u32[]{:S(2)}) %collective-permute-start.2) | collective-permute-done | bytes 524320 | tf_op jit(solution)/shard_map/ppermute | solution.py:267
  63.9 4.2 %collective-permute-start.4 = (bf16[1024,256]{1,0:T(8,128)(2,1)}, bf16[1024,256]{1,0:T(8,128)(2,1)}, u32[]{:S(2)}, u32[]{:S(2)}) collective-permute-start(bf16[1024,256]{1,0:T(8,128)(2,1)} %collective-permute-done.2.refs_1_), channel_id=1, source_target_pairs={{0,4},{1,5},{2,14},{3,15},{4,8},{5,9},{6,2},{7,3},{8,12},{9,13},{1... | collective-permute-start | bytes 1572872 | tf_op jit(solution)/shard_map/ppermute | solution.py:267
  68.1 7.0 %collective-permute-done.9.refs_0_ = bf16[1024,256]{1,0:T(8,128)(2,1)S(1)} collective-permute-done((bf16[1024,256]{1,0:T(8,128)(2,1)S(1)}, bf16[1024,256]{1,0:T(8,128)(2,1)S(1)}, u32[]{:S(2)}, u32[]{:S(2)}) %collective-permute-start.9) | collective-permute-done | bytes 524320 | tf_op jit(solution)/shard_map/ppermute | solution.py:267
  75.1 0.0 copy-start.1
  75.1 4.2 %collective-permute-start.10 = (bf16[1024,256]{1,0:T(8,128)(2,1)S(1)}, bf16[1024,256]{1,0:T(8,128)(2,1)S(1)}, u32[]{:S(2)}, u32[]{:S(2)}) collective-permute-start(bf16[1024,256]{1,0:T(8,128)(2,1)S(1)} %collective-permute-done.9.refs_0_), channel_id=1, source_target_pairs={{0,4},{1,5},{2,14},{3,15},{4,8},{5,9},{6,2},{7,3},{8,12},{9,13},{1... | collective-permute-start | bytes 1572872 | tf_op jit(solution)/shard_map/ppermute | solution.py:267
  79.4 7.0 %collective-permute-done.11.refs_1_ = bf16[1024,256]{1,0:T(8,128)(2,1)} collective-permute-done((bf16[1024,256]{1,0:T(8,128)(2,1)S(1)}, bf16[1024,256]{1,0:T(8,128)(2,1)}, u32[]{:S(2)}, u32[]{:S(2)}) %collective-permute-start.11) | collective-permute-done | bytes 524320 | tf_op jit(solution)/shard_map/ppermute | solution.py:267
  86.4 1.4 %collective-permute-start.5 = (bf16[1024,256]{1,0:T(8,128)(2,1)S(1)}, bf16[1024,256]{1,0:T(8,128)(2,1)S(1)}, u32[]{:S(2)}, u32[]{:S(2)}) collective-permute-start(bf16[1024,256]{1,0:T(8,128)(2,1)S(1)} %collective-permute-done.1.refs_0_), channel_id=1, source_target_pairs={{0,1},{1,0},{2,3},{3,2},{4,5},{5,4},{6,7},{7,6},{8,9},{9,8},{10,11... | collective-permute-start | bytes 1572872 | tf_op jit(solution)/shard_map/ppermute | solution.py:267
  87.7 0.0 collective-permute-done.3.refs_2_
  87.7 0.0 collective-permute-start.6
  87.8 0.0 collective-permute-done.4.refs_3_
  87.8 0.5 collective-permute-start.7
  88.3 1.2 %collective-permute-done.10.refs_2_ = bf16[1024,256]{1,0:T(8,128)(2,1)S(1)} collective-permute-done((bf16[1024,256]{1,0:T(8,128)(2,1)S(1)}, bf16[1024,256]{1,0:T(8,128)(2,1)S(1)}, u32[]{:S(2)}, u32[]{:S(2)}) %collective-permute-start.10) | collective-permute-done | bytes 524320 | tf_op jit(solution)/shard_map/ppermute | solution.py:267
  89.5 2.2 %collective-permute-start.8 = (bf16[1024,256]{1,0:T(8,128)(2,1)}, bf16[1024,256]{1,0:T(8,128)(2,1)}, u32[]{:S(2)}, u32[]{:S(2)}) collective-permute-start(bf16[1024,256]{1,0:T(8,128)(2,1)} %collective-permute-done.4.refs_3_), channel_id=1, source_target_pairs={{0,1},{1,0},{2,3},{3,2},{4,5},{5,4},{6,7},{7,6},{8,9},{9,8},{10,11... | collective-permute-start | bytes 1572872 | tf_op jit(solution)/shard_map/ppermute | solution.py:267
  91.7 0.0 copy-done.1
  91.7 0.0 collective-permute-done.5.refs_4_
  91.7 0.0 copy-done.4
  91.7 0.0 copy-start.5
  91.7 0.8 copy-done.5
  92.5 4.0 %collective-permute-start.12 = (bf16[1024,256]{1,0:T(8,128)(2,1)}, bf16[1024,256]{1,0:T(8,128)(2,1)S(1)}, u32[]{:S(2)}, u32[]{:S(2)}) collective-permute-start(bf16[1024,256]{1,0:T(8,128)(2,1)} %collective-permute-done.11.refs_1_), channel_id=1, source_target_pairs={{0,4},{1,5},{2,14},{3,15},{4,8},{5,9},{6,2},{7,3},{8,12},{9,13},{1... | collective-permute-start | bytes 1572872 | tf_op jit(solution)/shard_map/ppermute | solution.py:267
  96.5 0.1 add_convert_fusion.refs_1_.flag_ref
  96.6 0.0 collective-permute-done.6.refs_5_
  96.6 0.4 collective-permute-start.13
  97.0 0.0 collective-permute-done.7.refs_6_
  97.0 0.2 collective-permute-start.14
  97.2 0.0 collective-permute-done.8.refs_7_
  97.2 0.3 collective-permute-start.15
  97.5 0.0 collective-permute-done.beside
  97.5 0.0 slice-start.1
  97.5 0.0 slice-start.2
  97.5 9.6 %flux.1 = (bf16[1024,1024]{1,0:T(8,128)(2,1)}, f32[8,128]{1,0:T(8,128)S(1)}) custom-call(s32[2]{0:T(128)S(1)} %add_convert_fusion.refs_1_.flag_ref, bf16[1024,5120]{1,0:T(8,128)(2,1)} %get-tuple-element.16.dense_ref, bf16[1024,1024]{1,0:T(8,128)(2,1)} %get-tuple-element.18.own, bf16[1024,1024]{1,0:T(8,128)(2,1)} %collective-permute-done.beside, ...), custom_call_target="tpu_custom_call" | custom-call | tf_op jit(solution)/shard_map/flux/pallas_call | solution.py:347
  107.1 0.0 slice-done
  107.1 0.0 slice-done.1
  107.1 0.0 slice-done.2
  107.1 0.0 copy-start.2
  107.1 3.7 %near_flux.1 = (f32[1024,512]{1,0:T(8,128)S(1)}, f32[8,128]{1,0:T(8,128)S(1)}) custom-call(bf16[1024,5120]{1,0:T(8,128)(2,1)S(1)} %bitcast.12, bf16[1024,1024]{1,0:T(8,128)(2,1)} %get-tuple-element.18.own, bf16[1024,1024]{1,0:T(8,128)(2,1)} %collective-permute-done.beside, f32[8,128]{1,0:T(8,128)S(1)} %get-tuple-element.22.wait_ref), custom_call_target="tpu_custom_call" | custom-call | tf_op jit(solution)/shard_map/near_flux/pallas_call | solution.py:367
  110.8 0.0 collective-permute-done.12.refs_0_
  110.8 0.3 collective-permute-start.16
  111.1 0.0 collective-permute-done.13.refs_4_
  111.1 0.0 collective-permute-done.14.refs_5_
  111.1 0.0 collective-permute-done.15.refs_6_
  111.1 1.7 %collective-permute-done.16.refs_7_ = bf16[1024,256]{1,0:T(8,128)(2,1)S(1)} collective-permute-done((bf16[1024,256]{1,0:T(8,128)(2,1)S(1)}, bf16[1024,256]{1,0:T(8,128)(2,1)S(1)}, u32[]{:S(2)}, u32[]{:S(2)}) %collective-permute-start.16) | collective-permute-done | bytes 524320 | tf_op jit(solution)/shard_map/ppermute | solution.py:267
  112.8 0.0 copy-done.2
  112.8 6.4 %far_flux.1 = bf16[1024,1024]{1,0:T(8,128)(2,1)} custom-call(s32[2]{0:T(128)S(1)} %add_convert_fusion.refs_1_.flag_ref, bf16[1024,5120]{1,0:T(8,128)(2,1)S(1)} %bitcast.12, f32[1024,512]{1,0:T(8,128)S(1)} %get-tuple-element.23.prior_ref, bf16[1024,256]{1,0:T(8,128)(2,1)S(1)} %copy-done.2, ...), custom_call_target="tpu_custom_call", output_to_operand_aliasing={{}: (11, {})} | custom-call | tf_op jit(solution)/shard_map/far_flux/pallas_call | solution.py:383
  (6 shorter events, 0.0 us)
Async XLA Ops:
  0.0 9.4 %copy-start.3 = (s32[4,20]{1,0:T(4,128)S(1)}, s32[4,20]{1,0:T(4,128)}, u32[]{:S(2)}) copy-start(s32[4,20]{1,0:T(4,128)} %cols_ref.1) | copy-start | bytes 964
  2.6 32.6 %all-to-all-start = ((bf16[16,32,1152]{2,1,0:T(8,128)(2,1)}), bf16[16,32,1152]{2,1,0:T(8,128)(2,1)S(1)}, u32[]{:S(2)}, u32[]{:S(2)}) async-start(bf16[16,32,1152]{2,1,0:T(8,128)(2,1)} %bitcast.9), calls=%async_computation | async-start | bytes 2359296 | tf_op jit(solution)/shard_map/all_to_all | solution.py:297
  35.3 1.6 %copy-start = (bf16[1024,1024]{1,0:T(8,128)(2,1)S(1)}, bf16[1024,1024]{1,0:T(8,128)(2,1)}, u32[]{:S(2)}) copy-start(bf16[1024,1024]{1,0:T(8,128)(2,1)} %base_ref.1) | copy-start | bytes 6291460
  36.9 70.2 %slice-start = ((s8[10485760]{0:T(1024)(128)(4,1)}), s8[2097152]{0:T(1024)(128)(4,1)S(1)}, s32[]{:S(2)}) async-start(s8[10485760]{0:T(1024)(128)(4,1)} %bitcast.11), calls=%async_computation.1 | async-start | bytes 4194304
  39.6 57.9 %collective-permute-start = (bf16[1024,1024]{1,0:T(8,128)(2,1)}, bf16[1024,1024]{1,0:T(8,128)(2,1)}, u32[]{:S(2)}, u32[]{:S(2)}) collective-permute-start(bf16[1024,1024]{1,0:T(8,128)(2,1)} %get-tuple-element.18.own), channel_id=1, source_target_pairs={{0,1},{1,0},{2,3},{3,2},{4,5},{5,4},{6,7},{7,6},{8,9},{9,8},{10,11... | collective-permute-start | bytes 6291464 | tf_op jit(solution)/shard_map/ppermute | solution.py:267
  39.6 13.0 %collective-permute-start.1 = (bf16[1024,256]{1,0:T(8,128)(2,1)S(1)}, bf16[1024,256]{1,0:T(8,128)(2,1)S(1)}, u32[]{:S(2)}, u32[]{:S(2)}) collective-permute-start(bf16[1024,256]{1,0:T(8,128)(2,1)S(1)} %get-tuple-element.19), channel_id=1, source_target_pairs={{0,2},{1,3},{2,0},{3,1},{4,6},{5,7},{6,4},{7,5},{8,10},{9,11},{10,... | collective-permute-start | bytes 1572872 | tf_op jit(solution)/shard_map/ppermute | solution.py:267
  39.6 24.3 %collective-permute-start.2 = (bf16[1024,256]{1,0:T(8,128)(2,1)S(1)}, bf16[1024,256]{1,0:T(8,128)(2,1)}, u32[]{:S(2)}, u32[]{:S(2)}) collective-permute-start(bf16[1024,256]{1,0:T(8,128)(2,1)S(1)} %get-tuple-element.20), channel_id=1, source_target_pairs={{0,2},{1,3},{2,0},{3,1},{4,6},{5,7},{6,4},{7,5},{8,10},{9,11},{10,... | collective-permute-start | bytes 1572872 | tf_op jit(solution)/shard_map/ppermute | solution.py:267
  41.1 34.1 %collective-permute-start.9 = (bf16[1024,256]{1,0:T(8,128)(2,1)S(1)}, bf16[1024,256]{1,0:T(8,128)(2,1)S(1)}, u32[]{:S(2)}, u32[]{:S(2)}) collective-permute-start(bf16[1024,256]{1,0:T(8,128)(2,1)S(1)} %get-tuple-element.21), channel_id=1, source_target_pairs={{0,2},{1,3},{2,0},{3,1},{4,6},{5,7},{6,4},{7,5},{8,10},{9,11},{10,... | collective-permute-start | bytes 1572872 | tf_op jit(solution)/shard_map/ppermute | solution.py:267
  41.1 45.3 %collective-permute-start.11 = (bf16[1024,256]{1,0:T(8,128)(2,1)S(1)}, bf16[1024,256]{1,0:T(8,128)(2,1)}, u32[]{:S(2)}, u32[]{:S(2)}) collective-permute-start(bf16[1024,256]{1,0:T(8,128)(2,1)S(1)} %get-tuple-element.24), channel_id=1, source_target_pairs={{0,2},{1,3},{2,0},{3,1},{4,6},{5,7},{6,4},{7,5},{8,10},{9,11},{10,... | collective-permute-start | bytes 1572872 | tf_op jit(solution)/shard_map/ppermute | solution.py:267
  52.6 39.2 %copy-start.4 = (bf16[1024,256]{1,0:T(8,128)(2,1)}, bf16[1024,256]{1,0:T(8,128)(2,1)S(1)}, u32[]{:S(2)}) copy-start(bf16[1024,256]{1,0:T(8,128)(2,1)S(1)} %collective-permute-done.1.refs_0_) | copy-start | bytes 1572868
  52.6 35.2 %collective-permute-start.3 = (bf16[1024,256]{1,0:T(8,128)(2,1)S(1)}, bf16[1024,256]{1,0:T(8,128)(2,1)}, u32[]{:S(2)}, u32[]{:S(2)}) collective-permute-start(bf16[1024,256]{1,0:T(8,128)(2,1)S(1)} %collective-permute-done.1.refs_0_), channel_id=1, source_target_pairs={{0,4},{1,5},{2,14},{3,15},{4,8},{5,9},{6,2},{7,3},{8,12},{9,13},{1... | collective-permute-start | bytes 1572872 | tf_op jit(solution)/shard_map/ppermute | solution.py:267
  63.9 23.8 %collective-permute-start.4 = (bf16[1024,256]{1,0:T(8,128)(2,1)}, bf16[1024,256]{1,0:T(8,128)(2,1)}, u32[]{:S(2)}, u32[]{:S(2)}) collective-permute-start(bf16[1024,256]{1,0:T(8,128)(2,1)} %collective-permute-done.2.refs_1_), channel_id=1, source_target_pairs={{0,4},{1,5},{2,14},{3,15},{4,8},{5,9},{6,2},{7,3},{8,12},{9,13},{1... | collective-permute-start | bytes 1572872 | tf_op jit(solution)/shard_map/ppermute | solution.py:267
  75.1 16.6 %copy-start.1 = (bf16[1024,256]{1,0:T(8,128)(2,1)}, bf16[1024,256]{1,0:T(8,128)(2,1)S(1)}, u32[]{:S(2)}) copy-start(bf16[1024,256]{1,0:T(8,128)(2,1)S(1)} %collective-permute-done.9.refs_0_) | copy-start | bytes 1572868
  75.1 14.3 %collective-permute-start.10 = (bf16[1024,256]{1,0:T(8,128)(2,1)S(1)}, bf16[1024,256]{1,0:T(8,128)(2,1)S(1)}, u32[]{:S(2)}, u32[]{:S(2)}) collective-permute-start(bf16[1024,256]{1,0:T(8,128)(2,1)S(1)} %collective-permute-done.9.refs_0_), channel_id=1, source_target_pairs={{0,4},{1,5},{2,14},{3,15},{4,8},{5,9},{6,2},{7,3},{8,12},{9,13},{1... | collective-permute-start | bytes 1572872 | tf_op jit(solution)/shard_map/ppermute | solution.py:267
  86.4 5.3 %collective-permute-start.5 = (bf16[1024,256]{1,0:T(8,128)(2,1)S(1)}, bf16[1024,256]{1,0:T(8,128)(2,1)S(1)}, u32[]{:S(2)}, u32[]{:S(2)}) collective-permute-start(bf16[1024,256]{1,0:T(8,128)(2,1)S(1)} %collective-permute-done.1.refs_0_), channel_id=1, source_target_pairs={{0,1},{1,0},{2,3},{3,2},{4,5},{5,4},{6,7},{7,6},{8,9},{9,8},{10,11... | collective-permute-start | bytes 1572872 | tf_op jit(solution)/shard_map/ppermute | solution.py:267
  87.7 8.9 %collective-permute-start.6 = (bf16[1024,256]{1,0:T(8,128)(2,1)}, bf16[1024,256]{1,0:T(8,128)(2,1)}, u32[]{:S(2)}, u32[]{:S(2)}) collective-permute-start(bf16[1024,256]{1,0:T(8,128)(2,1)} %collective-permute-done.2.refs_1_), channel_id=1, source_target_pairs={{0,1},{1,0},{2,3},{3,2},{4,5},{5,4},{6,7},{7,6},{8,9},{9,8},{10,11... | collective-permute-start | bytes 1572872 | tf_op jit(solution)/shard_map/ppermute | solution.py:267
  87.8 9.2 %collective-permute-start.7 = (bf16[1024,256]{1,0:T(8,128)(2,1)}, bf16[1024,256]{1,0:T(8,128)(2,1)}, u32[]{:S(2)}, u32[]{:S(2)}) collective-permute-start(bf16[1024,256]{1,0:T(8,128)(2,1)} %collective-permute-done.3.refs_2_), channel_id=1, source_target_pairs={{0,1},{1,0},{2,3},{3,2},{4,5},{5,4},{6,7},{7,6},{8,9},{9,8},{10,11... | collective-permute-start | bytes 1572872 | tf_op jit(solution)/shard_map/ppermute | solution.py:267
  89.5 7.7 %collective-permute-start.8 = (bf16[1024,256]{1,0:T(8,128)(2,1)}, bf16[1024,256]{1,0:T(8,128)(2,1)}, u32[]{:S(2)}, u32[]{:S(2)}) collective-permute-start(bf16[1024,256]{1,0:T(8,128)(2,1)} %collective-permute-done.4.refs_3_), channel_id=1, source_target_pairs={{0,1},{1,0},{2,3},{3,2},{4,5},{5,4},{6,7},{7,6},{8,9},{9,8},{10,11... | collective-permute-start | bytes 1572872 | tf_op jit(solution)/shard_map/ppermute | solution.py:267
  91.7 0.8 copy-start.5
  92.5 18.3 %collective-permute-start.12 = (bf16[1024,256]{1,0:T(8,128)(2,1)}, bf16[1024,256]{1,0:T(8,128)(2,1)S(1)}, u32[]{:S(2)}, u32[]{:S(2)}) collective-permute-start(bf16[1024,256]{1,0:T(8,128)(2,1)} %collective-permute-done.11.refs_1_), channel_id=1, source_target_pairs={{0,4},{1,5},{2,14},{3,15},{4,8},{5,9},{6,2},{7,3},{8,12},{9,13},{1... | collective-permute-start | bytes 1572872 | tf_op jit(solution)/shard_map/ppermute | solution.py:267
  96.6 14.5 %collective-permute-start.13 = (bf16[1024,256]{1,0:T(8,128)(2,1)}, bf16[1024,256]{1,0:T(8,128)(2,1)S(1)}, u32[]{:S(2)}, u32[]{:S(2)}) collective-permute-start(bf16[1024,256]{1,0:T(8,128)(2,1)} %copy-done.1), channel_id=1, source_target_pairs={{0,1},{1,0},{2,3},{3,2},{4,5},{5,4},{6,7},{7,6},{8,9},{9,8},{10,11... | collective-permute-start | bytes 1572872 | tf_op jit(solution)/shard_map/ppermute | solution.py:267
  97.0 14.2 %collective-permute-start.14 = (bf16[1024,256]{1,0:T(8,128)(2,1)}, bf16[1024,256]{1,0:T(8,128)(2,1)S(1)}, u32[]{:S(2)}, u32[]{:S(2)}) collective-permute-start(bf16[1024,256]{1,0:T(8,128)(2,1)} %collective-permute-done.11.refs_1_), channel_id=1, source_target_pairs={{0,1},{1,0},{2,3},{3,2},{4,5},{5,4},{6,7},{7,6},{8,9},{9,8},{10,11... | collective-permute-start | bytes 1572872 | tf_op jit(solution)/shard_map/ppermute | solution.py:267
  97.2 13.9 %collective-permute-start.15 = (bf16[1024,256]{1,0:T(8,128)(2,1)S(1)}, bf16[1024,256]{1,0:T(8,128)(2,1)S(1)}, u32[]{:S(2)}, u32[]{:S(2)}) collective-permute-start(bf16[1024,256]{1,0:T(8,128)(2,1)S(1)} %collective-permute-done.10.refs_2_), channel_id=1, source_target_pairs={{0,1},{1,0},{2,3},{3,2},{4,5},{5,4},{6,7},{7,6},{8,9},{9,8},{10,11... | collective-permute-start | bytes 1572872 | tf_op jit(solution)/shard_map/ppermute | solution.py:267
  97.5 9.6 %slice-start.1 = ((s8[10485760]{0:T(1024)(128)(4,1)}), s8[4194304]{0:T(1024)(128)(4,1)S(1)}, s32[]{:S(2)}) async-start(s8[10485760]{0:T(1024)(128)(4,1)} %bitcast.11), calls=%async_computation.2 | async-start | bytes 8388608
  97.5 9.6 %slice-start.2 = ((s8[10485760]{0:T(1024)(128)(4,1)}), s8[4194304]{0:T(1024)(128)(4,1)S(1)}, s32[]{:S(2)}) async-start(s8[10485760]{0:T(1024)(128)(4,1)} %bitcast.11), calls=%async_computation.3 | async-start | bytes 8388608
  107.1 5.7 %copy-start.2 = (bf16[1024,256]{1,0:T(8,128)(2,1)S(1)}, bf16[1024,256]{1,0:T(8,128)(2,1)}, u32[]{:S(2)}) copy-start(bf16[1024,256]{1,0:T(8,128)(2,1)} %copy-done.1) | copy-start | bytes 1572868
  110.8 2.0 %collective-permute-start.16 = (bf16[1024,256]{1,0:T(8,128)(2,1)S(1)}, bf16[1024,256]{1,0:T(8,128)(2,1)S(1)}, u32[]{:S(2)}, u32[]{:S(2)}) collective-permute-start(bf16[1024,256]{1,0:T(8,128)(2,1)S(1)} %gate.7.refs_3_), channel_id=1, source_target_pairs={{0,1},{1,0},{2,3},{3,2},{4,5},{5,4},{6,7},{7,6},{8,9},{9,8},{10,11... | collective-permute-start | bytes 1572872 | tf_op jit(solution)/shard_map/ppermute | solution.py:267

commit v6 on v5

--- a/solution.py
+++ b/solution.py
@@ -52,7 +52,7 @@
     return [2 * unit, 2 * unit, 2 * unit, 2 * unit]
 
 
-def pack_kernel(capacity, owner_hbm, target_hbm, rows_hbm, out_ref, owner_ref, target_ref, rows_ref, sems):
+def pack_kernel(capacity, owner_hbm, target_hbm, rows_hbm, out_hbm, owner_ref, target_ref, rows_ref, out_ref, sems, out_sems):
     copies = [
         pltpu.make_async_copy(source, target, sems.at[i])
         for i, (source, target) in enumerate(
@@ -83,10 +83,20 @@
     out_ref[:, width:] = lax.dot_general(
         picker, tags, (((1,), (1,)), ((), ())), preferred_element_type=jnp.float32
     ).astype(jnp.bfloat16)
+    ends = [pl.ds(width, LANES), pl.ds(0, width // 2), pl.ds(width // 2, width // 2)]
+    outs = [
+        pltpu.make_async_copy(out_ref.at[:, end], out_hbm.at[:, end], out_sems.at[i])
+        for i, end in enumerate(ends)
+    ]
+    outs[0].start()
     copies[2].wait()
-    out_ref[:, :width] = jnp.dot(
-        picker, rows_ref[...], preferred_element_type=jnp.float32
-    ).astype(jnp.bfloat16)
+    for end, out in zip(ends[1:], outs[1:]):
+        out_ref[:, end] = jnp.dot(
+            picker, rows_ref[:, end], preferred_element_type=jnp.float32
+        ).astype(jnp.bfloat16)
+        out.start()
+    for out in outs:
+        out.wait()
 
 
 def inject_kernel(base_ref, arrived_ref, wait_ref, whole_ref, *out_refs):
@@ -282,13 +292,15 @@
 
     outgoing = pl.pallas_call(
         functools.partial(pack_kernel, capacity),
-        out_shape=jax.ShapeDtypeStruct((slots, width + LANES), jnp.bfloat16),
+        out_shape=pltpu.HBM((slots, width + LANES), jnp.bfloat16),
         in_specs=[HBM] * 3,
-        out_specs=VMEM,
+        out_specs=HBM,
         scratch_shapes=[
             pltpu.VMEM((1, term_rows.shape[0]), jnp.int32),
             pltpu.VMEM((1, term_rows.shape[0]), jnp.int32),
             pltpu.VMEM(term_rows.shape, jnp.bfloat16),
+            pltpu.VMEM((slots, width + LANES), jnp.bfloat16),
+            pltpu.SemaphoreType.DMA((3,)),
             pltpu.SemaphoreType.DMA((3,)),
         ],
         compiler_params=limit(16),

time: 120 us -> 119 us (level)
  no operation moved by 1% of the time
where the time goes in v6:
time: 119 us
  waiting for transfers between devices  49 us (41%)
  Pallas kernels  35.9 us (30%)
  starting transfers between devices  31.5 us (26%)
  local copies, waits for them, and re-layouts  2.5 us (2%)
    ppermute x17, waiting for transfers between devices, send(): return lax.ppermute(value, 'row', pairs)  34.1 us
    ppermute x17, starting transfers between devices, send(): return lax.ppermute(value, 'row', pairs)  24.9 us
    all_to_all x1, waiting for transfers between devices, shards(): lax.all_to_all(outgoing.reshape(devices, capacity, width + LANES), 'row',...  14.8 us
    pallas_call x1, Pallas kernels, shards(): pl.pallas_call(dense_kernel, out_shape=(pltpu.HBM((seg_dev, SLOTS * seg_d...  11 us
    pallas_call x1, Pallas kernels, shards(): pl.pallas_call(functools.partial(flux_kernel, 0, half), out_shape=(out_ty...  9.58 us
    all_to_all x1, starting transfers between devices, shards(): lax.all_to_all(outgoing.reshape(devices, capacity, width + LANES), 'row',...  6.68 us
    pallas_call x1, Pallas kernels, shards(): pl.pallas_call(functools.partial(far_kernel, wide, left), out_shape=out_t...  6.42 us
    pallas_call x1, Pallas kernels, shards(): pl.pallas_call(functools.partial(near_kernel, wide), out_shape=(jax.Shape...  3.67 us
  transfers between devices with their start and end apart: 18, of which 7 were waited for; matrix products, arithmetic and copies ran while one was open for 0% of the time, Pallas kernels for 20%

profile of v6, /device:TPU:7, one launch (start us, length us, event | category | flops | bytes accessed | tf_op | source)
XLA Modules:
  0.0 119.1 jit_solution(18288818252667820439)
XLA Ops:
  0.0 0.0 copy-start.3
  0.0 2.5 %pack_terms.1.wait_ref = bf16[512,1152]{1,0:T(8,128)(2,1)} custom-call(s32[1,256]{1,0:T(1,128)} %bitcast.15, s32[1,256]{1,0:T(1,128)} %bitcast.16, bf16[256,1024]{1,0:T(8,128)(2,1)} %rows_hbm.1), custom_call_target="tpu_custom_call" | custom-call | tf_op jit(solution)/shard_map/pack_terms/pallas_call | solution.py:293
  2.5 6.7 %all-to-all-start = ((bf16[16,32,1152]{2,1,0:T(8,128)(2,1)}), bf16[16,32,1152]{2,1,0:T(8,128)(2,1)S(1)}, u32[]{:S(2)}, u32[]{:S(2)}) async-start(bf16[16,32,1152]{2,1,0:T(8,128)(2,1)} %bitcast.14), calls=%async_computation | async-start | bytes 2359296 | tf_op jit(solution)/shard_map/all_to_all | solution.py:309
  9.1 0.1 stack.35.slot_ref
  9.2 0.0 copy-done.3
  9.2 11.0 %dense_blocks.1 = (bf16[1024,5120]{1,0:T(8,128)(2,1)}, f32[8,128]{1,0:T(8,128)S(1)}) custom-call(s32[4,20]{1,0:T(4,128)S(1)} %copy-done.3, s32[6]{0:T(128)S(1)} %stack.35.slot_ref, bf16[4,20,256,256]{3,2,1,0:T(8,128)(2,1)} %blocks_ref.1, bf16[512,1152]{1,0:T(8,128)(2,1)} %pack_terms.1.wait_ref), custom_call_target="tpu_custom_call" | custom-call | tf_op jit(solution)/shard_map/dense_blocks/pallas_call | solution.py:313
  20.3 14.8 %all-to-all-done = bf16[16,32,1152]{2,1,0:T(8,128)(2,1)S(1)} async-done(((bf16[16,32,1152]{2,1,0:T(8,128)(2,1)}), bf16[16,32,1152]{2,1,0:T(8,128)(2,1)S(1)}, u32[]{:S(2)}, u32[]{:S(2)}) %all-to-all-start) | async-done | bytes 1179680 | tf_op jit(solution)/shard_map/all_to_all | solution.py:309
  35.1 0.0 copy-start
  35.1 1.6 %copy-done = bf16[1024,1024]{1,0:T(8,128)(2,1)S(1)} copy-done((bf16[1024,1024]{1,0:T(8,128)(2,1)S(1)}, bf16[1024,1024]{1,0:T(8,128)(2,1)}, u32[]{:S(2)}) %copy-start) | copy-done | bytes 2097176
  36.7 0.0 slice-start
  36.7 2.7 %inject_terms.1 = (bf16[1024,1024]{1,0:T(8,128)(2,1)}, bf16[1024,256]{1,0:T(8,128)(2,1)S(1)}, bf16[1024,256]{1,0:T(8,128)(2,1)S(1)}, bf16[1024,256]{1,0:T(8,128)(2,1)S(1)}, bf16[1024,256]{1,0:T(8,128)(2,1)S(1)}) custom-call(bf16[1024,1024]{1,0:T(8,128)(2,1)S(1)} %copy-done, bf16[512,1152]{1,0:T(8,128)(2,1)S(1)} %bitcast.13, ...), custom_call_target="tpu_custom_call" | custom-call | tf_op jit(solution)/shard_map/inject_terms/pallas_call | solution.py:328
  39.4 0.0 collective-permute-start
  39.4 0.0 collective-permute-start.1
  39.4 1.5 %collective-permute-start.2 = (bf16[1024,256]{1,0:T(8,128)(2,1)S(1)}, bf16[1024,256]{1,0:T(8,128)(2,1)}, u32[]{:S(2)}, u32[]{:S(2)}) collective-permute-start(bf16[1024,256]{1,0:T(8,128)(2,1)S(1)} %get-tuple-element.20), channel_id=1, source_target_pairs={{0,2},{1,3},{2,0},{3,1},{4,6},{5,7},{6,4},{7,5},{8,10},{9,11},{10,... | collective-permute-start | bytes 1572872 | tf_op jit(solution)/shard_map/ppermute | solution.py:277
  40.9 0.0 collective-permute-start.9
  40.9 1.4 %collective-permute-start.11 = (bf16[1024,256]{1,0:T(8,128)(2,1)S(1)}, bf16[1024,256]{1,0:T(8,128)(2,1)}, u32[]{:S(2)}, u32[]{:S(2)}) collective-permute-start(bf16[1024,256]{1,0:T(8,128)(2,1)S(1)} %get-tuple-element.24), channel_id=1, source_target_pairs={{0,2},{1,3},{2,0},{3,1},{4,6},{5,7},{6,4},{7,5},{8,10},{9,11},{10,... | collective-permute-start | bytes 1572872 | tf_op jit(solution)/shard_map/ppermute | solution.py:277
  42.4 10.0 %collective-permute-done.1.refs_0_ = bf16[1024,256]{1,0:T(8,128)(2,1)S(1)} collective-permute-done((bf16[1024,256]{1,0:T(8,128)(2,1)S(1)}, bf16[1024,256]{1,0:T(8,128)(2,1)S(1)}, u32[]{:S(2)}, u32[]{:S(2)}) %collective-permute-start.1) | collective-permute-done | bytes 524320 | tf_op jit(solution)/shard_map/ppermute | solution.py:277
  52.4 0.0 copy-start.4
  52.4 4.2 %collective-permute-start.3 = (bf16[1024,256]{1,0:T(8,128)(2,1)S(1)}, bf16[1024,256]{1,0:T(8,128)(2,1)}, u32[]{:S(2)}, u32[]{:S(2)}) collective-permute-start(bf16[1024,256]{1,0:T(8,128)(2,1)S(1)} %collective-permute-done.1.refs_0_), channel_id=1, source_target_pairs={{0,4},{1,5},{2,14},{3,15},{4,8},{5,9},{6,2},{7,3},{8,12},{9,13},{1... | collective-permute-start | bytes 1572872 | tf_op jit(solution)/shard_map/ppermute | solution.py:277
  56.6 7.1 %collective-permute-done.2.refs_1_ = bf16[1024,256]{1,0:T(8,128)(2,1)} collective-permute-done((bf16[1024,256]{1,0:T(8,128)(2,1)S(1)}, bf16[1024,256]{1,0:T(8,128)(2,1)}, u32[]{:S(2)}, u32[]{:S(2)}) %collective-permute-start.2) | collective-permute-done | bytes 524320 | tf_op jit(solution)/shard_map/ppermute | solution.py:277
  63.8 4.2 %collective-permute-start.4 = (bf16[1024,256]{1,0:T(8,128)(2,1)}, bf16[1024,256]{1,0:T(8,128)(2,1)}, u32[]{:S(2)}, u32[]{:S(2)}) collective-permute-start(bf16[1024,256]{1,0:T(8,128)(2,1)} %collective-permute-done.2.refs_1_), channel_id=1, source_target_pairs={{0,4},{1,5},{2,14},{3,15},{4,8},{5,9},{6,2},{7,3},{8,12},{9,13},{1... | collective-permute-start | bytes 1572872 | tf_op jit(solution)/shard_map/ppermute | solution.py:277
  68.0 7.0 %collective-permute-done.9.refs_0_ = bf16[1024,256]{1,0:T(8,128)(2,1)S(1)} collective-permute-done((bf16[1024,256]{1,0:T(8,128)(2,1)S(1)}, bf16[1024,256]{1,0:T(8,128)(2,1)S(1)}, u32[]{:S(2)}, u32[]{:S(2)}) %collective-permute-start.9) | collective-permute-done | bytes 524320 | tf_op jit(solution)/shard_map/ppermute | solution.py:277
  75.0 0.0 copy-start.1
  75.0 4.2 %collective-permute-start.10 = (bf16[1024,256]{1,0:T(8,128)(2,1)S(1)}, bf16[1024,256]{1,0:T(8,128)(2,1)S(1)}, u32[]{:S(2)}, u32[]{:S(2)}) collective-permute-start(bf16[1024,256]{1,0:T(8,128)(2,1)S(1)} %collective-permute-done.9.refs_0_), channel_id=1, source_target_pairs={{0,4},{1,5},{2,14},{3,15},{4,8},{5,9},{6,2},{7,3},{8,12},{9,13},{1... | collective-permute-start | bytes 1572872 | tf_op jit(solution)/shard_map/ppermute | solution.py:277
  79.2 7.0 %collective-permute-done.11.refs_1_ = bf16[1024,256]{1,0:T(8,128)(2,1)} collective-permute-done((bf16[1024,256]{1,0:T(8,128)(2,1)S(1)}, bf16[1024,256]{1,0:T(8,128)(2,1)}, u32[]{:S(2)}, u32[]{:S(2)}) %collective-permute-start.11) | collective-permute-done | bytes 524320 | tf_op jit(solution)/shard_map/ppermute | solution.py:277
  86.2 1.4 %collective-permute-start.5 = (bf16[1024,256]{1,0:T(8,128)(2,1)S(1)}, bf16[1024,256]{1,0:T(8,128)(2,1)S(1)}, u32[]{:S(2)}, u32[]{:S(2)}) collective-permute-start(bf16[1024,256]{1,0:T(8,128)(2,1)S(1)} %collective-permute-done.1.refs_0_), channel_id=1, source_target_pairs={{0,1},{1,0},{2,3},{3,2},{4,5},{5,4},{6,7},{7,6},{8,9},{9,8},{10,11... | collective-permute-start | bytes 1572872 | tf_op jit(solution)/shard_map/ppermute | solution.py:277
  87.6 0.0 collective-permute-done.3.refs_2_
  87.6 0.0 collective-permute-start.6
  87.6 0.0 collective-permute-done.4.refs_3_
  87.6 0.5 collective-permute-start.7
  88.1 1.2 %collective-permute-done.10.refs_2_ = bf16[1024,256]{1,0:T(8,128)(2,1)S(1)} collective-permute-done((bf16[1024,256]{1,0:T(8,128)(2,1)S(1)}, bf16[1024,256]{1,0:T(8,128)(2,1)S(1)}, u32[]{:S(2)}, u32[]{:S(2)}) %collective-permute-start.10) | collective-permute-done | bytes 524320 | tf_op jit(solution)/shard_map/ppermute | solution.py:277
  89.3 2.2 %collective-permute-start.8 = (bf16[1024,256]{1,0:T(8,128)(2,1)}, bf16[1024,256]{1,0:T(8,128)(2,1)}, u32[]{:S(2)}, u32[]{:S(2)}) collective-permute-start(bf16[1024,256]{1,0:T(8,128)(2,1)} %collective-permute-done.4.refs_3_), channel_id=1, source_target_pairs={{0,1},{1,0},{2,3},{3,2},{4,5},{5,4},{6,7},{7,6},{8,9},{9,8},{10,11... | collective-permute-start | bytes 1572872 | tf_op jit(solution)/shard_map/ppermute | solution.py:277
  91.6 0.0 copy-done.1
  91.6 0.0 collective-permute-done.5.refs_4_
  91.6 0.0 copy-done.4
  91.6 0.0 copy-start.5
  91.6 0.8 copy-done.5
  92.4 4.0 %collective-permute-start.12 = (bf16[1024,256]{1,0:T(8,128)(2,1)}, bf16[1024,256]{1,0:T(8,128)(2,1)S(1)}, u32[]{:S(2)}, u32[]{:S(2)}) collective-permute-start(bf16[1024,256]{1,0:T(8,128)(2,1)} %collective-permute-done.11.refs_1_), channel_id=1, source_target_pairs={{0,4},{1,5},{2,14},{3,15},{4,8},{5,9},{6,2},{7,3},{8,12},{9,13},{1... | collective-permute-start | bytes 1572872 | tf_op jit(solution)/shard_map/ppermute | solution.py:277
  96.4 0.1 add_convert_fusion.refs_1_.flag_ref
  96.5 0.0 collective-permute-done.6.refs_5_
  96.5 0.4 collective-permute-start.13
  96.8 0.0 collective-permute-done.7.refs_6_
  96.8 0.2 collective-permute-start.14
  97.0 0.0 collective-permute-done.8.refs_7_
  97.0 0.3 collective-permute-start.15
  97.3 0.0 collective-permute-done.beside
  97.3 0.0 slice-start.1
  97.3 0.0 slice-start.2
  97.3 9.6 %flux.1 = (bf16[1024,1024]{1,0:T(8,128)(2,1)}, f32[8,128]{1,0:T(8,128)S(1)}) custom-call(s32[2]{0:T(128)S(1)} %add_convert_fusion.refs_1_.flag_ref, bf16[1024,5120]{1,0:T(8,128)(2,1)} %get-tuple-element.16.dense_ref, bf16[1024,1024]{1,0:T(8,128)(2,1)} %get-tuple-element.18.own, bf16[1024,1024]{1,0:T(8,128)(2,1)} %collective-permute-done.beside, ...), custom_call_target="tpu_custom_call" | custom-call | tf_op jit(solution)/shard_map/flux/pallas_call | solution.py:359
  106.9 0.0 slice-done
  106.9 0.0 slice-done.1
  106.9 0.0 slice-done.2
  107.0 0.0 copy-start.2
  107.0 3.7 %near_flux.1 = (f32[1024,512]{1,0:T(8,128)S(1)}, f32[8,128]{1,0:T(8,128)S(1)}) custom-call(bf16[1024,5120]{1,0:T(8,128)(2,1)S(1)} %bitcast.12, bf16[1024,1024]{1,0:T(8,128)(2,1)} %get-tuple-element.18.own, bf16[1024,1024]{1,0:T(8,128)(2,1)} %collective-permute-done.beside, f32[8,128]{1,0:T(8,128)S(1)} %get-tuple-element.22.wait_ref), custom_call_target="tpu_custom_call" | custom-call | tf_op jit(solution)/shard_map/near_flux/pallas_call | solution.py:379
  110.7 0.0 collective-permute-done.12.refs_0_
  110.7 0.3 collective-permute-start.16
  111.0 0.0 collective-permute-done.13.refs_4_
  111.0 0.0 collective-permute-done.14.refs_5_
  111.0 0.0 collective-permute-done.15.refs_6_
  111.0 1.7 %collective-permute-done.16.refs_7_ = bf16[1024,256]{1,0:T(8,128)(2,1)S(1)} collective-permute-done((bf16[1024,256]{1,0:T(8,128)(2,1)S(1)}, bf16[1024,256]{1,0:T(8,128)(2,1)S(1)}, u32[]{:S(2)}, u32[]{:S(2)}) %collective-permute-start.16) | collective-permute-done | bytes 524320 | tf_op jit(solution)/shard_map/ppermute | solution.py:277
  112.7 0.0 copy-done.2
  112.7 6.4 %far_flux.1 = bf16[1024,1024]{1,0:T(8,128)(2,1)} custom-call(s32[2]{0:T(128)S(1)} %add_convert_fusion.refs_1_.flag_ref, bf16[1024,5120]{1,0:T(8,128)(2,1)S(1)} %bitcast.12, f32[1024,512]{1,0:T(8,128)S(1)} %get-tuple-element.23.prior_ref, bf16[1024,256]{1,0:T(8,128)(2,1)S(1)} %copy-done.2, ...), custom_call_target="tpu_custom_call", output_to_operand_aliasing={{}: (11, {})} | custom-call | tf_op jit(solution)/shard_map/far_flux/pallas_call | solution.py:395
  (6 shorter events, 0.0 us)
Async XLA Ops:
  0.0 9.2 %copy-start.3 = (s32[4,20]{1,0:T(4,128)S(1)}, s32[4,20]{1,0:T(4,128)}, u32[]{:S(2)}) copy-start(s32[4,20]{1,0:T(4,128)} %cols_ref.1) | copy-start | bytes 964
  2.5 32.6 %all-to-all-start = ((bf16[16,32,1152]{2,1,0:T(8,128)(2,1)}), bf16[16,32,1152]{2,1,0:T(8,128)(2,1)S(1)}, u32[]{:S(2)}, u32[]{:S(2)}) async-start(bf16[16,32,1152]{2,1,0:T(8,128)(2,1)} %bitcast.14), calls=%async_computation | async-start | bytes 2359296 | tf_op jit(solution)/shard_map/all_to_all | solution.py:309
  35.1 1.6 %copy-start = (bf16[1024,1024]{1,0:T(8,128)(2,1)S(1)}, bf16[1024,1024]{1,0:T(8,128)(2,1)}, u32[]{:S(2)}) copy-start(bf16[1024,1024]{1,0:T(8,128)(2,1)} %base_ref.1) | copy-start | bytes 6291460
  36.7 70.2 %slice-start = ((s8[10485760]{0:T(1024)(128)(4,1)}), s8[2097152]{0:T(1024)(128)(4,1)S(1)}, s32[]{:S(2)}) async-start(s8[10485760]{0:T(1024)(128)(4,1)} %bitcast.11), calls=%async_computation.1 | async-start | bytes 4194304
  39.4 57.9 %collective-permute-start = (bf16[1024,1024]{1,0:T(8,128)(2,1)}, bf16[1024,1024]{1,0:T(8,128)(2,1)}, u32[]{:S(2)}, u32[]{:S(2)}) collective-permute-start(bf16[1024,1024]{1,0:T(8,128)(2,1)} %get-tuple-element.18.own), channel_id=1, source_target_pairs={{0,1},{1,0},{2,3},{3,2},{4,5},{5,4},{6,7},{7,6},{8,9},{9,8},{10,11... | collective-permute-start | bytes 6291464 | tf_op jit(solution)/shard_map/ppermute | solution.py:277
  39.4 13.0 %collective-permute-start.1 = (bf16[1024,256]{1,0:T(8,128)(2,1)S(1)}, bf16[1024,256]{1,0:T(8,128)(2,1)S(1)}, u32[]{:S(2)}, u32[]{:S(2)}) collective-permute-start(bf16[1024,256]{1,0:T(8,128)(2,1)S(1)} %get-tuple-element.19), channel_id=1, source_target_pairs={{0,2},{1,3},{2,0},{3,1},{4,6},{5,7},{6,4},{7,5},{8,10},{9,11},{10,... | collective-permute-start | bytes 1572872 | tf_op jit(solution)/shard_map/ppermute | solution.py:277
  39.4 24.3 %collective-permute-start.2 = (bf16[1024,256]{1,0:T(8,128)(2,1)S(1)}, bf16[1024,256]{1,0:T(8,128)(2,1)}, u32[]{:S(2)}, u32[]{:S(2)}) collective-permute-start(bf16[1024,256]{1,0:T(8,128)(2,1)S(1)} %get-tuple-element.20), channel_id=1, source_target_pairs={{0,2},{1,3},{2,0},{3,1},{4,6},{5,7},{6,4},{7,5},{8,10},{9,11},{10,... | collective-permute-start | bytes 1572872 | tf_op jit(solution)/shard_map/ppermute | solution.py:277
  40.9 34.1 %collective-permute-start.9 = (bf16[1024,256]{1,0:T(8,128)(2,1)S(1)}, bf16[1024,256]{1,0:T(8,128)(2,1)S(1)}, u32[]{:S(2)}, u32[]{:S(2)}) collective-permute-start(bf16[1024,256]{1,0:T(8,128)(2,1)S(1)} %get-tuple-element.21), channel_id=1, source_target_pairs={{0,2},{1,3},{2,0},{3,1},{4,6},{5,7},{6,4},{7,5},{8,10},{9,11},{10,... | collective-permute-start | bytes 1572872 | tf_op jit(solution)/shard_map/ppermute | solution.py:277
  40.9 45.3 %collective-permute-start.11 = (bf16[1024,256]{1,0:T(8,128)(2,1)S(1)}, bf16[1024,256]{1,0:T(8,128)(2,1)}, u32[]{:S(2)}, u32[]{:S(2)}) collective-permute-start(bf16[1024,256]{1,0:T(8,128)(2,1)S(1)} %get-tuple-element.24), channel_id=1, source_target_pairs={{0,2},{1,3},{2,0},{3,1},{4,6},{5,7},{6,4},{7,5},{8,10},{9,11},{10,... | collective-permute-start | bytes 1572872 | tf_op jit(solution)/shard_map/ppermute | solution.py:277
  52.4 39.2 %copy-start.4 = (bf16[1024,256]{1,0:T(8,128)(2,1)}, bf16[1024,256]{1,0:T(8,128)(2,1)S(1)}, u32[]{:S(2)}) copy-start(bf16[1024,256]{1,0:T(8,128)(2,1)S(1)} %collective-permute-done.1.refs_0_) | copy-start | bytes 1572868
  52.4 35.2 %collective-permute-start.3 = (bf16[1024,256]{1,0:T(8,128)(2,1)S(1)}, bf16[1024,256]{1,0:T(8,128)(2,1)}, u32[]{:S(2)}, u32[]{:S(2)}) collective-permute-start(bf16[1024,256]{1,0:T(8,128)(2,1)S(1)} %collective-permute-done.1.refs_0_), channel_id=1, source_target_pairs={{0,4},{1,5},{2,14},{3,15},{4,8},{5,9},{6,2},{7,3},{8,12},{9,13},{1... | collective-permute-start | bytes 1572872 | tf_op jit(solution)/shard_map/ppermute | solution.py:277
  63.8 23.8 %collective-permute-start.4 = (bf16[1024,256]{1,0:T(8,128)(2,1)}, bf16[1024,256]{1,0:T(8,128)(2,1)}, u32[]{:S(2)}, u32[]{:S(2)}) collective-permute-start(bf16[1024,256]{1,0:T(8,128)(2,1)} %collective-permute-done.2.refs_1_), channel_id=1, source_target_pairs={{0,4},{1,5},{2,14},{3,15},{4,8},{5,9},{6,2},{7,3},{8,12},{9,13},{1... | collective-permute-start | bytes 1572872 | tf_op jit(solution)/shard_map/ppermute | solution.py:277
  75.0 16.6 %copy-start.1 = (bf16[1024,256]{1,0:T(8,128)(2,1)}, bf16[1024,256]{1,0:T(8,128)(2,1)S(1)}, u32[]{:S(2)}) copy-start(bf16[1024,256]{1,0:T(8,128)(2,1)S(1)} %collective-permute-done.9.refs_0_) | copy-start | bytes 1572868
  75.0 14.3 %collective-permute-start.10 = (bf16[1024,256]{1,0:T(8,128)(2,1)S(1)}, bf16[1024,256]{1,0:T(8,128)(2,1)S(1)}, u32[]{:S(2)}, u32[]{:S(2)}) collective-permute-start(bf16[1024,256]{1,0:T(8,128)(2,1)S(1)} %collective-permute-done.9.refs_0_), channel_id=1, source_target_pairs={{0,4},{1,5},{2,14},{3,15},{4,8},{5,9},{6,2},{7,3},{8,12},{9,13},{1... | collective-permute-start | bytes 1572872 | tf_op jit(solution)/shard_map/ppermute | solution.py:277
  86.2 5.3 %collective-permute-start.5 = (bf16[1024,256]{1,0:T(8,128)(2,1)S(1)}, bf16[1024,256]{1,0:T(8,128)(2,1)S(1)}, u32[]{:S(2)}, u32[]{:S(2)}) collective-permute-start(bf16[1024,256]{1,0:T(8,128)(2,1)S(1)} %collective-permute-done.1.refs_0_), channel_id=1, source_target_pairs={{0,1},{1,0},{2,3},{3,2},{4,5},{5,4},{6,7},{7,6},{8,9},{9,8},{10,11... | collective-permute-start | bytes 1572872 | tf_op jit(solution)/shard_map/ppermute | solution.py:277
  87.6 8.9 %collective-permute-start.6 = (bf16[1024,256]{1,0:T(8,128)(2,1)}, bf16[1024,256]{1,0:T(8,128)(2,1)}, u32[]{:S(2)}, u32[]{:S(2)}) collective-permute-start(bf16[1024,256]{1,0:T(8,128)(2,1)} %collective-permute-done.2.refs_1_), channel_id=1, source_target_pairs={{0,1},{1,0},{2,3},{3,2},{4,5},{5,4},{6,7},{7,6},{8,9},{9,8},{10,11... | collective-permute-start | bytes 1572872 | tf_op jit(solution)/shard_map/ppermute | solution.py:277
  87.6 9.2 %collective-permute-start.7 = (bf16[1024,256]{1,0:T(8,128)(2,1)}, bf16[1024,256]{1,0:T(8,128)(2,1)}, u32[]{:S(2)}, u32[]{:S(2)}) collective-permute-start(bf16[1024,256]{1,0:T(8,128)(2,1)} %collective-permute-done.3.refs_2_), channel_id=1, source_target_pairs={{0,1},{1,0},{2,3},{3,2},{4,5},{5,4},{6,7},{7,6},{8,9},{9,8},{10,11... | collective-permute-start | bytes 1572872 | tf_op jit(solution)/shard_map/ppermute | solution.py:277
  89.3 7.7 %collective-permute-start.8 = (bf16[1024,256]{1,0:T(8,128)(2,1)}, bf16[1024,256]{1,0:T(8,128)(2,1)}, u32[]{:S(2)}, u32[]{:S(2)}) collective-permute-start(bf16[1024,256]{1,0:T(8,128)(2,1)} %collective-permute-done.4.refs_3_), channel_id=1, source_target_pairs={{0,1},{1,0},{2,3},{3,2},{4,5},{5,4},{6,7},{7,6},{8,9},{9,8},{10,11... | collective-permute-start | bytes 1572872 | tf_op jit(solution)/shard_map/ppermute | solution.py:277
  91.6 0.8 copy-start.5
  92.4 18.3 %collective-permute-start.12 = (bf16[1024,256]{1,0:T(8,128)(2,1)}, bf16[1024,256]{1,0:T(8,128)(2,1)S(1)}, u32[]{:S(2)}, u32[]{:S(2)}) collective-permute-start(bf16[1024,256]{1,0:T(8,128)(2,1)} %collective-permute-done.11.refs_1_), channel_id=1, source_target_pairs={{0,4},{1,5},{2,14},{3,15},{4,8},{5,9},{6,2},{7,3},{8,12},{9,13},{1... | collective-permute-start | bytes 1572872 | tf_op jit(solution)/shard_map/ppermute | solution.py:277
  96.5 14.5 %collective-permute-start.13 = (bf16[1024,256]{1,0:T(8,128)(2,1)}, bf16[1024,256]{1,0:T(8,128)(2,1)S(1)}, u32[]{:S(2)}, u32[]{:S(2)}) collective-permute-start(bf16[1024,256]{1,0:T(8,128)(2,1)} %copy-done.1), channel_id=1, source_target_pairs={{0,1},{1,0},{2,3},{3,2},{4,5},{5,4},{6,7},{7,6},{8,9},{9,8},{10,11... | collective-permute-start | bytes 1572872 | tf_op jit(solution)/shard_map/ppermute | solution.py:277
  96.8 14.2 %collective-permute-start.14 = (bf16[1024,256]{1,0:T(8,128)(2,1)}, bf16[1024,256]{1,0:T(8,128)(2,1)S(1)}, u32[]{:S(2)}, u32[]{:S(2)}) collective-permute-start(bf16[1024,256]{1,0:T(8,128)(2,1)} %collective-permute-done.11.refs_1_), channel_id=1, source_target_pairs={{0,1},{1,0},{2,3},{3,2},{4,5},{5,4},{6,7},{7,6},{8,9},{9,8},{10,11... | collective-permute-start | bytes 1572872 | tf_op jit(solution)/shard_map/ppermute | solution.py:277
  97.0 13.9 %collective-permute-start.15 = (bf16[1024,256]{1,0:T(8,128)(2,1)S(1)}, bf16[1024,256]{1,0:T(8,128)(2,1)S(1)}, u32[]{:S(2)}, u32[]{:S(2)}) collective-permute-start(bf16[1024,256]{1,0:T(8,128)(2,1)S(1)} %collective-permute-done.10.refs_2_), channel_id=1, source_target_pairs={{0,1},{1,0},{2,3},{3,2},{4,5},{5,4},{6,7},{7,6},{8,9},{9,8},{10,11... | collective-permute-start | bytes 1572872 | tf_op jit(solution)/shard_map/ppermute | solution.py:277
  97.3 9.6 %slice-start.1 = ((s8[10485760]{0:T(1024)(128)(4,1)}), s8[4194304]{0:T(1024)(128)(4,1)S(1)}, s32[]{:S(2)}) async-start(s8[10485760]{0:T(1024)(128)(4,1)} %bitcast.11), calls=%async_computation.2 | async-start | bytes 8388608
  97.3 9.6 %slice-start.2 = ((s8[10485760]{0:T(1024)(128)(4,1)}), s8[4194304]{0:T(1024)(128)(4,1)S(1)}, s32[]{:S(2)}) async-start(s8[10485760]{0:T(1024)(128)(4,1)} %bitcast.11), calls=%async_computation.3 | async-start | bytes 8388608
  107.0 5.7 %copy-start.2 = (bf16[1024,256]{1,0:T(8,128)(2,1)S(1)}, bf16[1024,256]{1,0:T(8,128)(2,1)}, u32[]{:S(2)}) copy-start(bf16[1024,256]{1,0:T(8,128)(2,1)} %copy-done.1) | copy-start | bytes 1572868
  110.7 2.0 %collective-permute-start.16 = (bf16[1024,256]{1,0:T(8,128)(2,1)S(1)}, bf16[1024,256]{1,0:T(8,128)(2,1)S(1)}, u32[]{:S(2)}, u32[]{:S(2)}) collective-permute-start(bf16[1024,256]{1,0:T(8,128)(2,1)S(1)} %gate.7.refs_3_), channel_id=1, source_target_pairs={{0,1},{1,0},{2,3},{3,2},{4,5},{5,4},{6,7},{7,6},{8,9},{9,8},{10,11... | collective-permute-start | bytes 1572872 | tf_op jit(solution)/shard_map/ppermute | solution.py:277

commit v7 on v6

--- a/solution.py
+++ b/solution.py
@@ -370,7 +370,7 @@
             pltpu.SemaphoreType.DMA((SLOTS, half)),
             pltpu.SemaphoreType.DMA,
         ],
-        compiler_params=limit(36),
+        compiler_params=limit(28),
         cost_estimate=cost(),
         name="flux",
     )(flag, *[in_hbm(item) for item in given], sign)

time: 119 us -> 119 us (level)
  no operation moved by 1% of the time
where the time goes in v7:
time: 119 us
  waiting for transfers between devices  49 us (41%)
  Pallas kernels  35.9 us (30%)
  starting transfers between devices  31.5 us (26%)
  local copies, waits for them, and re-layouts  2.5 us (2%)
    ppermute x17, waiting for transfers between devices, send(): return lax.ppermute(value, 'row', pairs)  34.1 us
    ppermute x17, starting transfers between devices, send(): return lax.ppermute(value, 'row', pairs)  24.9 us
    all_to_all x1, waiting for transfers between devices, shards(): lax.all_to_all(outgoing.reshape(devices, capacity, width + LANES), 'row',...  14.8 us
    pallas_call x1, Pallas kernels, shards(): pl.pallas_call(dense_kernel, out_shape=(pltpu.HBM((seg_dev, SLOTS * seg_d...  11 us
    pallas_call x1, Pallas kernels, shards(): pl.pallas_call(functools.partial(flux_kernel, 0, half), out_shape=(out_ty...  9.58 us
    all_to_all x1, starting transfers between devices, shards(): lax.all_to_all(outgoing.reshape(devices, capacity, width + LANES), 'row',...  6.68 us
    pallas_call x1, Pallas kernels, shards(): pl.pallas_call(functools.partial(far_kernel, wide, left), out_shape=out_t...  6.42 us
    pallas_call x1, Pallas kernels, shards(): pl.pallas_call(functools.partial(near_kernel, wide), out_shape=(jax.Shape...  3.67 us
  transfers between devices with their start and end apart: 18, of which 7 were waited for; matrix products, arithmetic and copies ran while one was open for 0% of the time, Pallas kernels for 20%

profile of v7, /device:TPU:7, one launch (start us, length us, event | category | flops | bytes accessed | tf_op | source)
XLA Modules:
  0.0 119.1 jit_solution(243617504074883262)
XLA Ops:
  0.0 0.0 copy-start.3
  0.0 2.5 %pack_terms.1.wait_ref = bf16[512,1152]{1,0:T(8,128)(2,1)} custom-call(s32[1,256]{1,0:T(1,128)} %bitcast.15, s32[1,256]{1,0:T(1,128)} %bitcast.16, bf16[256,1024]{1,0:T(8,128)(2,1)} %rows_hbm.1), custom_call_target="tpu_custom_call" | custom-call | tf_op jit(solution)/shard_map/pack_terms/pallas_call | solution.py:293
  2.5 6.7 %all-to-all-start = ((bf16[16,32,1152]{2,1,0:T(8,128)(2,1)}), bf16[16,32,1152]{2,1,0:T(8,128)(2,1)S(1)}, u32[]{:S(2)}, u32[]{:S(2)}) async-start(bf16[16,32,1152]{2,1,0:T(8,128)(2,1)} %bitcast.14), calls=%async_computation | async-start | bytes 2359296 | tf_op jit(solution)/shard_map/all_to_all | solution.py:309
  9.1 0.1 stack.35.slot_ref
  9.2 0.0 copy-done.3
  9.2 11.0 %dense_blocks.1 = (bf16[1024,5120]{1,0:T(8,128)(2,1)}, f32[8,128]{1,0:T(8,128)S(1)}) custom-call(s32[4,20]{1,0:T(4,128)S(1)} %copy-done.3, s32[6]{0:T(128)S(1)} %stack.35.slot_ref, bf16[4,20,256,256]{3,2,1,0:T(8,128)(2,1)} %blocks_ref.1, bf16[512,1152]{1,0:T(8,128)(2,1)} %pack_terms.1.wait_ref), custom_call_target="tpu_custom_call" | custom-call | tf_op jit(solution)/shard_map/dense_blocks/pallas_call | solution.py:313
  20.3 14.8 %all-to-all-done = bf16[16,32,1152]{2,1,0:T(8,128)(2,1)S(1)} async-done(((bf16[16,32,1152]{2,1,0:T(8,128)(2,1)}), bf16[16,32,1152]{2,1,0:T(8,128)(2,1)S(1)}, u32[]{:S(2)}, u32[]{:S(2)}) %all-to-all-start) | async-done | bytes 1179680 | tf_op jit(solution)/shard_map/all_to_all | solution.py:309
  35.1 0.0 copy-start
  35.1 1.6 %copy-done = bf16[1024,1024]{1,0:T(8,128)(2,1)S(1)} copy-done((bf16[1024,1024]{1,0:T(8,128)(2,1)S(1)}, bf16[1024,1024]{1,0:T(8,128)(2,1)}, u32[]{:S(2)}) %copy-start) | copy-done | bytes 2097176
  36.7 0.0 slice-start
  36.7 2.7 %inject_terms.1 = (bf16[1024,1024]{1,0:T(8,128)(2,1)}, bf16[1024,256]{1,0:T(8,128)(2,1)S(1)}, bf16[1024,256]{1,0:T(8,128)(2,1)S(1)}, bf16[1024,256]{1,0:T(8,128)(2,1)S(1)}, bf16[1024,256]{1,0:T(8,128)(2,1)S(1)}) custom-call(bf16[1024,1024]{1,0:T(8,128)(2,1)S(1)} %copy-done, bf16[512,1152]{1,0:T(8,128)(2,1)S(1)} %bitcast.13, ...), custom_call_target="tpu_custom_call" | custom-call | tf_op jit(solution)/shard_map/inject_terms/pallas_call | solution.py:328
  39.4 0.0 collective-permute-start
  39.4 0.0 collective-permute-start.1
  39.4 1.5 %collective-permute-start.2 = (bf16[1024,256]{1,0:T(8,128)(2,1)S(1)}, bf16[1024,256]{1,0:T(8,128)(2,1)}, u32[]{:S(2)}, u32[]{:S(2)}) collective-permute-start(bf16[1024,256]{1,0:T(8,128)(2,1)S(1)} %get-tuple-element.20), channel_id=1, source_target_pairs={{0,2},{1,3},{2,0},{3,1},{4,6},{5,7},{6,4},{7,5},{8,10},{9,11},{10,... | collective-permute-start | bytes 1572872 | tf_op jit(solution)/shard_map/ppermute | solution.py:277
  40.9 0.0 collective-permute-start.9
  40.9 1.4 %collective-permute-start.11 = (bf16[1024,256]{1,0:T(8,128)(2,1)S(1)}, bf16[1024,256]{1,0:T(8,128)(2,1)}, u32[]{:S(2)}, u32[]{:S(2)}) collective-permute-start(bf16[1024,256]{1,0:T(8,128)(2,1)S(1)} %get-tuple-element.24), channel_id=1, source_target_pairs={{0,2},{1,3},{2,0},{3,1},{4,6},{5,7},{6,4},{7,5},{8,10},{9,11},{10,... | collective-permute-start | bytes 1572872 | tf_op jit(solution)/shard_map/ppermute | solution.py:277
  42.4 10.0 %collective-permute-done.1.refs_0_ = bf16[1024,256]{1,0:T(8,128)(2,1)S(1)} collective-permute-done((bf16[1024,256]{1,0:T(8,128)(2,1)S(1)}, bf16[1024,256]{1,0:T(8,128)(2,1)S(1)}, u32[]{:S(2)}, u32[]{:S(2)}) %collective-permute-start.1) | collective-permute-done | bytes 524320 | tf_op jit(solution)/shard_map/ppermute | solution.py:277
  52.4 0.0 copy-start.4
  52.4 4.2 %collective-permute-start.3 = (bf16[1024,256]{1,0:T(8,128)(2,1)S(1)}, bf16[1024,256]{1,0:T(8,128)(2,1)}, u32[]{:S(2)}, u32[]{:S(2)}) collective-permute-start(bf16[1024,256]{1,0:T(8,128)(2,1)S(1)} %collective-permute-done.1.refs_0_), channel_id=1, source_target_pairs={{0,4},{1,5},{2,14},{3,15},{4,8},{5,9},{6,2},{7,3},{8,12},{9,13},{1... | collective-permute-start | bytes 1572872 | tf_op jit(solution)/shard_map/ppermute | solution.py:277
  56.6 7.1 %collective-permute-done.2.refs_1_ = bf16[1024,256]{1,0:T(8,128)(2,1)} collective-permute-done((bf16[1024,256]{1,0:T(8,128)(2,1)S(1)}, bf16[1024,256]{1,0:T(8,128)(2,1)}, u32[]{:S(2)}, u32[]{:S(2)}) %collective-permute-start.2) | collective-permute-done | bytes 524320 | tf_op jit(solution)/shard_map/ppermute | solution.py:277
  63.8 4.2 %collective-permute-start.4 = (bf16[1024,256]{1,0:T(8,128)(2,1)}, bf16[1024,256]{1,0:T(8,128)(2,1)}, u32[]{:S(2)}, u32[]{:S(2)}) collective-permute-start(bf16[1024,256]{1,0:T(8,128)(2,1)} %collective-permute-done.2.refs_1_), channel_id=1, source_target_pairs={{0,4},{1,5},{2,14},{3,15},{4,8},{5,9},{6,2},{7,3},{8,12},{9,13},{1... | collective-permute-start | bytes 1572872 | tf_op jit(solution)/shard_map/ppermute | solution.py:277
  68.0 7.0 %collective-permute-done.9.refs_0_ = bf16[1024,256]{1,0:T(8,128)(2,1)S(1)} collective-permute-done((bf16[1024,256]{1,0:T(8,128)(2,1)S(1)}, bf16[1024,256]{1,0:T(8,128)(2,1)S(1)}, u32[]{:S(2)}, u32[]{:S(2)}) %collective-permute-start.9) | collective-permute-done | bytes 524320 | tf_op jit(solution)/shard_map/ppermute | solution.py:277
  75.0 0.0 copy-start.1
  75.0 4.2 %collective-permute-start.10 = (bf16[1024,256]{1,0:T(8,128)(2,1)S(1)}, bf16[1024,256]{1,0:T(8,128)(2,1)S(1)}, u32[]{:S(2)}, u32[]{:S(2)}) collective-permute-start(bf16[1024,256]{1,0:T(8,128)(2,1)S(1)} %collective-permute-done.9.refs_0_), channel_id=1, source_target_pairs={{0,4},{1,5},{2,14},{3,15},{4,8},{5,9},{6,2},{7,3},{8,12},{9,13},{1... | collective-permute-start | bytes 1572872 | tf_op jit(solution)/shard_map/ppermute | solution.py:277
  79.2 7.0 %collective-permute-done.11.refs_1_ = bf16[1024,256]{1,0:T(8,128)(2,1)} collective-permute-done((bf16[1024,256]{1,0:T(8,128)(2,1)S(1)}, bf16[1024,256]{1,0:T(8,128)(2,1)}, u32[]{:S(2)}, u32[]{:S(2)}) %collective-permute-start.11) | collective-permute-done | bytes 524320 | tf_op jit(solution)/shard_map/ppermute | solution.py:277
  86.2 1.4 %collective-permute-start.5 = (bf16[1024,256]{1,0:T(8,128)(2,1)S(1)}, bf16[1024,256]{1,0:T(8,128)(2,1)S(1)}, u32[]{:S(2)}, u32[]{:S(2)}) collective-permute-start(bf16[1024,256]{1,0:T(8,128)(2,1)S(1)} %collective-permute-done.1.refs_0_), channel_id=1, source_target_pairs={{0,1},{1,0},{2,3},{3,2},{4,5},{5,4},{6,7},{7,6},{8,9},{9,8},{10,11... | collective-permute-start | bytes 1572872 | tf_op jit(solution)/shard_map/ppermute | solution.py:277
  87.6 0.0 collective-permute-done.3.refs_2_
  87.6 0.0 collective-permute-start.6
  87.6 0.0 collective-permute-done.4.refs_3_
  87.6 0.5 collective-permute-start.7
  88.1 1.2 %collective-permute-done.10.refs_2_ = bf16[1024,256]{1,0:T(8,128)(2,1)S(1)} collective-permute-done((bf16[1024,256]{1,0:T(8,128)(2,1)S(1)}, bf16[1024,256]{1,0:T(8,128)(2,1)S(1)}, u32[]{:S(2)}, u32[]{:S(2)}) %collective-permute-start.10) | collective-permute-done | bytes 524320 | tf_op jit(solution)/shard_map/ppermute | solution.py:277
  89.3 2.2 %collective-permute-start.8 = (bf16[1024,256]{1,0:T(8,128)(2,1)}, bf16[1024,256]{1,0:T(8,128)(2,1)}, u32[]{:S(2)}, u32[]{:S(2)}) collective-permute-start(bf16[1024,256]{1,0:T(8,128)(2,1)} %collective-permute-done.4.refs_3_), channel_id=1, source_target_pairs={{0,1},{1,0},{2,3},{3,2},{4,5},{5,4},{6,7},{7,6},{8,9},{9,8},{10,11... | collective-permute-start | bytes 1572872 | tf_op jit(solution)/shard_map/ppermute | solution.py:277
  91.6 0.0 copy-done.1
  91.6 0.0 collective-permute-done.5.refs_4_
  91.6 0.0 copy-done.4
  91.6 0.0 copy-start.5
  91.6 0.8 copy-done.5
  92.4 4.0 %collective-permute-start.12 = (bf16[1024,256]{1,0:T(8,128)(2,1)}, bf16[1024,256]{1,0:T(8,128)(2,1)S(1)}, u32[]{:S(2)}, u32[]{:S(2)}) collective-permute-start(bf16[1024,256]{1,0:T(8,128)(2,1)} %collective-permute-done.11.refs_1_), channel_id=1, source_target_pairs={{0,4},{1,5},{2,14},{3,15},{4,8},{5,9},{6,2},{7,3},{8,12},{9,13},{1... | collective-permute-start | bytes 1572872 | tf_op jit(solution)/shard_map/ppermute | solution.py:277
  96.4 0.1 add_convert_fusion.refs_1_.flag_ref
  96.5 0.0 collective-permute-done.6.refs_5_
  96.5 0.4 collective-permute-start.13
  96.8 0.0 collective-permute-done.7.refs_6_
  96.8 0.2 collective-permute-start.14
  97.0 0.0 collective-permute-done.8.refs_7_
  97.0 0.3 collective-permute-start.15
  97.3 0.0 collective-permute-done.beside
  97.3 0.0 slice-start.1
  97.3 0.0 slice-start.2
  97.3 9.6 %flux.1 = (bf16[1024,1024]{1,0:T(8,128)(2,1)}, f32[8,128]{1,0:T(8,128)S(1)}) custom-call(s32[2]{0:T(128)S(1)} %add_convert_fusion.refs_1_.flag_ref, bf16[1024,5120]{1,0:T(8,128)(2,1)} %get-tuple-element.16.dense_ref, bf16[1024,1024]{1,0:T(8,128)(2,1)} %get-tuple-element.18.own, bf16[1024,1024]{1,0:T(8,128)(2,1)} %collective-permute-done.beside, ...), custom_call_target="tpu_custom_call" | custom-call | tf_op jit(solution)/shard_map/flux/pallas_call | solution.py:359
  106.9 0.0 slice-done
  106.9 0.0 slice-done.1
  106.9 0.0 slice-done.2
  107.0 0.0 copy-start.2
  107.0 3.7 %near_flux.1 = (f32[1024,512]{1,0:T(8,128)S(1)}, f32[8,128]{1,0:T(8,128)S(1)}) custom-call(bf16[1024,5120]{1,0:T(8,128)(2,1)S(1)} %bitcast.12, bf16[1024,1024]{1,0:T(8,128)(2,1)} %get-tuple-element.18.own, bf16[1024,1024]{1,0:T(8,128)(2,1)} %collective-permute-done.beside, f32[8,128]{1,0:T(8,128)S(1)} %get-tuple-element.22.wait_ref), custom_call_target="tpu_custom_call" | custom-call | tf_op jit(solution)/shard_map/near_flux/pallas_call | solution.py:379
  110.7 0.0 collective-permute-done.12.refs_0_
  110.7 0.3 collective-permute-start.16
  111.0 0.0 collective-permute-done.13.refs_4_
  111.0 0.0 collective-permute-done.14.refs_5_
  111.0 0.0 collective-permute-done.15.refs_6_
  111.0 1.7 %collective-permute-done.16.refs_7_ = bf16[1024,256]{1,0:T(8,128)(2,1)S(1)} collective-permute-done((bf16[1024,256]{1,0:T(8,128)(2,1)S(1)}, bf16[1024,256]{1,0:T(8,128)(2,1)S(1)}, u32[]{:S(2)}, u32[]{:S(2)}) %collective-permute-start.16) | collective-permute-done | bytes 524320 | tf_op jit(solution)/shard_map/ppermute | solution.py:277
  112.7 0.0 copy-done.2
  112.7 6.4 %far_flux.1 = bf16[1024,1024]{1,0:T(8,128)(2,1)} custom-call(s32[2]{0:T(128)S(1)} %add_convert_fusion.refs_1_.flag_ref, bf16[1024,5120]{1,0:T(8,128)(2,1)S(1)} %bitcast.12, f32[1024,512]{1,0:T(8,128)S(1)} %get-tuple-element.23.prior_ref, bf16[1024,256]{1,0:T(8,128)(2,1)S(1)} %copy-done.2, ...), custom_call_target="tpu_custom_call", output_to_operand_aliasing={{}: (11, {})} | custom-call | tf_op jit(solution)/shard_map/far_flux/pallas_call | solution.py:395
  (6 shorter events, 0.0 us)
Async XLA Ops:
  0.0 9.2 %copy-start.3 = (s32[4,20]{1,0:T(4,128)S(1)}, s32[4,20]{1,0:T(4,128)}, u32[]{:S(2)}) copy-start(s32[4,20]{1,0:T(4,128)} %cols_ref.1) | copy-start | bytes 964
  2.5 32.6 %all-to-all-start = ((bf16[16,32,1152]{2,1,0:T(8,128)(2,1)}), bf16[16,32,1152]{2,1,0:T(8,128)(2,1)S(1)}, u32[]{:S(2)}, u32[]{:S(2)}) async-start(bf16[16,32,1152]{2,1,0:T(8,128)(2,1)} %bitcast.14), calls=%async_computation | async-start | bytes 2359296 | tf_op jit(solution)/shard_map/all_to_all | solution.py:309
  35.1 1.6 %copy-start = (bf16[1024,1024]{1,0:T(8,128)(2,1)S(1)}, bf16[1024,1024]{1,0:T(8,128)(2,1)}, u32[]{:S(2)}) copy-start(bf16[1024,1024]{1,0:T(8,128)(2,1)} %base_ref.1) | copy-start | bytes 6291460
  36.7 70.2 %slice-start = ((s8[10485760]{0:T(1024)(128)(4,1)}), s8[2097152]{0:T(1024)(128)(4,1)S(1)}, s32[]{:S(2)}) async-start(s8[10485760]{0:T(1024)(128)(4,1)} %bitcast.11), calls=%async_computation.1 | async-start | bytes 4194304
  39.4 57.9 %collective-permute-start = (bf16[1024,1024]{1,0:T(8,128)(2,1)}, bf16[1024,1024]{1,0:T(8,128)(2,1)}, u32[]{:S(2)}, u32[]{:S(2)}) collective-permute-start(bf16[1024,1024]{1,0:T(8,128)(2,1)} %get-tuple-element.18.own), channel_id=1, source_target_pairs={{0,1},{1,0},{2,3},{3,2},{4,5},{5,4},{6,7},{7,6},{8,9},{9,8},{10,11... | collective-permute-start | bytes 6291464 | tf_op jit(solution)/shard_map/ppermute | solution.py:277
  39.4 13.0 %collective-permute-start.1 = (bf16[1024,256]{1,0:T(8,128)(2,1)S(1)}, bf16[1024,256]{1,0:T(8,128)(2,1)S(1)}, u32[]{:S(2)}, u32[]{:S(2)}) collective-permute-start(bf16[1024,256]{1,0:T(8,128)(2,1)S(1)} %get-tuple-element.19), channel_id=1, source_target_pairs={{0,2},{1,3},{2,0},{3,1},{4,6},{5,7},{6,4},{7,5},{8,10},{9,11},{10,... | collective-permute-start | bytes 1572872 | tf_op jit(solution)/shard_map/ppermute | solution.py:277
  39.4 24.3 %collective-permute-start.2 = (bf16[1024,256]{1,0:T(8,128)(2,1)S(1)}, bf16[1024,256]{1,0:T(8,128)(2,1)}, u32[]{:S(2)}, u32[]{:S(2)}) collective-permute-start(bf16[1024,256]{1,0:T(8,128)(2,1)S(1)} %get-tuple-element.20), channel_id=1, source_target_pairs={{0,2},{1,3},{2,0},{3,1},{4,6},{5,7},{6,4},{7,5},{8,10},{9,11},{10,... | collective-permute-start | bytes 1572872 | tf_op jit(solution)/shard_map/ppermute | solution.py:277
  40.9 34.1 %collective-permute-start.9 = (bf16[1024,256]{1,0:T(8,128)(2,1)S(1)}, bf16[1024,256]{1,0:T(8,128)(2,1)S(1)}, u32[]{:S(2)}, u32[]{:S(2)}) collective-permute-start(bf16[1024,256]{1,0:T(8,128)(2,1)S(1)} %get-tuple-element.21), channel_id=1, source_target_pairs={{0,2},{1,3},{2,0},{3,1},{4,6},{5,7},{6,4},{7,5},{8,10},{9,11},{10,... | collective-permute-start | bytes 1572872 | tf_op jit(solution)/shard_map/ppermute | solution.py:277
  40.9 45.3 %collective-permute-start.11 = (bf16[1024,256]{1,0:T(8,128)(2,1)S(1)}, bf16[1024,256]{1,0:T(8,128)(2,1)}, u32[]{:S(2)}, u32[]{:S(2)}) collective-permute-start(bf16[1024,256]{1,0:T(8,128)(2,1)S(1)} %get-tuple-element.24), channel_id=1, source_target_pairs={{0,2},{1,3},{2,0},{3,1},{4,6},{5,7},{6,4},{7,5},{8,10},{9,11},{10,... | collective-permute-start | bytes 1572872 | tf_op jit(solution)/shard_map/ppermute | solution.py:277
  52.4 39.2 %copy-start.4 = (bf16[1024,256]{1,0:T(8,128)(2,1)}, bf16[1024,256]{1,0:T(8,128)(2,1)S(1)}, u32[]{:S(2)}) copy-start(bf16[1024,256]{1,0:T(8,128)(2,1)S(1)} %collective-permute-done.1.refs_0_) | copy-start | bytes 1572868
  52.4 35.2 %collective-permute-start.3 = (bf16[1024,256]{1,0:T(8,128)(2,1)S(1)}, bf16[1024,256]{1,0:T(8,128)(2,1)}, u32[]{:S(2)}, u32[]{:S(2)}) collective-permute-start(bf16[1024,256]{1,0:T(8,128)(2,1)S(1)} %collective-permute-done.1.refs_0_), channel_id=1, source_target_pairs={{0,4},{1,5},{2,14},{3,15},{4,8},{5,9},{6,2},{7,3},{8,12},{9,13},{1... | collective-permute-start | bytes 1572872 | tf_op jit(solution)/shard_map/ppermute | solution.py:277
  63.8 23.8 %collective-permute-start.4 = (bf16[1024,256]{1,0:T(8,128)(2,1)}, bf16[1024,256]{1,0:T(8,128)(2,1)}, u32[]{:S(2)}, u32[]{:S(2)}) collective-permute-start(bf16[1024,256]{1,0:T(8,128)(2,1)} %collective-permute-done.2.refs_1_), channel_id=1, source_target_pairs={{0,4},{1,5},{2,14},{3,15},{4,8},{5,9},{6,2},{7,3},{8,12},{9,13},{1... | collective-permute-start | bytes 1572872 | tf_op jit(solution)/shard_map/ppermute | solution.py:277
  75.0 16.6 %copy-start.1 = (bf16[1024,256]{1,0:T(8,128)(2,1)}, bf16[1024,256]{1,0:T(8,128)(2,1)S(1)}, u32[]{:S(2)}) copy-start(bf16[1024,256]{1,0:T(8,128)(2,1)S(1)} %collective-permute-done.9.refs_0_) | copy-start | bytes 1572868
  75.0 14.3 %collective-permute-start.10 = (bf16[1024,256]{1,0:T(8,128)(2,1)S(1)}, bf16[1024,256]{1,0:T(8,128)(2,1)S(1)}, u32[]{:S(2)}, u32[]{:S(2)}) collective-permute-start(bf16[1024,256]{1,0:T(8,128)(2,1)S(1)} %collective-permute-done.9.refs_0_), channel_id=1, source_target_pairs={{0,4},{1,5},{2,14},{3,15},{4,8},{5,9},{6,2},{7,3},{8,12},{9,13},{1... | collective-permute-start | bytes 1572872 | tf_op jit(solution)/shard_map/ppermute | solution.py:277
  86.2 5.3 %collective-permute-start.5 = (bf16[1024,256]{1,0:T(8,128)(2,1)S(1)}, bf16[1024,256]{1,0:T(8,128)(2,1)S(1)}, u32[]{:S(2)}, u32[]{:S(2)}) collective-permute-start(bf16[1024,256]{1,0:T(8,128)(2,1)S(1)} %collective-permute-done.1.refs_0_), channel_id=1, source_target_pairs={{0,1},{1,0},{2,3},{3,2},{4,5},{5,4},{6,7},{7,6},{8,9},{9,8},{10,11... | collective-permute-start | bytes 1572872 | tf_op jit(solution)/shard_map/ppermute | solution.py:277
  87.6 8.9 %collective-permute-start.6 = (bf16[1024,256]{1,0:T(8,128)(2,1)}, bf16[1024,256]{1,0:T(8,128)(2,1)}, u32[]{:S(2)}, u32[]{:S(2)}) collective-permute-start(bf16[1024,256]{1,0:T(8,128)(2,1)} %collective-permute-done.2.refs_1_), channel_id=1, source_target_pairs={{0,1},{1,0},{2,3},{3,2},{4,5},{5,4},{6,7},{7,6},{8,9},{9,8},{10,11... | collective-permute-start | bytes 1572872 | tf_op jit(solution)/shard_map/ppermute | solution.py:277
  87.6 9.2 %collective-permute-start.7 = (bf16[1024,256]{1,0:T(8,128)(2,1)}, bf16[1024,256]{1,0:T(8,128)(2,1)}, u32[]{:S(2)}, u32[]{:S(2)}) collective-permute-start(bf16[1024,256]{1,0:T(8,128)(2,1)} %collective-permute-done.3.refs_2_), channel_id=1, source_target_pairs={{0,1},{1,0},{2,3},{3,2},{4,5},{5,4},{6,7},{7,6},{8,9},{9,8},{10,11... | collective-permute-start | bytes 1572872 | tf_op jit(solution)/shard_map/ppermute | solution.py:277
  89.3 7.7 %collective-permute-start.8 = (bf16[1024,256]{1,0:T(8,128)(2,1)}, bf16[1024,256]{1,0:T(8,128)(2,1)}, u32[]{:S(2)}, u32[]{:S(2)}) collective-permute-start(bf16[1024,256]{1,0:T(8,128)(2,1)} %collective-permute-done.4.refs_3_), channel_id=1, source_target_pairs={{0,1},{1,0},{2,3},{3,2},{4,5},{5,4},{6,7},{7,6},{8,9},{9,8},{10,11... | collective-permute-start | bytes 1572872 | tf_op jit(solution)/shard_map/ppermute | solution.py:277
  91.6 0.8 copy-start.5
  92.4 18.3 %collective-permute-start.12 = (bf16[1024,256]{1,0:T(8,128)(2,1)}, bf16[1024,256]{1,0:T(8,128)(2,1)S(1)}, u32[]{:S(2)}, u32[]{:S(2)}) collective-permute-start(bf16[1024,256]{1,0:T(8,128)(2,1)} %collective-permute-done.11.refs_1_), channel_id=1, source_target_pairs={{0,4},{1,5},{2,14},{3,15},{4,8},{5,9},{6,2},{7,3},{8,12},{9,13},{1... | collective-permute-start | bytes 1572872 | tf_op jit(solution)/shard_map/ppermute | solution.py:277
  96.5 14.5 %collective-permute-start.13 = (bf16[1024,256]{1,0:T(8,128)(2,1)}, bf16[1024,256]{1,0:T(8,128)(2,1)S(1)}, u32[]{:S(2)}, u32[]{:S(2)}) collective-permute-start(bf16[1024,256]{1,0:T(8,128)(2,1)} %copy-done.1), channel_id=1, source_target_pairs={{0,1},{1,0},{2,3},{3,2},{4,5},{5,4},{6,7},{7,6},{8,9},{9,8},{10,11... | collective-permute-start | bytes 1572872 | tf_op jit(solution)/shard_map/ppermute | solution.py:277
  96.8 14.2 %collective-permute-start.14 = (bf16[1024,256]{1,0:T(8,128)(2,1)}, bf16[1024,256]{1,0:T(8,128)(2,1)S(1)}, u32[]{:S(2)}, u32[]{:S(2)}) collective-permute-start(bf16[1024,256]{1,0:T(8,128)(2,1)} %collective-permute-done.11.refs_1_), channel_id=1, source_target_pairs={{0,1},{1,0},{2,3},{3,2},{4,5},{5,4},{6,7},{7,6},{8,9},{9,8},{10,11... | collective-permute-start | bytes 1572872 | tf_op jit(solution)/shard_map/ppermute | solution.py:277
  97.0 13.9 %collective-permute-start.15 = (bf16[1024,256]{1,0:T(8,128)(2,1)S(1)}, bf16[1024,256]{1,0:T(8,128)(2,1)S(1)}, u32[]{:S(2)}, u32[]{:S(2)}) collective-permute-start(bf16[1024,256]{1,0:T(8,128)(2,1)S(1)} %collective-permute-done.10.refs_2_), channel_id=1, source_target_pairs={{0,1},{1,0},{2,3},{3,2},{4,5},{5,4},{6,7},{7,6},{8,9},{9,8},{10,11... | collective-permute-start | bytes 1572872 | tf_op jit(solution)/shard_map/ppermute | solution.py:277
  97.3 9.6 %slice-start.1 = ((s8[10485760]{0:T(1024)(128)(4,1)}), s8[4194304]{0:T(1024)(128)(4,1)S(1)}, s32[]{:S(2)}) async-start(s8[10485760]{0:T(1024)(128)(4,1)} %bitcast.11), calls=%async_computation.2 | async-start | bytes 8388608
  97.3 9.6 %slice-start.2 = ((s8[10485760]{0:T(1024)(128)(4,1)}), s8[4194304]{0:T(1024)(128)(4,1)S(1)}, s32[]{:S(2)}) async-start(s8[10485760]{0:T(1024)(128)(4,1)} %bitcast.11), calls=%async_computation.3 | async-start | bytes 8388608
  107.0 5.7 %copy-start.2 = (bf16[1024,256]{1,0:T(8,128)(2,1)S(1)}, bf16[1024,256]{1,0:T(8,128)(2,1)}, u32[]{:S(2)}) copy-start(bf16[1024,256]{1,0:T(8,128)(2,1)} %copy-done.1) | copy-start | bytes 1572868
  110.7 2.0 %collective-permute-start.16 = (bf16[1024,256]{1,0:T(8,128)(2,1)S(1)}, bf16[1024,256]{1,0:T(8,128)(2,1)S(1)}, u32[]{:S(2)}, u32[]{:S(2)}) collective-permute-start(bf16[1024,256]{1,0:T(8,128)(2,1)S(1)} %gate.7.refs_3_), channel_id=1, source_target_pairs={{0,1},{1,0},{2,3},{3,2},{4,5},{5,4},{6,7},{7,6},{8,9},{9,8},{10,11... | collective-permute-start | bytes 1572872 | tf_op jit(solution)/shard_map/ppermute | solution.py:277
